TPU v7x, 32 devices: a whole 2x2x4 slice. The times are simulated.
32 devices in a mesh: dp: 8 (over z, y), seq: 4 (over x, core).
Axes of the slice: x: 2, y: 2, z: 4, core: 2. Of those that a mesh axis runs over, the one named last changes fastest.
Arguments:
- activations: bfloat16 [4096, 1536], P(('dp', 'seq')), may hold values from -6 to 6
- cotangent: bfloat16 [4096, 1536], P(('dp', 'seq')), may hold values from -6 to 6
- doc_lengths: int32 [1, 8], replicated, may hold values from 1 to 2048, as said below
- routes: int32 [4096, 4], P(('dp', 'seq')), may hold values from 0 to 7, all different within a row; in each aligned block of 128 rows (0 to 127, 128 to 255, ...) at most 128 rows name the same one
- norm_gains: bfloat16 [2, 2, 1536], P(None, None, ('dp', 'seq')), may hold values from 0.5 to 1.5
- w_qkv: bfloat16 [2, 1536, 2048], P(None, ('dp', 'seq')), may hold values from -0.15625 to 0.15625
- w_out: bfloat16 [2, 1536, 1536], P(None, None, ('dp', 'seq')), may hold values from -0.875 to 0.875
- w_router: bfloat16 [2, 1536, 8], P(None, ('dp', 'seq')), may hold values from -0.078125 to 0.078125
- w_gate_up: bfloat16 [2, 8, 1536, 1536], P(None, 'dp'), may hold values from -0.15625 to 0.15625
- w_down: bfloat16 [2, 8, 768, 1536], P(None, 'dp'), may hold values from -0.4375 to 0.4375
Outputs:
- layer_out: bfloat16 [4096, 1536], P(('dp', 'seq'))
- input_grad: float32 [4096, 1536], P(('dp', 'seq'))
- gain_grad: float32 [2, 2, 1536], P(None, None, ('dp', 'seq'))
- qkv_grad: float32 [2, 1536, 2048], P(None, ('dp', 'seq'))
- out_proj_grad: float32 [2, 1536, 1536], P(None, None, ('dp', 'seq'))
- router_grad: float32 [2, 1536, 8], P(None, ('dp', 'seq'))
- gate_up_grad: float32 [2, 8, 1536, 1536], P(None, 'dp', 'seq')
- down_grad: float32 [2, 8, 768, 1536], P(None, 'dp', 'seq')
Inputs may be any that keep to these rules, and one draw needn't show every extreme that they name: `doc_lengths`: each row lists 8 - 1 documents and then the padded tail, sums to 4096, and one of its documents has exactly 2048 tokens. `routes`: A token names 4 different experts; in the rows of one device no expert is named more than 128 times.
All inputs are finite; a program needn't handle non-finite values.
Results may differ from a plain program's by a relative error of at most 0.025.
Values may be sent and summed in bfloat16 or wider, within the bound.
No kernel may reach another device: no remote copies, remote signals or barrier semaphores. Data moves between devices by JAX's collectives and lax.ppermute only.
A program may use at most 256 MiB of HBM per device.

v0:
```python
import math

import jax
import jax.numpy as jnp
from jax import lax
from jax.sharding import PartitionSpec as P

HEADS = 12
KV_HEADS = 2
HEAD = 128
WINDOW = 1024
SEQ_LEN = 8192


norm_eps = 1e-06
rope_base = 1000000.0
block_limit = 512


def passed_along(value, axis, steps):
    count = lax.axis_size(axis)
    first, last = (max(0, -steps), min(count, count - steps))
    return lax.ppermute(value, axis, [(source, source + steps) for source in range(first, last)])


def doc_labels(token_index, doc_lengths, seq_length):
    doc_total = doc_lengths.shape[1]
    doc_ends = jnp.cumsum(doc_lengths, axis=1)
    clamped = jnp.maximum(token_index, 0)
    seq_number = clamped // seq_length
    position = clamped % seq_length
    seq_pick = seq_number[:, None] == jnp.arange(doc_lengths.shape[0], dtype=jnp.int32)[None, :]
    token_ends = jnp.sum(jnp.where(seq_pick[:, :, None], doc_ends[None, :, :], 0), axis=1)
    doc_number = jnp.sum((position[:, None] >= token_ends).astype(jnp.int32), axis=1)
    doc_label = jnp.where(token_index >= 0, seq_number * doc_total + doc_number, -1)
    is_valid = (doc_number < doc_total - 1).astype(jnp.float32)
    return (doc_label, is_valid, position)


def rope_turn(vectors, position, direction):
    half_width = vectors.shape[-1] // 2
    frequency = rope_base ** (-jnp.arange(half_width, dtype=jnp.float32) * 2.0 / vectors.shape[-1])
    angles = position.astype(jnp.float32)[:, None] * frequency[None, :]
    cosine = jnp.cos(angles)[:, None, :]
    sine_part = direction * jnp.sin(angles)[:, None, :]
    first_half = vectors[..., :half_width]
    second_half = vectors[..., half_width:]
    return jnp.concatenate(
        [
            first_half * cosine - second_half * sine_part,
            second_half * cosine + first_half * sine_part,
        ],
        axis=-1,
    )


def norm_scale(stream):
    return lax.rsqrt(jnp.mean(stream * stream, axis=-1, keepdims=True) + norm_eps)


def norm_back(stream, scale, gain, out_grad):
    gain_grad = jnp.sum(out_grad * stream * scale, axis=0)
    scaled_grad = out_grad * gain
    stream_grad = scale * scaled_grad - stream * scale**3 * jnp.mean(
        scaled_grad * stream, axis=-1, keepdims=True
    )
    return (gain_grad, stream_grad)


def block_scores(head_queries, key_table, query_index, key_index, query_label, key_label):
    distance = query_index[:, None] - key_index[None, :]
    same_doc = query_label[:, None] == key_label[None, :]
    keep_mask = same_doc & (distance >= 0) & (distance < WINDOW)
    scores = jnp.einsum(
        "qhd,kd->hqk", head_queries, key_table[:, 0], preferred_element_type=jnp.float32
    ) * head_queries.shape[-1] ** (-0.5)
    return (head_queries, key_table, keep_mask, scores)


def attend_forward(head_queries, key_table, query_index, key_index, query_label, key_label):
    group_rows = head_queries.shape[0]
    block_rows = math.gcd(block_limit, group_rows)

    def one_block(block_start):
        query_piece, key_piece, keep_mask, scores = block_scores(
            head_queries, key_table, query_index, key_index, query_label, key_label
        )
        scores = jnp.where(keep_mask[None], scores, -jnp.inf)
        row_top = jnp.max(scores, axis=-1, keepdims=True)
        weights = jnp.exp(scores - row_top)
        row_total = jnp.sum(weights, axis=-1, keepdims=True)
        prob_rows = (weights / row_total).astype(jnp.bfloat16)
        block_out = jnp.einsum(
            "hqk,kd->qhd", prob_rows, key_piece[:, 1], preferred_element_type=jnp.float32
        )
        return (block_out, (row_top + jnp.log(row_total))[:, :, 0])

    starts = jnp.arange(group_rows // block_rows, dtype=jnp.int32) * block_rows
    block_outs, lse_rows = lax.map(one_block, starts)
    return (block_outs.reshape(head_queries.shape), lse_rows)


def attend_backward(
    head_queries, key_table, head_grad, lse_rows, query_index, key_index, query_label, key_label
):
    group_rows = head_queries.shape[0]
    block_rows = math.gcd(block_limit, group_rows)
    score_scale = head_queries.shape[-1] ** (-0.5)

    def one_block(pair_sums, inputs):
        block_start, log_total = inputs
        query_piece, key_piece, keep_mask, scores = block_scores(
            head_queries, key_table, query_index, key_index, query_label, key_label
        )
        prob_rows = jnp.where(keep_mask[None], jnp.exp(scores - log_total[:, :, None]), 0.0)
        prob_grad = jnp.einsum(
            "qhd,kd->hqk", head_grad, key_piece[:, 1], preferred_element_type=jnp.float32
        )
        row_dot = jnp.sum(prob_rows * prob_grad, axis=-1, keepdims=True)
        score_grad = (prob_rows * (prob_grad - row_dot)).astype(jnp.bfloat16)
        query_grad = (
            jnp.einsum(
                "hqk,kd->qhd", score_grad, key_piece[:, 0], preferred_element_type=jnp.float32
            )
            * score_scale
        )
        key_grad = (
            jnp.einsum("hqk,qhd->kd", score_grad, query_piece, preferred_element_type=jnp.float32)
            * score_scale
        )
        value_grad = jnp.einsum(
            "hqk,qhd->kd",
            prob_rows.astype(jnp.bfloat16),
            head_grad,
            preferred_element_type=jnp.float32,
        )
        updated = pair_sums + jnp.stack([key_grad, value_grad], axis=1)
        return (updated, query_grad)

    starts = jnp.arange(group_rows // block_rows, dtype=jnp.int32) * block_rows
    pair_sums, query_grads = lax.scan(
        one_block, jnp.zeros(key_table.shape, jnp.float32), (starts, lse_rows)
    )
    return (query_grads.reshape(head_queries.shape), pair_sums)


def per_device(
    activations,
    cotangent,
    doc_lengths,
    routes,
    norm_gains,
    w_qkv,
    w_out,
    w_router,
    w_gate_up,
    w_down,
):
    dp_count = lax.axis_size("dp")
    seq_count = lax.axis_size("seq")
    tok_rows, model_width = activations.shape
    group_rows = tok_rows * seq_count
    layer_count = w_qkv.shape[0]
    share_count = seq_count // KV_HEADS
    q_width = HEADS * HEAD
    kv_width = KV_HEADS * HEAD
    ff_width = w_down.shape[2]
    top_count = routes.shape[1]
    exp_here = w_gate_up.shape[1]
    expert_count = exp_here * dp_count
    capacity = 2 * tok_rows * top_count // expert_count
    assign_count = tok_rows * top_count
    seq_length = min(SEQ_LEN, tok_rows * dp_count * seq_count)
    edge_depth = -(-(WINDOW - 1) // group_rows)
    pad_rows = max(0, WINDOW - edge_depth * group_rows)
    dp_index = lax.axis_index("dp")
    seq_index = lax.axis_index("seq")
    own_index = (dp_index * seq_count + seq_index) * tok_rows + jnp.arange(
        tok_rows, dtype=jnp.int32
    )
    own_position = doc_labels(own_index, doc_lengths, seq_length)[2]
    group_start = dp_index * group_rows
    query_index = group_start + jnp.arange(group_rows, dtype=jnp.int32)
    key_index = (
        group_start
        - edge_depth * group_rows
        - pad_rows
        + jnp.arange(pad_rows + (edge_depth + 1) * group_rows, dtype=jnp.int32)
    )
    query_label, query_valid, group_position = doc_labels(query_index, doc_lengths, seq_length)
    key_label = doc_labels(key_index, doc_lengths, seq_length)[0]
    flat_expert = routes.reshape(assign_count)
    expert_ids = jnp.arange(expert_count, dtype=jnp.int32)
    chosen_mask = flat_expert[:, None] == expert_ids[None, :]
    running = jnp.cumsum(chosen_mask.astype(jnp.int32), axis=0)
    expert_rank = jnp.sum(jnp.where(chosen_mask, running - 1, 0), axis=1)
    slot_index = flat_expert * capacity + expert_rank
    source = (
        jnp.full((expert_count * capacity,), assign_count, jnp.int32)
        .at[slot_index]
        .set(jnp.arange(assign_count, dtype=jnp.int32))
    )
    source_token = jnp.where(source < assign_count, source // top_count, tok_rows)
    source_assign = jnp.minimum(source, assign_count)
    pick_expert = (routes[:, :, None] == expert_ids[None, None, :]).astype(jnp.float32)
    stream = activations.astype(jnp.float32)
    stored = []
    held_weights = []
    for layer_index in range(layer_count):
        gain_rows, qkv_full, out_full, router_full = (
            lax.all_gather(norm_gains[layer_index], ("dp", "seq"), axis=1, tiled=True),
            lax.all_gather(w_qkv[layer_index], ("dp", "seq"), axis=0, tiled=True),
            lax.all_gather(w_out[layer_index], ("dp", "seq"), axis=1, tiled=True),
            lax.all_gather(w_router[layer_index], ("dp", "seq"), axis=0, tiled=True),
        )
        held_weights.append((gain_rows, qkv_full, out_full, router_full))
        scale_one = norm_scale(stream)
        normed_one = (stream * scale_one * gain_rows[0].astype(jnp.float32)).astype(jnp.bfloat16)
        mixed_rows = jnp.dot(normed_one, qkv_full, preferred_element_type=jnp.float32)
        queries = rope_turn(
            mixed_rows[:, :q_width].reshape(tok_rows, HEADS, HEAD), own_position, 1.0
        ).astype(jnp.bfloat16)
        key_vecs = rope_turn(
            mixed_rows[:, q_width : q_width + kv_width].reshape(tok_rows, KV_HEADS, HEAD),
            own_position,
            1.0,
        ).astype(jnp.bfloat16)
        value_vecs = (
            mixed_rows[:, q_width + kv_width :]
            .reshape(tok_rows, KV_HEADS, HEAD)
            .astype(jnp.bfloat16)
        )
        kv_pairs = jnp.stack(
            [
                jnp.repeat(key_vecs, share_count, axis=1),
                jnp.repeat(value_vecs, share_count, axis=1),
            ],
            axis=2,
        )
        head_queries, head_pairs = (
            lax.all_to_all(queries, "seq", split_axis=1, concat_axis=0, tiled=True),
            lax.all_to_all(kv_pairs, "seq", split_axis=1, concat_axis=0, tiled=True),
        )
        local_pairs = head_pairs[:, 0]
        edge_list = []
        for shift_step in range(edge_depth, 0, -1):
            edge_list.append(passed_along(local_pairs, "dp", shift_step))
        key_table = jnp.concatenate(
            [jnp.zeros((pad_rows, 2, HEAD), jnp.bfloat16)] + edge_list + [local_pairs], axis=0
        )
        attended, lse_rows = attend_forward(
            head_queries, key_table, query_index, key_index, query_label, key_label
        )
        attended = (attended * query_valid[:, None, None]).astype(jnp.bfloat16)
        token_out = lax.all_to_all(
            attended, "seq", split_axis=0, concat_axis=1, tiled=True
        ).reshape(tok_rows, q_width)
        stream_mid = stream + jnp.dot(token_out, out_full, preferred_element_type=jnp.float32)
        scale_two = norm_scale(stream_mid)
        normed_two = (stream_mid * scale_two * gain_rows[1].astype(jnp.float32)).astype(
            jnp.bfloat16
        )
        logits = jnp.dot(normed_two, router_full, preferred_element_type=jnp.float32)
        gate_probs = jax.nn.softmax(jnp.sum(pick_expert * logits[:, None, :], axis=2), axis=1)
        padded_tokens = jnp.concatenate([normed_two, jnp.zeros((1, model_width), jnp.bfloat16)])
        outgoing = padded_tokens[source_token].reshape(dp_count, exp_here, capacity, model_width)
        gate_up_here = w_gate_up[layer_index]
        down_here = w_down[layer_index]
        arrived_rows = lax.all_to_all(outgoing, "dp", split_axis=0, concat_axis=0, tiled=True)
        expert_up_gate = jnp.einsum(
            "sxmd,xdf->sxmf", arrived_rows, gate_up_here, preferred_element_type=jnp.float32
        )
        expert_hidden = (
            jax.nn.silu(expert_up_gate[..., :ff_width]) * expert_up_gate[..., ff_width:]
        ).astype(jnp.bfloat16)
        expert_out = jnp.einsum(
            "sxmf,xfd->sxmd", expert_hidden, down_here, preferred_element_type=jnp.float32
        ).astype(jnp.bfloat16)
        returned = lax.all_to_all(expert_out, "dp", split_axis=0, concat_axis=0, tiled=True)
        arrived = arrived_rows
        returned_rows = returned.reshape(expert_count * capacity, model_width)[slot_index].reshape(
            tok_rows, top_count, model_width
        )
        stored.append(
            (
                stream,
                stream_mid,
                scale_one,
                scale_two,
                normed_one,
                normed_two,
                head_queries,
                key_table,
                lse_rows,
                token_out,
                attended,
                gate_probs,
                returned_rows,
                arrived,
            )
        )
        stream = stream_mid + jnp.sum(
            gate_probs[:, :, None] * returned_rows.astype(jnp.float32), axis=1
        )
    layer_out = stream.astype(jnp.bfloat16)
    stream_grad = cotangent.astype(jnp.float32)
    grad_layers = []
    for layer_index in range(layer_count - 1, -1, -1):
        (
            stream,
            stream_mid,
            scale_one,
            scale_two,
            normed_one,
            normed_two,
            head_queries,
            key_table,
            lse_rows,
            token_out,
            head_attended,
            gate_probs,
            returned_rows,
            arrived,
        ) = stored[layer_index]
        gain_rows, qkv_full, out_full, router_full = held_weights[layer_index]
        gate_up_here = w_gate_up[layer_index]
        down_here = w_down[layer_index]
        gate_grad = jnp.sum(returned_rows.astype(jnp.float32) * stream_grad[:, None, :], axis=2)
        sent_grad = (
            (gate_probs[:, :, None] * stream_grad[:, None, :])
            .astype(jnp.bfloat16)
            .reshape(assign_count, model_width)
        )
        sent_grad = jnp.concatenate([sent_grad, jnp.zeros((1, model_width), jnp.bfloat16)])[
            source_assign
        ]
        arrived_grad = lax.all_to_all(
            sent_grad.reshape(dp_count, exp_here, capacity, model_width),
            "dp",
            split_axis=0,
            concat_axis=0,
            tiled=True,
        )
        up_gate = jnp.einsum(
            "sxmd,xdf->sxmf", arrived, gate_up_here, preferred_element_type=jnp.float32
        )
        gate_part = up_gate[..., :ff_width]
        up_part = up_gate[..., ff_width:]
        sigmoid_gate = jax.nn.sigmoid(gate_part)
        activated = gate_part * sigmoid_gate
        hidden = (activated * up_part).astype(jnp.bfloat16)
        down_grad = jnp.einsum(
            "sxmf,sxmd->xfd", hidden, arrived_grad, preferred_element_type=jnp.float32
        )
        hidden_grad = jnp.einsum(
            "sxmd,xfd->sxmf", arrived_grad, down_here, preferred_element_type=jnp.float32
        )
        pair_grad = jnp.concatenate(
            [
                hidden_grad * up_part * sigmoid_gate * (1.0 + gate_part * (1.0 - sigmoid_gate)),
                hidden_grad * activated,
            ],
            axis=-1,
        ).astype(jnp.bfloat16)
        gate_up_grad = jnp.einsum(
            "sxmd,sxmf->xdf", arrived, pair_grad, preferred_element_type=jnp.float32
        )
        expert_in_grad = jnp.einsum(
            "sxmf,xdf->sxmd", pair_grad, gate_up_here, preferred_element_type=jnp.float32
        ).astype(jnp.bfloat16)
        back_grad = lax.all_to_all(expert_in_grad, "dp", split_axis=0, concat_axis=0, tiled=True)
        gate_up_sum, down_sum = (
            lax.psum_scatter(
                gate_up_grad.astype(jnp.bfloat16), "seq", scatter_dimension=1, tiled=True
            ).astype(jnp.float32),
            lax.psum_scatter(
                down_grad.astype(jnp.bfloat16), "seq", scatter_dimension=1, tiled=True
            ).astype(jnp.float32),
        )
        normed_grad = jnp.sum(
            back_grad.reshape(expert_count * capacity, model_width)[slot_index]
            .astype(jnp.float32)
            .reshape(tok_rows, top_count, model_width),
            axis=1,
        )
        chosen_grad = gate_probs * (
            gate_grad - jnp.sum(gate_probs * gate_grad, axis=1, keepdims=True)
        )
        logit_grad = jnp.sum(pick_expert * chosen_grad[:, :, None], axis=1).astype(jnp.bfloat16)
        router_grad = jnp.dot(normed_two.T, logit_grad, preferred_element_type=jnp.float32)
        normed_grad = normed_grad + jnp.dot(
            logit_grad, router_full.T, preferred_element_type=jnp.float32
        )
        gain_two_grad, mid_grad = norm_back(
            stream_mid, scale_two, gain_rows[1].astype(jnp.float32), normed_grad
        )
        mid_grad = stream_grad + mid_grad
        attn_grad = mid_grad.astype(jnp.bfloat16)
        token_grad = (
            jnp.dot(attn_grad, out_full.T, preferred_element_type=jnp.float32)
            .astype(jnp.bfloat16)
            .reshape(tok_rows, HEADS, HEAD)
        )
        head_grad = lax.all_to_all(token_grad, "seq", split_axis=1, concat_axis=0, tiled=True)
        head_grad = (head_grad * query_valid[:, None, None]).astype(jnp.bfloat16)
        query_grad, pair_sums = attend_backward(
            head_queries,
            key_table,
            head_grad,
            lse_rows,
            query_index,
            key_index,
            query_label,
            key_label,
        )
        own_pair = pair_sums[pad_rows + edge_depth * group_rows :]
        for shift_step in range(edge_depth, 0, -1):
            part_start = pad_rows + (edge_depth - shift_step) * group_rows
            own_pair = own_pair + passed_along(
                pair_sums[part_start : part_start + group_rows].astype(jnp.bfloat16),
                "dp",
                -shift_step,
            ).astype(jnp.float32)
        token_query_grad, token_pair_grad = (
            lax.all_to_all(
                query_grad.astype(jnp.bfloat16), "seq", split_axis=0, concat_axis=1, tiled=True
            ).astype(query_grad.dtype),
            lax.all_to_all(
                own_pair[:, None].astype(jnp.bfloat16),
                "seq",
                split_axis=0,
                concat_axis=1,
                tiled=True,
            ).astype(jnp.float32),
        )
        key_value_grad = jnp.sum(
            token_pair_grad.reshape(tok_rows, KV_HEADS, share_count, 2, HEAD), axis=2
        )
        query_lin = rope_turn(token_query_grad, own_position, -1.0).reshape(tok_rows, q_width)
        key_lin = rope_turn(key_value_grad[:, :, 0], own_position, -1.0).reshape(tok_rows, kv_width)
        value_lin = key_value_grad[:, :, 1].reshape(tok_rows, kv_width)
        mixed_grad = jnp.concatenate([query_lin, key_lin, value_lin], axis=1).astype(jnp.bfloat16)
        normed_one_grad = jnp.dot(mixed_grad, qkv_full.T, preferred_element_type=jnp.float32)
        gain_one_grad, front_grad = norm_back(
            stream, scale_one, gain_rows[0].astype(jnp.float32), normed_one_grad
        )
        stream_grad = mid_grad + front_grad
        gain_pair = jnp.stack([gain_one_grad, gain_two_grad])
        qkv_grad = jnp.dot(normed_one.T, mixed_grad, preferred_element_type=jnp.float32)
        out_grad = jnp.dot(token_out.T, attn_grad, preferred_element_type=jnp.float32)
        gain_sum, qkv_sum, out_sum, router_sum = (
            lax.psum_scatter(gain_pair, ("dp", "seq"), scatter_dimension=1, tiled=True),
            lax.psum_scatter(qkv_grad, ("dp", "seq"), scatter_dimension=0, tiled=True),
            lax.psum_scatter(out_grad, ("dp", "seq"), scatter_dimension=1, tiled=True),
            lax.psum_scatter(router_grad, ("dp", "seq"), scatter_dimension=0, tiled=True),
        )
        grad_layers.append((gain_sum, qkv_sum, out_sum, router_sum, gate_up_sum, down_sum))
    grad_layers = grad_layers[::-1]
    stacked = [jnp.stack([grad_entry[member] for grad_entry in grad_layers]) for member in range(6)]
    return (
        layer_out,
        stream_grad,
        stacked[0],
        stacked[1],
        stacked[2],
        stacked[3],
        stacked[4],
        stacked[5],
    )


def solution(mesh):
    return jax.shard_map(
        per_device,
        mesh=mesh,
        in_specs=(
            P(("dp", "seq"), None),
            P(("dp", "seq"), None),
            P(),
            P(("dp", "seq"), None),
            P(None, None, ("dp", "seq")),
            P(None, ("dp", "seq"), None),
            P(None, None, ("dp", "seq")),
            P(None, ("dp", "seq"), None),
            P(None, "dp", None, None),
            P(None, "dp", None, None),
        ),
        out_specs=(
            P(("dp", "seq"), None),
            P(("dp", "seq"), None),
            P(None, None, ("dp", "seq")),
            P(None, ("dp", "seq"), None),
            P(None, None, ("dp", "seq")),
            P(None, ("dp", "seq"), None),
            P(None, "dp", "seq", None),
            P(None, "dp", "seq", None),
        ),
        check_vma=False,
    )
```

profile of v0, /device:TPU:0, one launch (start us, length us, event | category | flops | bytes accessed | tf_op | source)
XLA Modules:
  0.0 2317.1 jit_solution(18235752665196768813)
XLA Ops:
  19.4 46.3 %all-gather = bf16[1,2,1536]{1,0,2:T(2,128)(2,1)S(1)} all-gather(bf16[1,2,48]{1,0,2:T(2,128)(2,1)S(1)} %copy.573), channel_id=2, replica_groups=mesh['dp'=8,'seq'=4] {'dp','seq'}, dimensions={2}, use_global_device_ids=true | all-gather | bytes 6336 | tf_op jit(solution)/shard_map/all_gather | solution.py:211
  65.7 25.1 %fusion.161 = (f32[1536]{0:T(1024)S(1)}, f32[1536]{0:T(1024)S(1)}) fusion(bf16[1,2,1536]{1,0,2:T(2,128)(2,1)S(1)} %all-gather), kind=kLoop, calls=%fused_computation.198 | loop fusion | flops 3072 | bytes 18432 | tf_op jit(solution)/shard_map/mul | solution.py:260
  114.8 6.5 all-to-all-done.1
  140.5 8.6 all-to-all-done.2
  149.4 6.4 all-gather.15.cloned.1.call-done
  166.5 101.5 %all_to_all.190 = bf16[8,1,128,1536]{3,2,1,0:T(8,128)(2,1)S(1)} all-to-all(bf16[8,1,128,1536]{3,2,1,0:T(8,128)(2,1)} %bitcast.573), channel_id=1, replica_groups=mesh['dp'=8,'seq'=4] {'dp'}, dimensions={0} | all-to-all | bytes 6291456 | tf_op jit(solution)/shard_map/all_to_all | solution.py:269
  268.1 8.1 fusion.53
  290.5 102.8 %all-gather.3 = bf16[1,1536,8]{2,0,1:T(2,128)(2,1)} all-gather(bf16[1,48,8]{2,0,1:T(2,128)(2,1)} %copy.576), channel_id=5, replica_groups=mesh['dp'=8,'seq'=4] {'dp','seq'}, dimensions={1}, use_global_device_ids=true | all-gather | bytes 25344 | tf_op jit(solution)/shard_map/all_gather | solution.py:214
  396.0 43.9 %all-gather.4 = bf16[1,2,1536]{1,0,2:T(2,128)(2,1)S(1)} all-gather(bf16[1,2,48]{1,0,2:T(2,128)(2,1)} %copy.577), channel_id=6, replica_groups=mesh['dp'=8,'seq'=4] {'dp','seq'}, dimensions={2}, use_global_device_ids=true | all-gather | bytes 6336 | tf_op jit(solution)/shard_map/all_gather | solution.py:211
  440.4 25.1 %fusion.159 = (f32[1536]{0:T(1024)S(1)}, f32[1536]{0:T(1024)S(1)}) fusion(bf16[1,2,1536]{1,0,2:T(2,128)(2,1)S(1)} %all-gather.4), kind=kLoop, calls=%fused_computation.194 | loop fusion | flops 3072 | bytes 18432 | tf_op jit(solution)/shard_map/mul | solution.py:260
  519.9 11.6 all_to_all.191
  542.8 7.3 all-to-all-start.8
  550.2 92.6 %all-gather.7 = bf16[1,1536,8]{2,0,1:T(2,128)(2,1)S(1)} all-gather(bf16[1,48,8]{2,0,1:T(2,128)(2,1)S(1)} %copy.580), channel_id=9, replica_groups=mesh['dp'=8,'seq'=4] {'dp','seq'}, dimensions={1}, use_global_device_ids=true | all-gather | bytes 25344 | tf_op jit(solution)/shard_map/all_gather | solution.py:214
  665.5 9.7 all-to-all-start.10
  675.2 9.7 fusion.50
  684.9 61.5 %all-to-all-done.10 = bf16[8,1,128,1536]{3,2,1,0:T(8,128)(2,1)S(1)} async-done(((bf16[8,1,128,1536]{3,2,1,0:T(8,128)(2,1)}), bf16[8,1,128,1536]{3,2,1,0:T(8,128)(2,1)S(1)}, u32[]{:S(2)}, u32[]{:S(2)}) %all-to-all-start.10) | async-done | bytes 3145760 | tf_op jit(solution)/shard_map/all_to_all | solution.py:337
  746.4 8.3 fusion.138
  756.4 8.8 fusion.71
  768.8 6.4 fusion.67
  775.3 64.4 %all-to-all-done.11 = bf16[8,1,128,1536]{3,2,1,0:T(8,128)(2,1)S(1)} async-done(((bf16[8,1,128,1536]{3,2,1,0:T(8,128)(2,1)}), bf16[8,1,128,1536]{3,2,1,0:T(8,128)(2,1)S(1)}, u32[]{:S(2)}, u32[]{:S(2)}) %all-to-all-start.11) | async-done | bytes 3145760 | tf_op jit(solution)/shard_map/all_to_all | solution.py:371
  852.3 62.3 %all-to-all-done.9 = bf16[8,1,128,1536]{3,2,1,0:T(8,128)(2,1)} async-done(((bf16[8,1,128,1536]{3,2,1,0:T(8,128)(2,1)}), bf16[8,1,128,1536]{3,2,1,0:T(8,128)(2,1)}, u32[]{:S(2)}, u32[]{:S(2)}) %all-to-all-start.9) | async-done | bytes 3145760 | tf_op jit(solution)/shard_map/all_to_all | solution.py:279
  914.5 6.8 gather_fusion.3
  951.1 7.3 all-to-all-done.12
  964.1 5.8 fusion.115
  1007.6 5.7 multiply_reduce_fusion.5
  1026.1 77.9 %all_to_all.192 = bf16[8,1,128,1536]{3,2,1,0:T(8,128)(2,1)S(1)} all-to-all(bf16[8,1,128,1536]{3,2,1,0:T(8,128)(2,1)} %bitcast.572), channel_id=1, replica_groups=mesh['dp'=8,'seq'=4] {'dp'}, dimensions={0} | all-to-all | bytes 6291456 | tf_op jit(solution)/shard_map/all_to_all | solution.py:337
  1104.0 7.3 fusion.139
  1113.0 6.5 fusion.68
  1137.8 6.4 fusion.99
  1144.3 51.3 %all-to-all-done.16 = bf16[8,1,128,1536]{3,2,1,0:T(8,128)(2,1)S(1)} async-done(((bf16[8,1,128,1536]{3,2,1,0:T(8,128)(2,1)}), bf16[8,1,128,1536]{3,2,1,0:T(8,128)(2,1)S(1)}, u32[]{:S(2)}, u32[]{:S(2)}) %all-to-all-start.16) | async-done | bytes 3145760 | tf_op jit(solution)/shard_map/all_to_all | solution.py:371
  1215.8 6.4 fusion.96
  1223.9 5.9 fusion
  1265.4 5.7 fusion.158
  1272.5 9.1 fusion.15
  1281.6 9.2 fusion.14
  1304.3 7.4 fusion.180
  1312.5 6.5 fusion.179
  1319.9 11.1 reduce-scatter.39.cloned.1.call-done
  1331.8 98.9 %reduce-scatter.41.cloned.1.call-done = f32[48,8]{1,0:T(8,128)} async-done(((f32[1536,8]{1,0:T(8,128)}), f32[48,8]{1,0:T(8,128)}) %reduce-scatter.41.cloned.1.call-update) | async-done | bytes 1552
  1432.2 33.8 %reduce-scatter.35.cloned.1.call-done = bf16[1,192,1536]{2,1,0:T(8,128)(2,1)} async-done(((bf16[1,768,1536]{2,1,0:T(8,128)(2,1)}), bf16[1,192,1536]{2,1,0:T(8,128)(2,1)}) %reduce-scatter.35.cloned.1.call-update) | async-done | bytes 589840 | tf_op jit(solution)/shard_map/reduce_scatter | solution.py:376
  1466.0 35.8 %reduce-scatter.33.cloned.1.call-done = bf16[1,192,1536]{2,1,0:T(8,128)(2,1)} async-done(((bf16[1,768,1536]{2,1,0:T(8,128)(2,1)}), bf16[1,192,1536]{2,1,0:T(8,128)(2,1)}) %reduce-scatter.33.cloned.1.call-update) | async-done | bytes 589840 | tf_op jit(solution)/shard_map/reduce_scatter | solution.py:376
  1505.8 97.1 %reduce-scatter.37.cloned.1.call-done = f32[48,2]{1,0:T(8,128)} async-done(((f32[1536,2]{1,0:T(8,128)}), f32[48,2]{1,0:T(8,128)}) %reduce-scatter.37.cloned.1.call-update) | async-done | bytes 400
  1604.3 48.6 %reduce-scatter.31.cloned.1.call-done = bf16[1,384,1536]{2,1,0:T(8,128)(2,1)} async-done(((bf16[1,1536,1536]{2,1,0:T(8,128)(2,1)}), bf16[1,384,1536]{2,1,0:T(8,128)(2,1)}) %reduce-scatter.31.cloned.1.call-update) | async-done | bytes 1179664 | tf_op jit(solution)/shard_map/reduce_scatter | solution.py:373
  1653.0 50.4 %reduce-scatter.29.cloned.1.call-done = bf16[1,384,1536]{2,1,0:T(8,128)(2,1)} async-done(((bf16[1,1536,1536]{2,1,0:T(8,128)(2,1)}), bf16[1,384,1536]{2,1,0:T(8,128)(2,1)}) %reduce-scatter.29.cloned.1.call-update) | async-done | bytes 1179664 | tf_op jit(solution)/shard_map/reduce_scatter | solution.py:373
  1707.5 137.5 %reduce-scatter.27.cloned.1.call-done = f32[1536,48]{0,1:T(8,128)} async-done(((f32[1536,1536]{0,1:T(8,128)}), f32[1536,48]{0,1:T(8,128)}) %reduce-scatter.27.cloned.1.call-update) | async-done | bytes 294928 | tf_op jit(solution)/shard_map/reduce_scatter | solution.py:454
  1845.0 141.2 %reduce-scatter.25.cloned.1.call-done = f32[1536,48]{0,1:T(8,128)} async-done(((f32[1536,1536]{0,1:T(8,128)}), f32[1536,48]{0,1:T(8,128)}) %reduce-scatter.25.cloned.1.call-update) | async-done | bytes 294928 | tf_op jit(solution)/shard_map/reduce_scatter | solution.py:454
  1988.1 158.5 %reduce-scatter.23.cloned.1.call-done = f32[48,2048]{1,0:T(8,128)} async-done(((f32[1536,2048]{1,0:T(8,128)}), f32[48,2048]{1,0:T(8,128)}) %reduce-scatter.23.cloned.1.call-update) | async-done | bytes 393232 | tf_op jit(solution)/shard_map/reduce_scatter | solution.py:453
  2146.6 161.4 %reduce-scatter.21.cloned.1.call-done = f32[48,2048]{1,0:T(8,128)} async-done(((f32[1536,2048]{1,0:T(8,128)}), f32[48,2048]{1,0:T(8,128)}) %reduce-scatter.21.cloned.1.call-update) | async-done | bytes 393232 | tf_op jit(solution)/shard_map/reduce_scatter | solution.py:453
  (599 shorter events, 383.4 us)
Async XLA Ops:
  7.2 85.1 %copy-start.17 = (bf16[128,1536]{1,0:T(8,128)(2,1)S(1)}, bf16[128,1536]{1,0:T(8,128)(2,1)}, u32[]{:S(2)}) copy-start(bf16[128,1536]{1,0:T(8,128)(2,1)} %param.10) | copy-start | bytes 1179652
  7.2 85.0 %all-gather.13.cloned.1.call-start = ((), (), s32[]{:S(2)}) async-start(), calls=%async_computation.40 | async-start | bytes 6488064 | tf_op jit(solution)/shard_map/all_gather | solution.py:212
  9.1 146.7 %all-gather.15.cloned.1.call-start = ((), (), s32[]{:S(2)}) async-start(), calls=%async_computation.41 | async-start | bytes 4866048 | tf_op jit(solution)/shard_map/all_gather | solution.py:213
  10.9 470.1 %all-gather.17.cloned.1.call-start = ((), (), s32[]{:S(2)}) async-start(), calls=%async_computation.42 | async-start | bytes 6488064 | tf_op jit(solution)/shard_map/all_gather | solution.py:212
  98.0 9.4 all-to-all-start
  107.4 13.9 all-to-all-start.1
  110.9 10.6 collective-permute-start.1
  112.2 11.0 collective-permute-start
  133.1 16.0 all-to-all-start.2
  160.9 304.7 %copy-start.20 = (bf16[128,1536]{1,0:T(8,128)(2,1)}, bf16[128,1536]{1,0:T(8,128)(2,1)S(1)}, u32[]{:S(2)}) copy-start(bf16[128,1536]{1,0:T(8,128)(2,1)S(1)} %multiply_convert_fusion.8) | copy-start | bytes 1179652
  166.5 113.4 %slice-start.10 = ((s8[4718592]{0:T(1024)(128)(4,1)}), s8[4194304]{0:T(1024)(128)(4,1)S(1)}, s32[]{:S(2)}) async-start(s8[4718592]{0:T(1024)(128)(4,1)} %bitcast.653), calls=%async_computation.58 | async-start | bytes 8388608
  283.9 184.6 %all-to-all-start.4 = ((bf16[8,1,128,1536]{3,2,1,0:T(8,128)(2,1)}), bf16[8,1,128,1536]{3,2,1,0:T(8,128)(2,1)S(1)}, u32[]{:S(2)}, u32[]{:S(2)}) async-start(bf16[8,1,128,1536]{3,2,1,0:T(8,128)(2,1)} %fusion.66), calls=%async_computation.4 | async-start | bytes 6291456 | tf_op jit(solution)/shard_map/all_to_all | solution.py:279
  287.9 243.9 %all-gather.19.cloned.1.call-start = ((), (), s32[]{:S(2)}) async-start(), calls=%async_computation.43 | async-start | bytes 4866048 | tf_op jit(solution)/shard_map/all_gather | solution.py:213
  488.8 9.5 all-to-all-start.5
  498.4 10.9 all-to-all-start.6
  501.9 7.8 collective-permute-start.3
  503.2 7.8 collective-permute-start.2
  542.8 101.4 %copy-start.28 = (bf16[128,1536]{1,0:T(8,128)(2,1)S(1)}, bf16[128,1536]{1,0:T(8,128)(2,1)}, u32[]{:S(2)}) copy-start(bf16[128,1536]{1,0:T(8,128)(2,1)} %param.11) | copy-start | bytes 1179652
  542.8 122.7 %all-to-all-start.8 = ((bf16[8,1,128,1536]{3,2,1,0:T(8,128)(2,1)}), bf16[8,1,128,1536]{3,2,1,0:T(8,128)(2,1)}, u32[]{:S(2)}, u32[]{:S(2)}) async-start(bf16[8,1,128,1536]{3,2,1,0:T(8,128)(2,1)} %bitcast.570), calls=%async_computation.8 | async-start | bytes 6291456 | tf_op jit(solution)/shard_map/all_to_all | solution.py:269
  665.5 80.9 %all-to-all-start.10 = ((bf16[8,1,128,1536]{3,2,1,0:T(8,128)(2,1)}), bf16[8,1,128,1536]{3,2,1,0:T(8,128)(2,1)S(1)}, u32[]{:S(2)}, u32[]{:S(2)}) async-start(bf16[8,1,128,1536]{3,2,1,0:T(8,128)(2,1)} %bitcast.571), calls=%async_computation.10 | async-start | bytes 6291456 | tf_op jit(solution)/shard_map/all_to_all | solution.py:337
  765.2 74.5 %all-to-all-start.11 = ((bf16[8,1,128,1536]{3,2,1,0:T(8,128)(2,1)}), bf16[8,1,128,1536]{3,2,1,0:T(8,128)(2,1)S(1)}, u32[]{:S(2)}, u32[]{:S(2)}) async-start(bf16[8,1,128,1536]{3,2,1,0:T(8,128)(2,1)} %fusion.71), calls=%async_computation.11 | async-start | bytes 6291456 | tf_op jit(solution)/shard_map/all_to_all | solution.py:371
  839.7 74.8 %all-to-all-start.9 = ((bf16[8,1,128,1536]{3,2,1,0:T(8,128)(2,1)}), bf16[8,1,128,1536]{3,2,1,0:T(8,128)(2,1)}, u32[]{:S(2)}, u32[]{:S(2)}) async-start(bf16[8,1,128,1536]{3,2,1,0:T(8,128)(2,1)} %fusion.67), calls=%async_computation.9 | async-start | bytes 6291456 | tf_op jit(solution)/shard_map/all_to_all | solution.py:279
  947.4 11.1 all-to-all-start.12
  978.7 11.4 collective-permute-start.4
  980.1 10.2 collective-permute-start.5
  983.4 12.3 all-to-all-start.13
  995.7 9.8 all-to-all-start.14
  1026.1 86.9 %slice-start.7 = ((s8[9437184]{0:T(1024)(128)(4,1)}), s8[4194304]{0:T(1024)(128)(4,1)S(1)}, s32[]{:S(2)}) async-start(s8[9437184]{0:T(1024)(128)(4,1)} %bitcast.651), calls=%async_computation.55 | async-start | bytes 8388608
  1119.5 76.1 %all-to-all-start.16 = ((bf16[8,1,128,1536]{3,2,1,0:T(8,128)(2,1)}), bf16[8,1,128,1536]{3,2,1,0:T(8,128)(2,1)S(1)}, u32[]{:S(2)}, u32[]{:S(2)}) async-start(bf16[8,1,128,1536]{3,2,1,0:T(8,128)(2,1)} %fusion.68), calls=%async_computation.16 | async-start | bytes 6291456 | tf_op jit(solution)/shard_map/all_to_all | solution.py:371
  1123.3 195.8 %reduce-scatter.43.cloned.1.call-start = ((), (), s32[]{:S(2)}) async-start(), calls=%async_computation.47 | async-start | bytes 811008
  1125.9 205.2 %reduce-scatter.39.cloned.1.call-start = ((), (), s32[]{:S(2)}) async-start(), calls=%async_computation.45 | async-start | bytes 811008
  1134.2 296.6 %reduce-scatter.41.cloned.1.call-start = ((), (), s32[]{:S(2)}) async-start(), calls=%async_computation.46 | async-start | bytes 811008
  1137.5 328.4 %reduce-scatter.35.cloned.1.call-start = ((), (), s32[]{:S(2)}) async-start(), calls=%async_computation.39 | async-start | bytes 2949120 | tf_op jit(solution)/shard_map/reduce_scatter | solution.py:376
  1212.1 11.1 all-to-all-start.17
  1215.5 286.3 %reduce-scatter.33.cloned.1.call-start = ((), (), s32[]{:S(2)}) async-start(), calls=%async_computation.38 | async-start | bytes 2949120 | tf_op jit(solution)/shard_map/reduce_scatter | solution.py:376
  1238.0 11.3 collective-permute-start.6
  1239.3 10.3 collective-permute-start.7
  1242.5 12.3 all-to-all-start.18
  1254.8 9.4 all-to-all-start.19
  1258.2 344.7 %reduce-scatter.37.cloned.1.call-start = ((), (), s32[]{:S(2)}) async-start(), calls=%async_computation.44 | async-start | bytes 811008
  1272.4 380.5 %reduce-scatter.31.cloned.1.call-start = ((), (), s32[]{:S(2)}) async-start(), calls=%async_computation.37 | async-start | bytes 5898240 | tf_op jit(solution)/shard_map/reduce_scatter | solution.py:373
  1281.6 421.8 %reduce-scatter.29.cloned.1.call-start = ((), (), s32[]{:S(2)}) async-start(), calls=%async_computation.36 | async-start | bytes 5898240 | tf_op jit(solution)/shard_map/reduce_scatter | solution.py:373
  1290.8 554.1 %reduce-scatter.27.cloned.1.call-start = ((), (), s32[]{:S(2)}) async-start(), calls=%async_computation.35 | async-start | bytes 9732096 | tf_op jit(solution)/shard_map/reduce_scatter | solution.py:454
  1297.1 689.1 %reduce-scatter.25.cloned.1.call-start = ((), (), s32[]{:S(2)}) async-start(), calls=%async_computation.34 | async-start | bytes 9732096 | tf_op jit(solution)/shard_map/reduce_scatter | solution.py:454
  1303.1 843.5 %reduce-scatter.23.cloned.1.call-start = ((), (), s32[]{:S(2)}) async-start(), calls=%async_computation.33 | async-start | bytes 12976128 | tf_op jit(solution)/shard_map/reduce_scatter | solution.py:453
  1311.7 996.4 %reduce-scatter.21.cloned.1.call-start = ((), (), s32[]{:S(2)}) async-start(), calls=%async_computation.32 | async-start | bytes 12976128 | tf_op jit(solution)/shard_map/reduce_scatter | solution.py:453
  1319.0 185.6 %copy-start.116 = (f32[128]{0:T(128)S(1)}, f32[128]{0:T(128)}, u32[]{:S(2)}) copy-start(f32[128]{0:T(128)} %get-tuple-element.104) | copy-start | bytes 1540
  1319.1 185.6 %copy-start.115 = (f32[128]{0:T(128)S(1)}, f32[128]{0:T(128)}, u32[]{:S(2)}) copy-start(f32[128]{0:T(128)} %get-tuple-element.194) | copy-start | bytes 1540
  (126 other events, 1370.0 us)
Sparse Core Ops, SparseCore 0:
  11.4 73.9 all-gather.12
  89.0 66.7 all-gather.14
  158.7 97.4 all-gather.16
  291.4 102.5 all-gather.18
  1128.9 102.6 reduce-scatter.42
  1236.6 94.3 reduce-scatter.38
  1336.1 94.5 reduce-scatter.40
  1433.9 32.0 reduce-scatter.34
  1468.7 33.0 reduce-scatter.32
  1507.3 95.5 reduce-scatter.36
  1606.0 46.8 reduce-scatter.30
  1655.5 47.8 reduce-scatter.28
  1709.3 135.6 reduce-scatter.26
  1851.7 134.4 reduce-scatter.24
  1992.1 154.4 reduce-scatter.22
  2153.5 154.4 reduce-scatter.20
where the time goes:
time: 2330 us; the launch traced here: 2320 us
  waiting for transfers between devices  1280 us (55%)
  blocking collectives  477 us (20%)
  matrix products  188 us (8%)
  other arithmetic  135 us (6%)
  local copies, waits for them, and re-layouts  133 us (6%)
  starting transfers between devices  85 us (4%)
    reduce_scatter x2, waiting for transfers between devices, per_device(): lax.psum_scatter(qkv_grad, ('dp', 'seq'), scatter_dimension=0, tiled=True)  320 us
    reduce_scatter x2, waiting for transfers between devices, per_device(): lax.psum_scatter(out_grad, ('dp', 'seq'), scatter_dimension=1, tiled=True)  279 us
    unnamed x20, waiting for transfers between devices  209 us
    all_gather x2, blocking collectives, per_device(): lax.all_gather(w_router[layer_index], ('dp', 'seq'), axis=0, tiled=True)  195 us
    all_to_all x2, waiting for transfers between devices, per_device(): lax.all_to_all(expert_in_grad, 'dp', split_axis=0, concat_axis=0, tiled=T...  116 us
    all_to_all x1, blocking collectives, per_device(): lax.all_to_all(outgoing, 'dp', split_axis=0, concat_axis=0, tiled=True)  102 us
    reduce_scatter x2, waiting for transfers between devices, per_device(): lax.psum_scatter(gate_up_grad.astype(jnp.bfloat16), 'seq', scatter_dimens...  99.1 us
    all_gather x2, blocking collectives, per_device(): lax.all_gather(norm_gains[layer_index], ('dp', 'seq'), axis=1, tiled=True)  90.2 us
  transfers between devices with their start and end apart: 41, of which 34 were waited for; matrix products, arithmetic and copies ran while one was open for 14% of the time, Pallas kernels for 0%

commit v1 on v0

v1 whole, which is shorter than its diff:
```python
import jax
import jax.numpy as jnp
from jax import lax
from jax.sharding import PartitionSpec as P

HEADS = 12
KV_HEADS = 2
HEAD = 128
WINDOW = 1024
SEQ_LEN = 8192


norm_eps = 1e-06
rope_base = 1000000.0


ALL = ("dp", "seq")
CORES = 2
LINE_MOST = 4
f32 = jnp.float32
bf16 = jnp.bfloat16


def dot(left, right, dims):
    return lax.dot_general(left, right, (dims, ((), ())), preferred_element_type=f32)


class Wires:
    def __init__(self):
        self.dp_count = lax.axis_size("dp")
        self.seq_count = lax.axis_size("seq")
        self.pairs = self.seq_count // CORES
        self.length = self.dp_count // 2
        dp_index = lax.axis_index("dp")
        seq_index = lax.axis_index("seq")
        self.dp_index = dp_index
        self.line = dp_index // 2
        self.side = dp_index % 2
        self.pair = seq_index // CORES
        self.core = seq_index % CORES
        self.chip = dp_index * self.pairs + self.pair
        self.chips = self.dp_count * self.pairs
        self.by_line = self.length <= LINE_MOST and self.pairs == 2

    def to_core(self, value):
        return lax.ppermute(value, "seq", [(i, i ^ 1) for i in range(self.seq_count)])

    def to_pair(self, value):
        return lax.ppermute(value, "seq", [(i, i ^ 2) for i in range(self.seq_count)])

    def to_side(self, value):
        return lax.ppermute(value, "dp", [(i, i ^ 1) for i in range(self.dp_count)])

    def up(self, value, first, last):
        return lax.ppermute(
            value, "dp", [(i, i + 2) for i in range(2 * first, 2 * min(last, self.length - 1))]
        )

    def down(self, value, first, last):
        return lax.ppermute(
            value, "dp", [(i, i - 2) for i in range(2 * max(first, 1), 2 * last)]
        )

    def chips_on(self, value, steps):
        count = self.dp_count * self.seq_count
        offset = steps * CORES
        first, last = (max(0, -offset), min(count, count - offset))
        return lax.ppermute(value, ALL, [(i, i + offset) for i in range(first, last)])

    def ordered(self, flag, own, other, axis):
        return jnp.stack(
            [jnp.where(flag == 0, own, other), jnp.where(flag == 0, other, own)], axis=axis
        )

    def line_gather(self, value):
        count = self.length
        ups, downs = [value], [value]
        for step in range(1, count):
            ups.append(self.up(ups[-1], step - 1, count))
            downs.append(self.down(downs[-1], 0, count - step + 1))
        return [value] + [
            jnp.where(self.line >= k, ups[k], downs[count - k]) for k in range(1, count)
        ]

    def line_scatter(self, blocks):
        count = self.length
        total = blocks[0].astype(f32)
        for rising in (True, False):
            carried = None
            for step in range(1, count):
                piece = blocks[step] if rising else blocks[count - step]
                if carried is not None:
                    piece = (piece.astype(f32) + carried.astype(f32)).astype(bf16)
                if rising:
                    carried = self.up(piece, 0, step)
                else:
                    carried = self.down(piece, count - step, count)
            if carried is not None:
                total = total + carried.astype(f32)
        return total

    def token_gather(self, value):
        if not self.by_line:
            return [lax.all_gather(value, "dp", axis=0, tiled=True)]
        return [
            jnp.concatenate([block, self.to_side(block)], axis=0)
            for block in self.line_gather(value)
        ]

    def token_scatter(self, blocks):
        if not self.by_line:
            return lax.psum_scatter(blocks[0], "dp", scatter_dimension=0, tiled=True).astype(f32)
        rows = blocks[0].shape[0] // 2
        summed = []
        for k, block in enumerate(blocks):
            total = block[:rows].astype(f32) + self.to_side(block[rows:]).astype(f32)
            summed.append(total if k == 0 else total.astype(bf16))
        return self.line_scatter(summed)

    def token_owner(self):
        if not self.by_line:
            return [list(range(self.dp_count))]
        owners = []
        for k in range(self.length):
            place = lax.rem(self.line - k + self.length, self.length)
            owners.append([place * 2 + self.side, place * 2 + 1 - self.side])
        return owners

    def core_groups(self):
        count = self.dp_count * self.seq_count
        return [list(range(core, count, CORES)) for core in range(CORES)]

    def chip_gather(self, block):
        rows, columns = block.shape
        if not self.by_line:
            return lax.all_gather(
                block, ALL, axis=0, tiled=True, axis_index_groups=self.core_groups()
            )
        half = rows // 2
        whole = jnp.zeros((self.chips * rows, columns), block.dtype)
        for k, piece in enumerate(self.line_gather(block)):
            one, two = piece[:half], piece[half:]
            one = self.ordered(self.side, one, self.to_side(one), 0)
            two = self.ordered(self.pair, two, self.to_pair(two), 0)
            one = self.ordered(self.pair, one, self.to_pair(one), 1)
            two = self.ordered(self.side, two, self.to_side(two), 0)
            piece = jnp.stack([one, two], axis=2).reshape(4 * rows, columns)
            place = lax.rem(self.line - k + self.length, self.length)
            whole = lax.dynamic_update_slice(whole, piece, (place * 4 * rows, 0))
        return whole

    def picked(self, flag, stacked, axis):
        first, second = (
            lax.index_in_dim(stacked, 0, axis, keepdims=False),
            lax.index_in_dim(stacked, 1, axis, keepdims=False),
        )
        return jnp.where(flag == 0, first, second), jnp.where(flag == 0, second, first)

    def chip_scatter(self, whole):
        columns = whole.shape[1]
        rows = whole.shape[0] // self.chips
        if not self.by_line:
            return lax.psum_scatter(
                whole,
                ALL,
                scatter_dimension=0,
                tiled=True,
                axis_index_groups=self.core_groups(),
            ).astype(f32)
        half = rows // 2
        summed = []

        def step(flag, stacked, axis, move):
            kept, sent = self.picked(flag, stacked, axis)
            return (kept.astype(f32) + move(sent).astype(f32)).astype(bf16)

        for k in range(self.length):
            place = lax.rem(self.line - k + self.length, self.length)
            piece = lax.dynamic_slice(whole, (place * 4 * rows, 0), (4 * rows, columns))
            piece = piece.reshape(2, 2, 2, half, columns)
            one, two = piece[:, :, 0], piece[:, :, 1]
            one = step(self.pair, one, 1, self.to_pair)
            two = step(self.side, two, 0, self.to_side)
            one = step(self.side, one, 0, self.to_side)
            two = step(self.pair, two, 0, self.to_pair)
            summed.append(jnp.concatenate([one, two], axis=0))
        return self.line_scatter(summed)

    def chip_rows(self, value):
        return jnp.concatenate([value, self.to_core(value)], axis=0)

    def chip_sum(self, value):
        rows = value.shape[0] // 2
        return value[:rows] + self.to_core(value[rows:].astype(bf16)).astype(f32)

    def seq_scatter(self, value):
        rows, columns = value.shape
        if self.pairs != 2:
            return lax.psum_scatter(value, "seq", scatter_dimension=0, tiled=True).astype(f32)
        piece = value.reshape(2, 2, rows // 4, columns)
        kept, sent = self.picked(self.core, piece, 1)
        piece = (kept.astype(f32) + self.to_core(sent).astype(f32)).astype(bf16)
        kept, sent = self.picked(self.pair, piece, 0)
        return kept.astype(f32) + self.to_pair(sent).astype(f32)


def doc_labels(token_index, doc_lengths, seq_length):
    doc_total = doc_lengths.shape[1]
    doc_ends = jnp.cumsum(doc_lengths, axis=1)
    clamped = jnp.maximum(token_index, 0)
    seq_number = clamped // seq_length
    position = clamped % seq_length
    seq_pick = seq_number[:, None] == jnp.arange(doc_lengths.shape[0], dtype=jnp.int32)[None, :]
    token_ends = jnp.sum(jnp.where(seq_pick[:, :, None], doc_ends[None, :, :], 0), axis=1)
    doc_number = jnp.sum((position[:, None] >= token_ends).astype(jnp.int32), axis=1)
    doc_label = jnp.where(token_index >= 0, seq_number * doc_total + doc_number, -1)
    is_valid = (doc_number < doc_total - 1).astype(jnp.float32)
    return (doc_label, is_valid, position)


def rope_turn(vectors, position, direction):
    half_width = vectors.shape[-1] // 2
    frequency = rope_base ** (-jnp.arange(half_width, dtype=jnp.float32) * 2.0 / vectors.shape[-1])
    angles = position.astype(jnp.float32)[:, None] * frequency[None, :]
    cosine = jnp.cos(angles)[:, None, :]
    sine_part = direction * jnp.sin(angles)[:, None, :]
    first_half = vectors[..., :half_width]
    second_half = vectors[..., half_width:]
    return jnp.concatenate(
        [
            first_half * cosine - second_half * sine_part,
            second_half * cosine + first_half * sine_part,
        ],
        axis=-1,
    )


def norm_scale(stream):
    return lax.rsqrt(jnp.mean(stream * stream, axis=-1, keepdims=True) + norm_eps)


def norm_back(stream, scale, gain, out_grad):
    gain_grad = jnp.sum(out_grad * stream * scale, axis=0)
    scaled_grad = out_grad * gain
    stream_grad = scale * scaled_grad - stream * scale**3 * jnp.mean(
        scaled_grad * stream, axis=-1, keepdims=True
    )
    return (gain_grad, stream_grad)


def keep_rule(query_index, key_index, query_label, key_label):
    distance = query_index[:, None] - key_index[None, :]
    same_doc = query_label[:, None] == key_label[None, :]
    return same_doc & (distance >= 0) & (distance < WINDOW)


def attend_forward(queries, keys, values, keep_mask):
    scores = jnp.einsum("qhd,kd->hqk", queries, keys, preferred_element_type=f32) * HEAD ** (-0.5)
    scores = jnp.where(keep_mask[None], scores, -jnp.inf)
    row_top = jnp.max(scores, axis=-1, keepdims=True)
    weights = jnp.exp(scores - row_top)
    row_total = jnp.sum(weights, axis=-1, keepdims=True)
    prob_rows = (weights / row_total).astype(bf16)
    out = jnp.einsum("hqk,kd->qhd", prob_rows, values, preferred_element_type=f32)
    return (out, row_top + jnp.log(row_total))


def attend_backward(queries, keys, values, head_grad, log_total, keep_mask):
    score_scale = HEAD ** (-0.5)
    scores = jnp.einsum("qhd,kd->hqk", queries, keys, preferred_element_type=f32) * score_scale
    prob_rows = jnp.where(keep_mask[None], jnp.exp(scores - log_total), 0.0)
    prob_grad = jnp.einsum("qhd,kd->hqk", head_grad, values, preferred_element_type=f32)
    row_dot = jnp.sum(prob_rows * prob_grad, axis=-1, keepdims=True)
    score_grad = (prob_rows * (prob_grad - row_dot)).astype(bf16)
    query_grad = (
        jnp.einsum("hqk,kd->qhd", score_grad, keys, preferred_element_type=f32) * score_scale
    )
    key_grad = (
        jnp.einsum("hqk,qhd->kd", score_grad, queries, preferred_element_type=f32) * score_scale
    )
    value_grad = jnp.einsum(
        "hqk,qhd->kd", prob_rows.astype(bf16), head_grad, preferred_element_type=f32
    )
    return (query_grad, key_grad, value_grad)


def expert_gates(normed, router, routes, expert_ids):
    logits = dot(normed, router, ((1,), (0,)))
    named = jnp.any(routes[:, :, None] == expert_ids[None, None, :], axis=1)
    top = jnp.max(jnp.where(named, logits, -jnp.inf), axis=1, keepdims=True)
    weights = jnp.where(named, jnp.exp(logits - top), 0.0)
    return weights / jnp.sum(weights, axis=1, keepdims=True), named


def per_device(
    activations,
    cotangent,
    doc_lengths,
    routes,
    norm_gains,
    w_qkv,
    w_out,
    w_router,
    w_gate_up,
    w_down,
):
    wires = Wires()
    tok_rows, model_width = activations.shape
    layer_count = w_qkv.shape[0]
    heads_here = HEADS // CORES
    q_width = heads_here * HEAD
    qkv_width = q_width + 2 * HEAD
    ff_width = w_down.shape[2]
    expert_count = w_router.shape[2]
    chip_tokens = CORES * tok_rows
    device_count = wires.dp_count * wires.seq_count
    seq_length = min(SEQ_LEN, tok_rows * device_count)
    depth = min(-(-(WINDOW - 1) // chip_tokens), wires.chips - 1)
    core = wires.core

    def chip_index_of(first_chip, chips):
        block = first_chip + jnp.arange(chips, dtype=jnp.int32)
        order = jnp.stack([core, 1 - core]).astype(jnp.int32)
        start = block[:, None] * chip_tokens + order[None, :] * tok_rows
        return (start[:, :, None] + jnp.arange(tok_rows, dtype=jnp.int32)).reshape(-1)

    query_index = chip_index_of(wires.chip, 1)
    key_index = chip_index_of(wires.chip - depth, depth + 1)
    query_label, query_valid, position = doc_labels(query_index, doc_lengths, seq_length)
    key_label = doc_labels(key_index, doc_lengths, seq_length)[0]
    keep_mask = keep_rule(query_index, key_index, query_label, key_label)
    expert_ids = jnp.arange(expert_count, dtype=jnp.int32)
    my_expert = (expert_ids == wires.dp_index)[None, :]
    all_routes = lax.all_gather(routes, "dp", axis=0)
    block_routes = [
        jnp.concatenate(
            [lax.dynamic_index_in_dim(all_routes, owner, 0, keepdims=False) for owner in owners]
        )
        for owners in wires.token_owner()
    ]

    small_width = -(-(expert_count + 2) // 128) * 128

    def packed_weights(layer_index):
        out_rows = w_out[layer_index].T
        qkv = w_qkv[layer_index]
        small = jnp.concatenate([w_router[layer_index], norm_gains[layer_index].T], axis=1)
        small = jnp.pad(small, ((0, 0), (0, small_width - small.shape[1])))
        fronts, backs = [], []
        for c in range(CORES):
            fronts.append(
                jnp.concatenate(
                    [
                        qkv[:, c * q_width : (c + 1) * q_width],
                        qkv[:, HEADS * HEAD + c * HEAD :][:, :HEAD],
                        qkv[:, (HEADS + KV_HEADS + c) * HEAD :][:, :HEAD],
                        small,
                    ],
                    axis=1,
                )
            )
            backs.append(out_rows[:, c * q_width : (c + 1) * q_width])
        result = []
        for first, second in (fronts, backs):
            kept = jnp.where(core == 0, first, second)
            sent = jnp.where(core == 0, second, first)
            block = wires.ordered(core, kept, wires.to_core(sent), 0)
            result.append(block.reshape(2 * kept.shape[0], kept.shape[1]))
        return result

    held_weights = []
    for layer_index in range(layer_count):
        front, back = packed_weights(layer_index)
        front = wires.chip_gather(front)
        back = wires.chip_gather(back)
        small = front[:, qkv_width:]
        held_weights.append(
            (
                small[:, expert_count : expert_count + 2].astype(f32).T,
                front[:, :qkv_width],
                back,
                small[:, :expert_count],
            )
        )
    stream = activations.astype(f32)
    stored = []
    for layer_index in range(layer_count):
        gain_rows, qkv_here, out_here, router = held_weights[layer_index]
        gate_up_here = w_gate_up[layer_index, 0]
        down_here = w_down[layer_index, 0]
        scale_one = norm_scale(stream)
        normed_one = wires.chip_rows((stream * scale_one * gain_rows[0]).astype(bf16))
        mixed = dot(normed_one, qkv_here, ((1,), (0,)))
        queries = rope_turn(
            mixed[:, :q_width].reshape(chip_tokens, heads_here, HEAD), position, 1.0
        ).astype(bf16)
        own_keys = rope_turn(mixed[:, None, q_width : q_width + HEAD], position, 1.0)[:, 0]
        own_pair = jnp.concatenate([own_keys, mixed[:, q_width + HEAD :]], axis=1).astype(bf16)
        table = jnp.concatenate(
            [wires.chips_on(own_pair, step) for step in range(depth, 0, -1)] + [own_pair], axis=0
        )
        keys, values = table[:, :HEAD], table[:, HEAD:]
        attended, log_total = attend_forward(queries, keys, values, keep_mask)
        attended = (
            (attended * query_valid[:, None, None]).astype(bf16).reshape(chip_tokens, q_width)
        )
        stream_mid = stream + wires.chip_sum(dot(attended, out_here, ((1,), (1,))))
        scale_two = norm_scale(stream_mid)
        normed_two = (stream_mid * scale_two * gain_rows[1]).astype(bf16)
        blocks = wires.token_gather(normed_two)
        block_gates, up_gates, block_outs = [], [], []
        for block, route_rows in zip(blocks, block_routes):
            gates = expert_gates(block, router, route_rows, expert_ids)[0]
            gate = jnp.sum(jnp.where(my_expert, gates, 0.0), axis=1, keepdims=True)
            up_gate = dot(block, gate_up_here, ((1,), (0,)))
            hidden = (jax.nn.silu(up_gate[:, :ff_width]) * up_gate[:, ff_width:]).astype(bf16)
            out = dot(hidden, down_here, ((1,), (0,)))
            block_gates.append(gate)
            up_gates.append(up_gate)
            block_outs.append((out * gate).astype(bf16))
        stored.append(
            (
                stream,
                stream_mid,
                scale_one,
                scale_two,
                normed_one,
                normed_two,
                queries,
                keys,
                values,
                log_total,
                attended,
                blocks,
                block_gates,
                up_gates,
            )
        )
        stream = stream_mid + wires.token_scatter(block_outs)
    layer_out = stream.astype(bf16)
    stream_grad = cotangent.astype(f32)
    grad_layers = []
    for layer_index in range(layer_count - 1, -1, -1):
        (
            stream,
            stream_mid,
            scale_one,
            scale_two,
            normed_one,
            normed_two,
            queries,
            keys,
            values,
            log_total,
            attended,
            blocks,
            block_gates,
            up_gates,
        ) = stored[layer_index]
        gain_rows, qkv_here, out_here, router = held_weights[layer_index]
        gate_up_here = w_gate_up[layer_index, 0]
        down_here = w_down[layer_index, 0]
        grad_blocks = wires.token_gather(stream_grad.astype(bf16))
        pair_grads, hiddens, in_grads, gate_grads = [], [], [], []
        for grad_block, gate, up_gate in zip(grad_blocks, block_gates, up_gates):
            gate_part = up_gate[:, :ff_width]
            up_part = up_gate[:, ff_width:]
            sigmoid_gate = jax.nn.sigmoid(gate_part)
            activated = gate_part * sigmoid_gate
            hidden = activated * up_part
            back = dot(grad_block, down_here, ((1,), (1,)))
            gate_grads.append(jnp.sum(hidden * back, axis=1))
            hidden_grad = back * gate
            pair_grad = jnp.concatenate(
                [
                    hidden_grad * up_part * sigmoid_gate * (1.0 + gate_part * (1.0 - sigmoid_gate)),
                    hidden_grad * activated,
                ],
                axis=1,
            ).astype(bf16)
            pair_grads.append(pair_grad)
            hiddens.append((hidden * gate).astype(bf16))
            in_grads.append(dot(pair_grad, gate_up_here, ((1,), (1,))).astype(bf16))
        gate_rows = jnp.zeros((wires.dp_count, tok_rows), f32)
        for owners, gate_grad in zip(wires.token_owner(), gate_grads):
            for place, owner in enumerate(owners):
                gate_rows = lax.dynamic_update_slice(
                    gate_rows, gate_grad[place * tok_rows :][None, :tok_rows], (owner, 0)
                )
        gate_rows = lax.all_to_all(gate_rows, "dp", split_axis=0, concat_axis=0, tiled=True)
        normed_grad = wires.token_scatter(in_grads)
        pair_all = jnp.concatenate(pair_grads, axis=0)
        gate_up_grad = dot(jnp.concatenate(blocks, axis=0), pair_all, ((0,), (0,))).astype(bf16)
        down_grad = dot(
            jnp.concatenate(hiddens, axis=0), jnp.concatenate(grad_blocks, axis=0), ((0,), (0,))
        ).astype(bf16)
        gate_up_sum = wires.seq_scatter(gate_up_grad)
        down_sum = wires.seq_scatter(down_grad)
        gates, named = expert_gates(normed_two, router, routes, expert_ids)
        gate_grad = jnp.where(named, gate_rows.T, 0.0)
        logit_grad = gates * (gate_grad - jnp.sum(gates * gate_grad, axis=1, keepdims=True))
        logit_grad = logit_grad.astype(bf16)
        router_grad = dot(normed_two, logit_grad, ((0,), (0,)))
        normed_grad = normed_grad + dot(logit_grad, router, ((1,), (1,)))
        gain_two_grad, mid_grad = norm_back(stream_mid, scale_two, gain_rows[1], normed_grad)
        mid_grad = stream_grad + mid_grad
        attn_grad = wires.chip_rows(mid_grad.astype(bf16))
        head_grad = dot(attn_grad, out_here, ((1,), (0,))) * query_valid[:, None]
        head_grad = head_grad.astype(bf16).reshape(chip_tokens, heads_here, HEAD)
        out_grad = dot(attn_grad, attended, ((0,), (0,))).astype(bf16)
        query_grad, key_grad, value_grad = attend_backward(
            queries, keys, values, head_grad, log_total, keep_mask
        )
        pair_sums = jnp.concatenate([key_grad, value_grad], axis=1)
        own_grad = pair_sums[depth * chip_tokens :]
        for step in range(depth, 0, -1):
            first = (depth - step) * chip_tokens
            part = pair_sums[first : first + chip_tokens].astype(bf16)
            own_grad = own_grad + wires.chips_on(part, -step).astype(f32)
        query_lin = rope_turn(query_grad, position, -1.0).reshape(chip_tokens, q_width)
        key_lin = rope_turn(own_grad[:, None, :HEAD], position, -1.0)[:, 0]
        mixed_grad = jnp.concatenate([query_lin, key_lin, own_grad[:, HEAD:]], axis=1).astype(bf16)
        normed_one_grad = wires.chip_sum(dot(mixed_grad, qkv_here, ((1,), (1,))))
        gain_one_grad, front_grad = norm_back(stream, scale_one, gain_rows[0], normed_one_grad)
        stream_grad = mid_grad + front_grad
        qkv_grad = dot(normed_one, mixed_grad, ((0,), (0,))).astype(bf16)
        small = jnp.concatenate([router_grad, jnp.stack([gain_one_grad, gain_two_grad]).T], axis=1)
        small = jnp.pad(small, ((0, 0), (0, small_width - small.shape[1]))).astype(bf16)

        def shared(value):
            rows = value.shape[0] // 2
            kept, sent = wires.picked(core, value.reshape(2, rows, value.shape[1]), 0)
            return kept, wires.to_core(sent.astype(bf16)).astype(f32)

        back_own, back_other = shared(wires.chip_scatter(out_grad))
        front_own, front_other = shared(
            wires.chip_scatter(jnp.concatenate([qkv_grad, small], axis=1))
        )
        out_sum = wires.ordered(core, back_own, back_other, 1)
        out_sum = out_sum.reshape(out_sum.shape[0], HEADS * HEAD).T
        small_sum = (front_own + front_other)[:, qkv_width:]
        qkv_pair = wires.ordered(core, front_own[:, :qkv_width], front_other[:, :qkv_width], 1)
        rows = qkv_pair.shape[0]
        qkv_sum = jnp.concatenate(
            [
                qkv_pair[:, :, :q_width].reshape(rows, HEADS * HEAD),
                qkv_pair[:, :, q_width : q_width + HEAD].reshape(rows, KV_HEADS * HEAD),
                qkv_pair[:, :, q_width + HEAD :].reshape(rows, KV_HEADS * HEAD),
            ],
            axis=1,
        )
        gain_sum = small_sum[:, expert_count : expert_count + 2].T
        router_sum = small_sum[:, :expert_count]
        grad_layers.append((gain_sum, qkv_sum, out_sum, router_sum, gate_up_sum, down_sum))
    grad_layers = grad_layers[::-1]
    stacked = [jnp.stack([grad_entry[member] for grad_entry in grad_layers]) for member in range(6)]
    return (
        layer_out,
        stream_grad,
        stacked[0],
        stacked[1],
        stacked[2],
        stacked[3],
        stacked[4][:, None],
        stacked[5][:, None],
    )


def solution(mesh):
    return jax.shard_map(
        per_device,
        mesh=mesh,
        in_specs=(
            P(("dp", "seq"), None),
            P(("dp", "seq"), None),
            P(),
            P(("dp", "seq"), None),
            P(None, None, ("dp", "seq")),
            P(None, ("dp", "seq"), None),
            P(None, None, ("dp", "seq")),
            P(None, ("dp", "seq"), None),
            P(None, "dp", None, None),
            P(None, "dp", None, None),
        ),
        out_specs=(
            P(("dp", "seq"), None),
            P(("dp", "seq"), None),
            P(None, None, ("dp", "seq")),
            P(None, ("dp", "seq"), None),
            P(None, None, ("dp", "seq")),
            P(None, ("dp", "seq"), None),
            P(None, "dp", "seq", None),
            P(None, "dp", "seq", None),
        ),
        check_vma=False,
    )
```

time: 2330 us -> 1460 us (0.63)
  waiting for transfers between devices: 1280 us -> 442 us
  blocking collectives: 477 us -> 28.4 us
  starting transfers between devices: 85 us -> 494 us
  other arithmetic: 135 us -> 177 us
  matrix products: 188 us -> 164 us
    reduce_scatter x8 -> x0, waiting for transfers between devices: 767 us -> none  [the longest x2 320 us: per_device(): lax.psum_scatter(qkv_grad, ('dp', 'seq'), scatter_dimension=0, tiled=True)]
    ppermute x8 -> x296, starting transfers between devices: 10.8 us -> 484 us  [the longest x48 188 us: up(): lax.ppermute(value, 'dp', [(i, i + 2) for i in range(2 * first, 2 * min(l...]
    ppermute x8 -> x296, waiting for transfers between devices: 8.62 us -> 442 us  [the longest x96 153 us: to_side(): return lax.ppermute(value, 'dp', [(i, i ^ 1) for i in range(self.dp_count)])]
    all_to_all x17 -> x2, waiting for transfers between devices: 292 us -> 0.01 us  [per_device(): lax.all_to_all(gate_rows, 'dp', split_axis=0, concat_axis=0, tiled=True)]
    all_gather x4 -> x1, blocking collectives: 286 us -> 28.4 us  [per_device(): all_routes = lax.all_gather(routes, 'dp', axis=0)]
    unnamed x20 -> x0, waiting for transfers between devices: 209 us -> none
    all_to_all x3 -> x0, blocking collectives: 191 us -> none  [the longest x1 102 us: per_device(): lax.all_to_all(outgoing, 'dp', split_axis=0, concat_axis=0, tiled=True)]
    all_to_all x17 -> x2, starting transfers between devices: 72.6 us -> 9.6 us  [per_device(): lax.all_to_all(gate_rows, 'dp', split_axis=0, concat_axis=0, tiled=True)]
  transfers between devices with their start and end apart: 41 -> 298, of which waited for: 34 -> 129; matrix products, arithmetic and copies ran while one was open for 14% -> 31% of each run, Pallas kernels for 0% -> 0%
where the time goes in v1:
time: 1460 us; the launch traced here: 1450 us
  starting transfers between devices  494 us (34%)
  waiting for transfers between devices  442 us (30%)
  other arithmetic  177 us (12%)
  matrix products  164 us (11%)
  local copies, waits for them, and re-layouts  132 us (9%)
  blocking collectives  28.4 us (2%)
    ppermute x48, starting transfers between devices, up(): lax.ppermute(value, 'dp', [(i, i + 2) for i in range(2 * first, 2 * min(l...  188 us
    ppermute x96, waiting for transfers between devices, to_side(): return lax.ppermute(value, 'dp', [(i, i ^ 1) for i in range(self.dp_count)])  153 us
    dot_general x62, matrix products, dot(): lax.dot_general(left, right, (dims, ((), ())), preferred_element_type=f32)  126 us
    ppermute x48, waiting for transfers between devices, down(): lax.ppermute(value, 'dp', [(i, i - 2) for i in range(2 * max(first, 1), 2...  112 us
    ppermute x68, waiting for transfers between devices, to_pair(): lax.ppermute(value, 'seq', [(i, i ^ 2) for i in range(self.seq_count)])  105 us
    ppermute x96, starting transfers between devices, to_side(): return lax.ppermute(value, 'dp', [(i, i ^ 1) for i in range(self.dp_count)])  99.4 us
    ppermute x68, starting transfers between devices, to_pair(): lax.ppermute(value, 'seq', [(i, i ^ 2) for i in range(self.seq_count)])  82.8 us
    ppermute x48, waiting for transfers between devices, up(): lax.ppermute(value, 'dp', [(i, i + 2) for i in range(2 * first, 2 * min(l...  62 us
  transfers between devices with their start and end apart: 298, of which 129 were waited for; matrix products, arithmetic and copies ran while one was open for 31% of the time, Pallas kernels for 0%

profile of v1, /device:TPU:0, one launch (start us, length us, event | category | flops | bytes accessed | tf_op | source)
XLA Modules:
  0.0 1447.8 jit_solution(6141423681159658604)
XLA Ops:
  2.3 6.8 collective-permute-start.100
  12.3 5.6 collective-permute-start.72
  24.8 28.4 %all-gather = s32[1024,4]{0,1:T(4,128)S(1)} all-gather(s32[128,4]{0,1:T(4,128)S(1)} %copy-done.247), channel_id=2, replica_groups=mesh['dp'=8,'seq'=4] {'dp'}, dimensions={0}, use_global_device_ids=true | all-gather | bytes 18432 | tf_op jit(solution)/shard_map/all_gather | solution.py:334
  90.2 5.7 collective-permute-done.1
  96.5 5.3 collective-permute-done.102
  102.1 5.2 collective-permute-done.104
  107.6 5.1 collective-permute-done.32
  113.9 5.3 collective-permute-start.105
  128.3 7.6 collective-permute-done.107
  141.6 5.1 collective-permute-done.74
  176.9 7.1 collective-permute-done.36
  185.3 7.2 collective-permute-done.108
  247.3 5.8 collective-permute-done.40
  253.4 5.2 collective-permute-done.38
  359.2 6.7 collective-permute-start.25
  400.6 6.9 collective-permute-done.57
  435.1 5.3 collective-permute-done.156
  476.7 6.6 collective-permute-done.65
  509.9 5.1 collective-permute-start.68
  520.3 12.8 collective-permute-done.71
  546.4 5.8 collective-permute-start.97
  583.2 6.7 collective-permute-done.129
  594.4 8.1 collective-permute-done.132
  605.0 9.3 collective-permute-done.135
  617.2 6.4 collective-permute-done.136
  626.4 6.4 collective-permute-done.133
  635.7 5.1 collective-permute-done.130
  672.8 14.3 convolution_convert_fusion
  692.3 5.9 all-to-all-start
  698.2 5.2 convolution_convert_fusion.4
  723.7 5.8 collective-permute-done.138
  735.6 6.5 collective-permute-done.158
  749.1 6.4 collective-permute-done.139
  776.5 38.4 %collective-permute-start.160 = (bf16[128,1536]{1,0:T(8,128)(2,1)S(1)}, bf16[128,1536]{1,0:T(8,128)(2,1)S(1)}, u32[]{:S(2)}, u32[]{:S(2)}) collective-permute-start(bf16[128,1536]{1,0:T(8,128)(2,1)S(1)} %get-tuple-element.107), channel_id=1, source_target_pairs={{0,8},{4,12},{8,16},{12,20},{16,24},{20,28},{1,9},{5,13},{9,17},{1... | collective-permute-start | bytes 1179656 | tf_op jit(solution)/shard_map/ppermute | solution.py:55
  845.7 5.7 fusion.131
  937.4 5.0 collective-permute-start.283
  947.7 5.9 collective-permute-start.172
  985.2 7.3 collective-permute-done.221
  994.2 5.0 collective-permute-done.219
  1076.4 5.2 collective-permute-start.236
  1101.3 10.4 collective-permute-done.181
  1115.3 8.5 collective-permute-done.182
  1164.1 7.8 convolution_convert_fusion.1
  1172.0 5.5 fusion.107
  1205.9 5.7 collective-permute-done.186
  1211.5 9.0 collective-permute-done.189
  1234.5 5.7 fusion.128
  1378.0 5.8 collective-permute-start.208
  (1976 shorter events, 1066.3 us)
Async XLA Ops:
  1.8 57.7 %collective-permute-start.28 = (bf16[48,768]{1,0:T(8,128)(2,1)S(1)}, bf16[48,768]{1,0:T(8,128)(2,1)S(1)}, u32[]{:S(2)}, u32[]{:S(2)}) collective-permute-start(bf16[48,768]{1,0:T(8,128)(2,1)S(1)} %broadcast_select_fusion.38), channel_id=1, source_target_pairs={{0,1},{1,0},{2,3},{3,2},{4,5},{5,4},{6,7},{7,6},{8,9},{9,8},{10,11... | collective-permute-start | bytes 221192 | tf_op jit(solution)/shard_map/ppermute | solution.py:46
  2.3 57.3 %collective-permute-start.100 = (bf16[48,768]{1,0:T(8,128)(2,1)S(1)}, bf16[48,768]{1,0:T(8,128)(2,1)S(1)}, u32[]{:S(2)}, u32[]{:S(2)}) collective-permute-start(bf16[48,768]{1,0:T(8,128)(2,1)S(1)} %broadcast_select_fusion.34), channel_id=1, source_target_pairs={{0,1},{1,0},{2,3},{3,2},{4,5},{5,4},{6,7},{7,6},{8,9},{9,8},{10,11... | collective-permute-start | bytes 221192 | tf_op jit(solution)/shard_map/ppermute | solution.py:46
  11.7 52.2 %collective-permute-start = (bf16[48,1152]{1,0:T(8,128)(2,1)S(1)}, bf16[48,1152]{1,0:T(8,128)(2,1)S(1)}, u32[]{:S(2)}, u32[]{:S(2)}) collective-permute-start(bf16[48,1152]{1,0:T(8,128)(2,1)S(1)} %broadcast_select_fusion.30), channel_id=1, source_target_pairs={{0,1},{1,0},{2,3},{3,2},{4,5},{5,4},{6,7},{7,6},{8,9},{9,8},{10,11... | collective-permute-start | bytes 331784 | tf_op jit(solution)/shard_map/ppermute | solution.py:46
  12.3 48.9 %collective-permute-start.72 = (bf16[48,1152]{1,0:T(8,128)(2,1)S(1)}, bf16[48,1152]{1,0:T(8,128)(2,1)S(1)}, u32[]{:S(2)}, u32[]{:S(2)}) collective-permute-start(bf16[48,1152]{1,0:T(8,128)(2,1)S(1)} %broadcast_select_fusion.26), channel_id=1, source_target_pairs={{0,1},{1,0},{2,3},{3,2},{4,5},{5,4},{6,7},{7,6},{8,9},{9,8},{10,11... | collective-permute-start | bytes 331784 | tf_op jit(solution)/shard_map/ppermute | solution.py:46
  17.9 186.8 %collective-permute-start.146 = (bf16[128,1536]{1,0:T(8,128)(2,1)}, bf16[128,1536]{1,0:T(8,128)(2,1)}, u32[]{:S(2)}, u32[]{:S(2)}) collective-permute-start(bf16[128,1536]{1,0:T(8,128)(2,1)} %param.11), channel_id=1, source_target_pairs={{0,8},{4,12},{8,16},{12,20},{16,24},{20,28},{1,9},{5,13},{9,17},{1... | collective-permute-start | bytes 1179656 | tf_op jit(solution)/shard_map/ppermute | solution.py:55
  68.3 45.6 %collective-permute-start.34 = (bf16[96,768]{1,0:T(8,128)(2,1)S(1)}, bf16[96,768]{1,0:T(8,128)(2,1)S(1)}, u32[]{:S(2)}, u32[]{:S(2)}) collective-permute-start(bf16[96,768]{1,0:T(8,128)(2,1)S(1)} %bitcast.1616), channel_id=1, source_target_pairs={{8,0},{12,4},{16,8},{20,12},{24,16},{28,20},{9,1},{13,5},{17,9},{2... | collective-permute-start | bytes 442376 | tf_op jit(solution)/shard_map/ppermute | solution.py:60
  69.7 49.6 %collective-permute-start.33 = (bf16[96,768]{1,0:T(8,128)(2,1)S(1)}, bf16[96,768]{1,0:T(8,128)(2,1)S(1)}, u32[]{:S(2)}, u32[]{:S(2)}) collective-permute-start(bf16[96,768]{1,0:T(8,128)(2,1)S(1)} %bitcast.1617), channel_id=1, source_target_pairs={{0,8},{4,12},{8,16},{12,20},{16,24},{20,28},{1,9},{5,13},{9,17},{1... | collective-permute-start | bytes 442376 | tf_op jit(solution)/shard_map/ppermute | solution.py:55
  74.3 47.6 %collective-permute-start.106 = (bf16[96,768]{1,0:T(8,128)(2,1)S(1)}, bf16[96,768]{1,0:T(8,128)(2,1)S(1)}, u32[]{:S(2)}, u32[]{:S(2)}) collective-permute-start(bf16[96,768]{1,0:T(8,128)(2,1)S(1)} %bitcast.1614), channel_id=1, source_target_pairs={{8,0},{12,4},{16,8},{20,12},{24,16},{28,20},{9,1},{13,5},{17,9},{2... | collective-permute-start | bytes 442376 | tf_op jit(solution)/shard_map/ppermute | solution.py:60
  122.3 83.1 %collective-permute-start.149 = (bf16[128,1536]{1,0:T(8,128)(2,1)}, bf16[128,1536]{1,0:T(8,128)(2,1)}, u32[]{:S(2)}, u32[]{:S(2)}) collective-permute-start(bf16[128,1536]{1,0:T(8,128)(2,1)} %param.11), channel_id=1, source_target_pairs={{8,0},{12,4},{16,8},{20,12},{24,16},{28,20},{9,1},{13,5},{17,9},{2... | collective-permute-start | bytes 1179656 | tf_op jit(solution)/shard_map/ppermute | solution.py:60
  135.9 59.5 %collective-permute-start.6 = (bf16[96,1152]{1,0:T(8,128)(2,1)}, bf16[96,1152]{1,0:T(8,128)(2,1)}, u32[]{:S(2)}, u32[]{:S(2)}) collective-permute-start(bf16[96,1152]{1,0:T(8,128)(2,1)} %bitcast.17), channel_id=1, source_target_pairs={{8,0},{12,4},{16,8},{20,12},{24,16},{28,20},{9,1},{13,5},{17,9},{2... | collective-permute-start | bytes 663560 | tf_op jit(solution)/shard_map/ppermute | solution.py:60
  170.6 29.4 %collective-permute-start.5 = (bf16[96,1152]{1,0:T(8,128)(2,1)}, bf16[96,1152]{1,0:T(8,128)(2,1)S(1)}, u32[]{:S(2)}, u32[]{:S(2)}) collective-permute-start(bf16[96,1152]{1,0:T(8,128)(2,1)} %bitcast.17), channel_id=1, source_target_pairs={{0,8},{4,12},{8,16},{12,20},{16,24},{20,28},{1,9},{5,13},{9,17},{1... | collective-permute-start | bytes 663560 | tf_op jit(solution)/shard_map/ppermute | solution.py:55
  205.4 108.7 %collective-permute-start.147 = (bf16[128,1536]{1,0:T(8,128)(2,1)}, bf16[128,1536]{1,0:T(8,128)(2,1)}, u32[]{:S(2)}, u32[]{:S(2)}) collective-permute-start(bf16[128,1536]{1,0:T(8,128)(2,1)} %collective-permute-done.146), channel_id=1, source_target_pairs={{8,16},{12,20},{16,24},{20,28},{9,17},{13,21},{17,25},{21,29},{10,... | collective-permute-start | bytes 1179656 | tf_op jit(solution)/shard_map/ppermute | solution.py:55
  208.1 106.8 %collective-permute-start.152 = (bf16[128,1536]{1,0:T(8,128)(2,1)}, bf16[128,1536]{1,0:T(8,128)(2,1)}, u32[]{:S(2)}, u32[]{:S(2)}) collective-permute-start(bf16[128,1536]{1,0:T(8,128)(2,1)} %collective-permute-done.149), channel_id=1, source_target_pairs={{8,0},{12,4},{16,8},{20,12},{9,1},{13,5},{17,9},{21,13},{10,2},{14... | collective-permute-start | bytes 1179656 | tf_op jit(solution)/shard_map/ppermute | solution.py:60
  209.6 49.1 %collective-permute-start.45 = (bf16[2,48,768]{2,1,0:T(8,128)(2,1)S(1)}, bf16[2,48,768]{2,1,0:T(8,128)(2,1)S(1)}, u32[]{:S(2)}, u32[]{:S(2)}) collective-permute-start(bf16[2,48,768]{2,1,0:T(8,128)(2,1)S(1)} %pad_maximum_fusion.96), channel_id=1, source_target_pairs={{0,4},{4,0},{8,12},{12,8},{16,20},{20,16},{24,28},{28,24},{1,5},{5... | collective-permute-start | bytes 442376 | tf_op jit(solution)/shard_map/ppermute | solution.py:52
  258.7 26.9 %collective-permute-start.8 = (bf16[96,1152]{1,0:T(8,128)(2,1)S(1)}, bf16[96,1152]{1,0:T(8,128)(2,1)S(1)}, u32[]{:S(2)}, u32[]{:S(2)}) collective-permute-start(bf16[96,1152]{1,0:T(8,128)(2,1)S(1)} %collective-permute-done.7), channel_id=1, source_target_pairs={{8,0},{12,4},{9,1},{13,5},{10,2},{14,6},{11,3},{15,7}} | collective-permute-start | bytes 663560 | tf_op jit(solution)/shard_map/ppermute | solution.py:60
  315.8 218.4 %collective-permute-start.148 = (bf16[128,1536]{1,0:T(8,128)(2,1)}, bf16[128,1536]{1,0:T(8,128)(2,1)}, u32[]{:S(2)}, u32[]{:S(2)}) collective-permute-start(bf16[128,1536]{1,0:T(8,128)(2,1)} %collective-permute-done.147), channel_id=1, source_target_pairs={{16,24},{20,28},{17,25},{21,29},{18,26},{22,30},{19,27},{23,31}} | collective-permute-start | bytes 1179656 | tf_op jit(solution)/shard_map/ppermute | solution.py:55
  317.2 105.5 %collective-permute-start.155 = (bf16[128,1536]{1,0:T(8,128)(2,1)}, bf16[128,1536]{1,0:T(8,128)(2,1)}, u32[]{:S(2)}, u32[]{:S(2)}) collective-permute-start(bf16[128,1536]{1,0:T(8,128)(2,1)} %collective-permute-done.152), channel_id=1, source_target_pairs={{8,0},{12,4},{9,1},{13,5},{10,2},{14,6},{11,3},{15,7}} | collective-permute-start | bytes 1179656 | tf_op jit(solution)/shard_map/ppermute | solution.py:60
  536.2 37.5 %collective-permute-start.150 = (bf16[128,1536]{1,0:T(8,128)(2,1)}, bf16[128,1536]{1,0:T(8,128)(2,1)}, u32[]{:S(2)}, u32[]{:S(2)}) collective-permute-start(bf16[128,1536]{1,0:T(8,128)(2,1)} %get-tuple-element.74), channel_id=1, source_target_pairs={{0,4},{4,0},{8,12},{12,8},{16,20},{20,16},{24,28},{28,24},{1,5},{5... | collective-permute-start | bytes 1179656 | tf_op jit(solution)/shard_map/ppermute | solution.py:52
  648.9 100.1 %collective-permute-start.131 = (bf16[128,1536]{1,0:T(8,128)(2,1)}, bf16[128,1536]{1,0:T(8,128)(2,1)}, u32[]{:S(2)}, u32[]{:S(2)}) collective-permute-start(bf16[128,1536]{1,0:T(8,128)(2,1)} %slice.1687), channel_id=1, source_target_pairs={{0,4},{4,0},{8,12},{12,8},{16,20},{20,16},{24,28},{28,24},{1,5},{5... | collective-permute-start | bytes 1179656 | tf_op jit(solution)/shard_map/ppermute | solution.py:52
  651.4 109.8 %collective-permute-start.151 = (bf16[128,1536]{1,0:T(8,128)(2,1)}, bf16[128,1536]{1,0:T(8,128)(2,1)}, u32[]{:S(2)}, u32[]{:S(2)}) collective-permute-start(bf16[128,1536]{1,0:T(8,128)(2,1)} %slice.1699), channel_id=1, source_target_pairs={{0,4},{4,0},{8,12},{12,8},{16,20},{20,16},{24,28},{28,24},{1,5},{5... | collective-permute-start | bytes 1179656 | tf_op jit(solution)/shard_map/ppermute | solution.py:52
  656.8 65.3 %collective-permute-start.134 = (bf16[128,1536]{1,0:T(8,128)(2,1)}, bf16[128,1536]{1,0:T(8,128)(2,1)S(1)}, u32[]{:S(2)}, u32[]{:S(2)}) collective-permute-start(bf16[128,1536]{1,0:T(8,128)(2,1)} %slice.1691), channel_id=1, source_target_pairs={{0,4},{4,0},{8,12},{12,8},{16,20},{20,16},{24,28},{28,24},{1,5},{5... | collective-permute-start | bytes 1179656 | tf_op jit(solution)/shard_map/ppermute | solution.py:52
  662.9 52.4 %collective-permute-start.137 = (bf16[128,1536]{1,0:T(8,128)(2,1)}, bf16[128,1536]{1,0:T(8,128)(2,1)}, u32[]{:S(2)}, u32[]{:S(2)}) collective-permute-start(bf16[128,1536]{1,0:T(8,128)(2,1)} %slice.1695), channel_id=1, source_target_pairs={{0,4},{4,0},{8,12},{12,8},{16,20},{20,16},{24,28},{28,24},{1,5},{5... | collective-permute-start | bytes 1179656 | tf_op jit(solution)/shard_map/ppermute | solution.py:52
  667.0 49.6 %collective-permute-start.157 = (bf16[128,1536]{1,0:T(8,128)(2,1)}, bf16[128,1536]{1,0:T(8,128)(2,1)}, u32[]{:S(2)}, u32[]{:S(2)}) collective-permute-start(bf16[128,1536]{1,0:T(8,128)(2,1)} %slice.1703), channel_id=1, source_target_pairs={{0,4},{4,0},{8,12},{12,8},{16,20},{20,16},{24,28},{28,24},{1,5},{5... | collective-permute-start | bytes 1179656 | tf_op jit(solution)/shard_map/ppermute | solution.py:52
  715.3 28.5 %collective-permute-start.294 = (bf16[2,192,1536]{2,1,0:T(8,128)(2,1)}, bf16[2,192,1536]{2,1,0:T(8,128)(2,1)S(1)}, u32[]{:S(2)}, u32[]{:S(2)}) collective-permute-start(bf16[2,192,1536]{2,1,0:T(8,128)(2,1)} %select_bitcast_fusion.2), channel_id=1, source_target_pairs={{0,1},{1,0},{2,3},{3,2},{4,5},{5,4},{6,7},{7,6},{8,9},{9,8},{10,11... | collective-permute-start | bytes 3538952 | tf_op jit(solution)/shard_map/ppermute | solution.py:46
  734.1 91.3 %collective-permute-start.125 = (bf16[128,1536]{1,0:T(8,128)(2,1)S(1)}, bf16[128,1536]{1,0:T(8,128)(2,1)S(1)}, u32[]{:S(2)}, u32[]{:S(2)}) collective-permute-start(bf16[128,1536]{1,0:T(8,128)(2,1)S(1)} %copy-done.180), channel_id=1, source_target_pairs={{0,4},{4,0},{8,12},{12,8},{16,20},{20,16},{24,28},{28,24},{1,5},{5... | collective-permute-start | bytes 1179656 | tf_op jit(solution)/shard_map/ppermute | solution.py:52
  742.1 75.4 %collective-permute-start.145 = (bf16[128,1536]{1,0:T(8,128)(2,1)S(1)}, bf16[128,1536]{1,0:T(8,128)(2,1)S(1)}, u32[]{:S(2)}, u32[]{:S(2)}) collective-permute-start(bf16[128,1536]{1,0:T(8,128)(2,1)S(1)} %copy-done.181), channel_id=1, source_target_pairs={{0,4},{4,0},{8,12},{12,8},{16,20},{20,16},{24,28},{28,24},{1,5},{5... | collective-permute-start | bytes 1179656 | tf_op jit(solution)/shard_map/ppermute | solution.py:52
  749.0 66.1 %collective-permute-start.290 = (bf16[2,384,1536]{2,1,0:T(8,128)(2,1)S(1)}, bf16[2,384,1536]{2,1,0:T(8,128)(2,1)S(1)}, u32[]{:S(2)}, u32[]{:S(2)}) collective-permute-start(bf16[2,384,1536]{2,1,0:T(8,128)(2,1)S(1)} %copy-done.82), channel_id=1, source_target_pairs={{0,1},{1,0},{2,3},{3,2},{4,5},{5,4},{6,7},{7,6},{8,9},{9,8},{10,11... | collective-permute-start | bytes 7077896 | tf_op jit(solution)/shard_map/ppermute | solution.py:46
  769.0 56.5 %collective-permute-start.140 = (bf16[128,1536]{1,0:T(8,128)(2,1)S(1)}, bf16[128,1536]{1,0:T(8,128)(2,1)S(1)}, u32[]{:S(2)}, u32[]{:S(2)}) collective-permute-start(bf16[128,1536]{1,0:T(8,128)(2,1)S(1)} %get-tuple-element.109), channel_id=1, source_target_pairs={{0,8},{4,12},{8,16},{12,20},{16,24},{20,28},{1,9},{5,13},{9,17},{1... | collective-permute-start | bytes 1179656 | tf_op jit(solution)/shard_map/ppermute | solution.py:55
  776.5 43.7 %collective-permute-start.160 = (bf16[128,1536]{1,0:T(8,128)(2,1)S(1)}, bf16[128,1536]{1,0:T(8,128)(2,1)S(1)}, u32[]{:S(2)}, u32[]{:S(2)}) collective-permute-start(bf16[128,1536]{1,0:T(8,128)(2,1)S(1)} %get-tuple-element.107), channel_id=1, source_target_pairs={{0,8},{4,12},{8,16},{12,20},{16,24},{20,28},{1,9},{5,13},{9,17},{1... | collective-permute-start | bytes 1179656 | tf_op jit(solution)/shard_map/ppermute | solution.py:55
  832.8 205.0 %collective-permute-start.291 = (bf16[384,1536]{1,0:T(8,128)(2,1)}, bf16[384,1536]{1,0:T(8,128)(2,1)}, u32[]{:S(2)}, u32[]{:S(2)}) collective-permute-start(bf16[384,1536]{1,0:T(8,128)(2,1)} %select_bitcast_fusion.4), channel_id=1, source_target_pairs={{0,2},{1,3},{2,0},{3,1},{4,6},{5,7},{6,4},{7,5},{8,10},{9,11},{10,... | collective-permute-start | bytes 3538952 | tf_op jit(solution)/shard_map/ppermute | solution.py:49
  903.7 40.8 %collective-permute-start.169 = (bf16[128,1536]{1,0:T(8,128)(2,1)S(1)}, bf16[128,1536]{1,0:T(8,128)(2,1)S(1)}, u32[]{:S(2)}, u32[]{:S(2)}) collective-permute-start(bf16[128,1536]{1,0:T(8,128)(2,1)S(1)} %slice.2863), channel_id=1, source_target_pairs={{0,1},{1,0},{2,3},{3,2},{4,5},{5,4},{6,7},{7,6},{8,9},{9,8},{10,11... | collective-permute-start | bytes 1179656 | tf_op jit(solution)/shard_map/ppermute | solution.py:46
  937.4 41.7 %collective-permute-start.283 = (bf16[96,768]{1,0:T(8,128)(2,1)}, bf16[96,768]{1,0:T(8,128)(2,1)}, u32[]{:S(2)}, u32[]{:S(2)}) collective-permute-start(bf16[96,768]{1,0:T(8,128)(2,1)} %add_convert_fusion.30), channel_id=1, source_target_pairs={{0,8},{4,12},{8,16},{12,20},{16,24},{20,28},{1,9},{5,13},{9,17},{1... | collective-permute-start | bytes 442376 | tf_op jit(solution)/shard_map/ppermute | solution.py:55
  943.1 38.6 %collective-permute-start.286 = (bf16[96,768]{1,0:T(8,128)(2,1)}, bf16[96,768]{1,0:T(8,128)(2,1)}, u32[]{:S(2)}, u32[]{:S(2)}) collective-permute-start(bf16[96,768]{1,0:T(8,128)(2,1)} %add_convert_fusion.29), channel_id=1, source_target_pairs={{8,0},{12,4},{16,8},{20,12},{24,16},{28,20},{9,1},{13,5},{17,9},{2... | collective-permute-start | bytes 442376 | tf_op jit(solution)/shard_map/ppermute | solution.py:60
  946.4 127.2 %collective-permute-start.175 = (bf16[128,1536]{1,0:T(8,128)(2,1)}, bf16[128,1536]{1,0:T(8,128)(2,1)}, u32[]{:S(2)}, u32[]{:S(2)}) collective-permute-start(bf16[128,1536]{1,0:T(8,128)(2,1)} %get-tuple-element.63), channel_id=1, source_target_pairs={{8,0},{12,4},{16,8},{20,12},{24,16},{28,20},{9,1},{13,5},{17,9},{2... | collective-permute-start | bytes 1179656 | tf_op jit(solution)/shard_map/ppermute | solution.py:60
  947.7 127.2 %collective-permute-start.172 = (bf16[128,1536]{1,0:T(8,128)(2,1)}, bf16[128,1536]{1,0:T(8,128)(2,1)}, u32[]{:S(2)}, u32[]{:S(2)}) collective-permute-start(bf16[128,1536]{1,0:T(8,128)(2,1)} %get-tuple-element.63), channel_id=1, source_target_pairs={{0,8},{4,12},{8,16},{12,20},{16,24},{20,28},{1,9},{5,13},{9,17},{1... | collective-permute-start | bytes 1179656 | tf_op jit(solution)/shard_map/ppermute | solution.py:55
  979.1 86.8 %collective-permute-start.170 = (bf16[128,1536]{1,0:T(8,128)(2,1)}, bf16[128,1536]{1,0:T(8,128)(2,1)S(1)}, u32[]{:S(2)}, u32[]{:S(2)}) collective-permute-start(bf16[128,1536]{1,0:T(8,128)(2,1)} %get-tuple-element.63), channel_id=1, source_target_pairs={{0,4},{4,0},{8,12},{12,8},{16,20},{20,16},{24,28},{28,24},{1,5},{5... | collective-permute-start | bytes 1179656 | tf_op jit(solution)/shard_map/ppermute | solution.py:52
  1073.0 132.8 %collective-permute-start.171 = (bf16[128,1536]{1,0:T(8,128)(2,1)}, bf16[128,1536]{1,0:T(8,128)(2,1)}, u32[]{:S(2)}, u32[]{:S(2)}) collective-permute-start(bf16[128,1536]{1,0:T(8,128)(2,1)} %slice.1719), channel_id=1, source_target_pairs={{0,4},{4,0},{8,12},{12,8},{16,20},{20,16},{24,28},{28,24},{1,5},{5... | collective-permute-start | bytes 1179656 | tf_op jit(solution)/shard_map/ppermute | solution.py:52
  1099.7 39.7 %collective-permute-start.174 = (bf16[128,1536]{1,0:T(8,128)(2,1)}, bf16[128,1536]{1,0:T(8,128)(2,1)}, u32[]{:S(2)}, u32[]{:S(2)}) collective-permute-start(bf16[128,1536]{1,0:T(8,128)(2,1)} %collective-permute-done.173), channel_id=1, source_target_pairs={{16,24},{20,28},{17,25},{21,29},{18,26},{22,30},{19,27},{23,31}} | collective-permute-start | bytes 1179656 | tf_op jit(solution)/shard_map/ppermute | solution.py:55
  1148.1 31.5 %collective-permute-start.180 = (bf16[128,1536]{1,0:T(8,128)(2,1)}, bf16[128,1536]{1,0:T(8,128)(2,1)S(1)}, u32[]{:S(2)}, u32[]{:S(2)}) collective-permute-start(bf16[128,1536]{1,0:T(8,128)(2,1)} %slice.1723), channel_id=1, source_target_pairs={{0,4},{4,0},{8,12},{12,8},{16,20},{20,16},{24,28},{28,24},{1,5},{5... | collective-permute-start | bytes 1179656 | tf_op jit(solution)/shard_map/ppermute | solution.py:52
  1149.1 30.6 %collective-permute-start.184 = (bf16[128,1536]{1,0:T(8,128)(2,1)S(1)}, bf16[128,1536]{1,0:T(8,128)(2,1)S(1)}, u32[]{:S(2)}, u32[]{:S(2)}) collective-permute-start(bf16[128,1536]{1,0:T(8,128)(2,1)S(1)} %add_convert_fusion.3), channel_id=1, source_target_pairs={{0,8},{4,12},{1,9},{5,13},{2,10},{6,14},{3,11},{7,15}} | collective-permute-start | bytes 1179656 | tf_op jit(solution)/shard_map/ppermute | solution.py:55
  1160.5 32.1 %all-to-all-start.1 = ((f32[8,1,128]{2,1,0:T(1,128)}), f32[8,1,128]{2,1,0:T(1,128)S(1)}, u32[]{:S(2)}, u32[]{:S(2)}) async-start(f32[8,1,128]{2,1,0:T(1,128)} %constant_dynamic-update-slice_fusion.42), calls=%async_computation.1 | async-start | bytes 8192 | tf_op jit(solution)/shard_map/all_to_all | solution.py:490
  1192.6 128.9 %collective-permute-start.288 = (bf16[2,384,1536]{2,1,0:T(8,128)(2,1)}, bf16[2,384,1536]{2,1,0:T(8,128)(2,1)}, u32[]{:S(2)}, u32[]{:S(2)}) collective-permute-start(bf16[2,384,1536]{2,1,0:T(8,128)(2,1)} %select_bitcast_fusion.1), channel_id=1, source_target_pairs={{0,1},{1,0},{2,3},{3,2},{4,5},{5,4},{6,7},{7,6},{8,9},{9,8},{10,11... | collective-permute-start | bytes 7077896 | tf_op jit(solution)/shard_map/ppermute | solution.py:46
  1289.9 46.6 %collective-permute-start.195 = (bf16[128,1536]{1,0:T(8,128)(2,1)S(1)}, bf16[128,1536]{1,0:T(8,128)(2,1)S(1)}, u32[]{:S(2)}, u32[]{:S(2)}) collective-permute-start(bf16[128,1536]{1,0:T(8,128)(2,1)S(1)} %slice.2862), channel_id=1, source_target_pairs={{0,1},{1,0},{2,3},{3,2},{4,5},{5,4},{6,7},{7,6},{8,9},{9,8},{10,11... | collective-permute-start | bytes 1179656 | tf_op jit(solution)/shard_map/ppermute | solution.py:46
  1325.3 115.1 %collective-permute-start.289 = (bf16[384,1536]{1,0:T(8,128)(2,1)}, bf16[384,1536]{1,0:T(8,128)(2,1)}, u32[]{:S(2)}, u32[]{:S(2)}) collective-permute-start(bf16[384,1536]{1,0:T(8,128)(2,1)} %select_bitcast_fusion.5), channel_id=1, source_target_pairs={{0,2},{1,3},{2,0},{3,1},{4,6},{5,7},{6,4},{7,5},{8,10},{9,11},{10,... | collective-permute-start | bytes 3538952 | tf_op jit(solution)/shard_map/ppermute | solution.py:49
  1330.7 36.0 %collective-permute-start.260 = (bf16[96,768]{1,0:T(8,128)(2,1)}, bf16[96,768]{1,0:T(8,128)(2,1)}, u32[]{:S(2)}, u32[]{:S(2)}) collective-permute-start(bf16[96,768]{1,0:T(8,128)(2,1)} %add_convert_fusion.32), channel_id=1, source_target_pairs={{0,8},{4,12},{8,16},{12,20},{16,24},{20,28},{1,9},{5,13},{9,17},{1... | collective-permute-start | bytes 442376 | tf_op jit(solution)/shard_map/ppermute | solution.py:55
  1335.2 32.1 %collective-permute-start.263 = (bf16[96,768]{1,0:T(8,128)(2,1)S(1)}, bf16[96,768]{1,0:T(8,128)(2,1)}, u32[]{:S(2)}, u32[]{:S(2)}) collective-permute-start(bf16[96,768]{1,0:T(8,128)(2,1)S(1)} %add_convert_fusion.31), channel_id=1, source_target_pairs={{8,0},{12,4},{16,8},{20,12},{24,16},{28,20},{9,1},{13,5},{17,9},{2... | collective-permute-start | bytes 442376 | tf_op jit(solution)/shard_map/ppermute | solution.py:60
  1384.0 38.8 %collective-permute-start.199 = (bf16[48,1152]{1,0:T(8,128)(2,1)S(1)}, bf16[48,1152]{1,0:T(8,128)(2,1)S(1)}, u32[]{:S(2)}, u32[]{:S(2)}) collective-permute-start(bf16[48,1152]{1,0:T(8,128)(2,1)S(1)} %select_bitcast_fusion.122), channel_id=1, source_target_pairs={{0,2},{1,3},{2,0},{3,1},{4,6},{5,7},{6,4},{7,5},{8,10},{9,11},{10,... | collective-permute-start | bytes 331784 | tf_op jit(solution)/shard_map/ppermute | solution.py:49
  1386.1 47.5 %collective-permute-start.197 = (bf16[48,1152]{1,0:T(8,128)(2,1)S(1)}, bf16[48,1152]{1,0:T(8,128)(2,1)S(1)}, u32[]{:S(2)}, u32[]{:S(2)}) collective-permute-start(bf16[48,1152]{1,0:T(8,128)(2,1)S(1)} %select_bitcast_fusion.123), channel_id=1, source_target_pairs={{0,4},{4,0},{8,12},{12,8},{16,20},{20,16},{24,28},{28,24},{1,5},{5... | collective-permute-start | bytes 331784 | tf_op jit(solution)/shard_map/ppermute | solution.py:52
  (577 other events, 7544.7 us)

commit v2 on v1

--- a/solution.py
+++ b/solution.py
@@ -1,6 +1,8 @@
 import jax
 import jax.numpy as jnp
 from jax import lax
+from jax.experimental import pallas as pl
+from jax.experimental.pallas import tpu as pltpu
 from jax.sharding import PartitionSpec as P
 
 HEADS = 12
@@ -16,7 +18,9 @@
 
 ALL = ("dp", "seq")
 CORES = 2
-LINE_MOST = 4
+LINE = 4
+HIDDEN_SCORE = -1e30
+KERNEL_BYTES = 24 * 2**20
 f32 = jnp.float32
 bf16 = jnp.bfloat16
 
@@ -40,7 +44,7 @@
         self.core = seq_index % CORES
         self.chip = dp_index * self.pairs + self.pair
         self.chips = self.dp_count * self.pairs
-        self.by_line = self.length <= LINE_MOST and self.pairs == 2
+        self.by_line = self.length == LINE and self.pairs == 2
 
     def to_core(self, value):
         return lax.ppermute(value, "seq", [(i, i ^ 1) for i in range(self.seq_count)])
@@ -51,15 +55,9 @@
     def to_side(self, value):
         return lax.ppermute(value, "dp", [(i, i ^ 1) for i in range(self.dp_count)])
 
-    def up(self, value, first, last):
-        return lax.ppermute(
-            value, "dp", [(i, i + 2) for i in range(2 * first, 2 * min(last, self.length - 1))]
-        )
-
-    def down(self, value, first, last):
-        return lax.ppermute(
-            value, "dp", [(i, i - 2) for i in range(2 * max(first, 1), 2 * last)]
-        )
+    def along(self, value, steps):
+        count = self.dp_count
+        return lax.ppermute(value, "dp", [(i, (i + 2 * steps) % count) for i in range(count)])
 
     def chips_on(self, value, steps):
         count = self.dp_count * self.seq_count
@@ -72,82 +70,72 @@
             [jnp.where(flag == 0, own, other), jnp.where(flag == 0, other, own)], axis=axis
         )
 
-    def line_gather(self, value):
-        count = self.length
-        ups, downs = [value], [value]
-        for step in range(1, count):
-            ups.append(self.up(ups[-1], step - 1, count))
-            downs.append(self.down(downs[-1], 0, count - step + 1))
-        return [value] + [
-            jnp.where(self.line >= k, ups[k], downs[count - k]) for k in range(1, count)
-        ]
-
-    def line_scatter(self, blocks):
-        count = self.length
-        total = blocks[0].astype(f32)
-        for rising in (True, False):
-            carried = None
-            for step in range(1, count):
-                piece = blocks[step] if rising else blocks[count - step]
-                if carried is not None:
-                    piece = (piece.astype(f32) + carried.astype(f32)).astype(bf16)
-                if rising:
-                    carried = self.up(piece, 0, step)
-                else:
-                    carried = self.down(piece, count - step, count)
-            if carried is not None:
-                total = total + carried.astype(f32)
-        return total
-
     def token_gather(self, value):
         if not self.by_line:
             return [lax.all_gather(value, "dp", axis=0, tiled=True)]
+        side = self.to_side(value)
+        one, three = self.along(value, 1), self.along(value, 3)
+        held, one, three = lax.optimization_barrier((value, one, three))
+        two = self.along(held, 2)
+        odd = jnp.concatenate([one, three], axis=0)
         return [
-            jnp.concatenate([block, self.to_side(block)], axis=0)
-            for block in self.line_gather(value)
+            jnp.concatenate([value, side], axis=0),
+            jnp.concatenate([odd, self.to_side(odd)], axis=0),
+            jnp.concatenate([two, self.to_side(two)], axis=0),
         ]
 
     def token_scatter(self, blocks):
         if not self.by_line:
             return lax.psum_scatter(blocks[0], "dp", scatter_dimension=0, tiled=True).astype(f32)
         rows = blocks[0].shape[0] // 2
-        summed = []
-        for k, block in enumerate(blocks):
-            total = block[:rows].astype(f32) + self.to_side(block[rows:]).astype(f32)
-            summed.append(total if k == 0 else total.astype(bf16))
-        return self.line_scatter(summed)
+
+        def folded(block):
+            half = block.shape[0] // 2
+            return block[:half].astype(f32) + self.to_side(block[half:]).astype(f32)
+
+        odd = folded(blocks[1]).astype(bf16)
+        one, three = self.along(odd[:rows], -1), self.along(odd[rows:], -3)
+        two = folded(blocks[2]).astype(bf16)
+        held, one, three = lax.optimization_barrier((two, one, three))
+        two = self.along(held, -2)
+        return folded(blocks[0]) + one.astype(f32) + three.astype(f32) + two.astype(f32)
 
     def token_owner(self):
         if not self.by_line:
             return [list(range(self.dp_count))]
-        owners = []
-        for k in range(self.length):
-            place = lax.rem(self.line - k + self.length, self.length)
-            owners.append([place * 2 + self.side, place * 2 + 1 - self.side])
-        return owners
+        place = [lax.rem(self.line - k + self.length, self.length) * 2 for k in range(LINE)]
+        return [
+            [place[k] + side for side in (self.side, 1 - self.side) for k in members]
+            for members in ((0,), (1, 3), (2,))
+        ]
 
     def core_groups(self):
         count = self.dp_count * self.seq_count
         return [list(range(core, count, CORES)) for core in range(CORES)]
 
-    def chip_gather(self, block):
-        rows, columns = block.shape
+    def chip_gather(self, one, two):
+        rows, width = one.shape
         if not self.by_line:
-            return lax.all_gather(
-                block, ALL, axis=0, tiled=True, axis_index_groups=self.core_groups()
+            whole = lax.all_gather(
+                jnp.concatenate([one, two], axis=1),
+                ALL,
+                axis=0,
+                tiled=True,
+                axis_index_groups=self.core_groups(),
             )
-        half = rows // 2
-        whole = jnp.zeros((self.chips * rows, columns), block.dtype)
-        for k, piece in enumerate(self.line_gather(block)):
-            one, two = piece[:half], piece[half:]
-            one = self.ordered(self.side, one, self.to_side(one), 0)
-            two = self.ordered(self.pair, two, self.to_pair(two), 0)
-            one = self.ordered(self.pair, one, self.to_pair(one), 1)
-            two = self.ordered(self.side, two, self.to_side(two), 0)
-            piece = jnp.stack([one, two], axis=2).reshape(4 * rows, columns)
+            return whole[:, :width], whole[:, width:]
+        block = jnp.concatenate([one, two], axis=1)
+        lines = jnp.zeros((LINE,) + block.shape, block.dtype)
+        for k in range(LINE):
+            piece = block if k == 0 else self.along(block, k)
             place = lax.rem(self.line - k + self.length, self.length)
-            whole = lax.dynamic_update_slice(whole, piece, (place * 4 * rows, 0))
-        return whole
+            lines = lax.dynamic_update_slice(lines, piece[None], (place, 0, 0))
+        one, two = lines[:, :, :width], lines[:, :, width:]
+        one = self.ordered(self.side, one, self.to_side(one), 1)
+        two = self.ordered(self.pair, two, self.to_pair(two), 1)
+        one = self.ordered(self.pair, one, self.to_pair(one), 2)
+        two = self.ordered(self.side, two, self.to_side(two), 1)
+        return one.reshape(self.chips * rows, -1), two.reshape(self.chips * rows, -1)
 
     def picked(self, flag, stacked, axis):
         first, second = (
@@ -156,35 +144,37 @@
         )
         return jnp.where(flag == 0, first, second), jnp.where(flag == 0, second, first)
 
-    def chip_scatter(self, whole):
-        columns = whole.shape[1]
-        rows = whole.shape[0] // self.chips
+    def chip_scatter(self, one, two):
+        width = one.shape[1]
+        rows = one.shape[0] // self.chips
         if not self.by_line:
-            return lax.psum_scatter(
-                whole,
+            total = lax.psum_scatter(
+                jnp.concatenate([one, two], axis=1),
                 ALL,
                 scatter_dimension=0,
                 tiled=True,
                 axis_index_groups=self.core_groups(),
             ).astype(f32)
-        half = rows // 2
-        summed = []
+            return total[:, :width], total[:, width:]
 
         def step(flag, stacked, axis, move):
             kept, sent = self.picked(flag, stacked, axis)
             return (kept.astype(f32) + move(sent).astype(f32)).astype(bf16)
 
-        for k in range(self.length):
+        one = one.reshape(LINE, 2, 2, rows, -1)
+        two = two.reshape(LINE, 2, 2, rows, -1)
+        one = step(self.pair, one, 2, self.to_pair)
+        two = step(self.side, two, 1, self.to_side)
+        one = step(self.side, one, 1, self.to_side)
+        two = step(self.pair, two, 1, self.to_pair)
+        both = jnp.concatenate([one, two], axis=2)
+        total = None
+        for k in range(LINE):
             place = lax.rem(self.line - k + self.length, self.length)
-            piece = lax.dynamic_slice(whole, (place * 4 * rows, 0), (4 * rows, columns))
-            piece = piece.reshape(2, 2, 2, half, columns)
-            one, two = piece[:, :, 0], piece[:, :, 1]
-            one = step(self.pair, one, 1, self.to_pair)
-            two = step(self.side, two, 0, self.to_side)
-            one = step(self.side, one, 0, self.to_side)
-            two = step(self.pair, two, 0, self.to_pair)
-            summed.append(jnp.concatenate([one, two], axis=0))
-        return self.line_scatter(summed)
+            piece = lax.dynamic_index_in_dim(both, place, 0, keepdims=False)
+            piece = (piece if k == 0 else self.along(piece, -k)).astype(f32)
+            total = piece if k == 0 else total + piece
+        return total[:, :width], total[:, width:]
 
     def chip_rows(self, value):
         return jnp.concatenate([value, self.to_core(value)], axis=0)
@@ -218,21 +208,21 @@
     return (doc_label, is_valid, position)
 
 
-def rope_turn(vectors, position, direction):
-    half_width = vectors.shape[-1] // 2
-    frequency = rope_base ** (-jnp.arange(half_width, dtype=jnp.float32) * 2.0 / vectors.shape[-1])
+def turn_tables(position):
+    half_width = HEAD // 2
+    frequency = rope_base ** (-jnp.arange(half_width, dtype=jnp.float32) * 2.0 / HEAD)
     angles = position.astype(jnp.float32)[:, None] * frequency[None, :]
-    cosine = jnp.cos(angles)[:, None, :]
-    sine_part = direction * jnp.sin(angles)[:, None, :]
-    first_half = vectors[..., :half_width]
-    second_half = vectors[..., half_width:]
-    return jnp.concatenate(
-        [
-            first_half * cosine - second_half * sine_part,
-            second_half * cosine + first_half * sine_part,
-        ],
-        axis=-1,
+    cosine, sine = jnp.cos(angles), jnp.sin(angles)
+    return (
+        jnp.concatenate([cosine, cosine], axis=1),
+        jnp.concatenate([-sine, sine], axis=1),
     )
+
+
+def rope_turn(vectors, turn, direction):
+    half_width = HEAD // 2
+    swapped = jnp.concatenate([vectors[:, half_width:], vectors[:, :half_width]], axis=1)
+    return vectors * turn[0] + swapped * (direction * turn[1])
 
 
 def norm_scale(stream):
@@ -254,34 +244,107 @@
     return same_doc & (distance >= 0) & (distance < WINDOW)
 
 
-def attend_forward(queries, keys, values, keep_mask):
-    scores = jnp.einsum("qhd,kd->hqk", queries, keys, preferred_element_type=f32) * HEAD ** (-0.5)
-    scores = jnp.where(keep_mask[None], scores, -jnp.inf)
-    row_top = jnp.max(scores, axis=-1, keepdims=True)
-    weights = jnp.exp(scores - row_top)
-    row_total = jnp.sum(weights, axis=-1, keepdims=True)
-    prob_rows = (weights / row_total).astype(bf16)
-    out = jnp.einsum("hqk,kd->qhd", prob_rows, values, preferred_element_type=f32)
-    return (out, row_top + jnp.log(row_total))
-
-
-def attend_backward(queries, keys, values, head_grad, log_total, keep_mask):
-    score_scale = HEAD ** (-0.5)
-    scores = jnp.einsum("qhd,kd->hqk", queries, keys, preferred_element_type=f32) * score_scale
-    prob_rows = jnp.where(keep_mask[None], jnp.exp(scores - log_total), 0.0)
-    prob_grad = jnp.einsum("qhd,kd->hqk", head_grad, values, preferred_element_type=f32)
-    row_dot = jnp.sum(prob_rows * prob_grad, axis=-1, keepdims=True)
+def turned(vectors, cosine, sine):
+    return vectors * cosine + pltpu.roll(vectors, HEAD // 2, 1) * sine
+
+
+def score_probs(queries, keys, bias):
+    scores = dot(queries, keys, ((1,), (1,))) * HEAD ** (-0.5) + bias
+    weights = jnp.exp(scores - jnp.max(scores, axis=1, keepdims=True))
+    return weights * (1.0 / jnp.sum(weights, axis=1, keepdims=True))
+
+
+def forward_kernel(mixed, keys, values, bias, cosine, sine, valid, attended, queries):
+    turned_queries = turned(mixed[...], cosine[...], sine[...]).astype(bf16)
+    queries[...] = turned_queries
+    prob_rows = score_probs(turned_queries, keys[...], bias[...]).astype(bf16)
+    out = dot(prob_rows, values[...], ((1,), (0,)))
+    attended[...] = (out * valid[...]).astype(bf16)
+
+
+def attend_forward(mixed, table, bias, turn, valid):
+    rows = mixed.shape[0]
+    key_rows = table.shape[0]
+    heads = HEADS // CORES
+    per_head = pl.BlockSpec((rows, HEAD), lambda h: (0, h))
+    fixed = pl.BlockSpec((rows, HEAD), lambda h: (0, 0))
+    return pl.pallas_call(
+        forward_kernel,
+        grid=(heads,),
+        in_specs=[
+            per_head,
+            pl.BlockSpec((key_rows, HEAD), lambda h: (0, 0)),
+            pl.BlockSpec((key_rows, HEAD), lambda h: (0, 1)),
+            pl.BlockSpec((rows, key_rows), lambda h: (0, 0)),
+            fixed,
+            fixed,
+            fixed,
+        ],
+        out_specs=[per_head, per_head],
+        out_shape=[jax.ShapeDtypeStruct((rows, heads * HEAD), bf16)] * 2,
+        compiler_params=pltpu.CompilerParams(vmem_limit_bytes=KERNEL_BYTES),
+        cost_estimate=pl.CostEstimate(
+            flops=4 * heads * rows * key_rows * HEAD,
+            bytes_accessed=4 * rows * key_rows + 8 * rows * heads * HEAD,
+            transcendentals=heads * rows * key_rows,
+        ),
+        name="attend_forward",
+    )(mixed, table, table, bias, turn[0], turn[1], valid)
+
+
+def backward_kernel(
+    queries, head_grad, keys, values, bias, cosine, sine, query_grad, key_grad, value_grad
+):
+    scale = HEAD ** (-0.5)
+
+    @pl.when(pl.program_id(0) == 0)
+    def _():
+        key_grad[...] = jnp.zeros_like(key_grad)
+        value_grad[...] = jnp.zeros_like(value_grad)
+
+    prob_rows = score_probs(queries[...], keys[...], bias[...])
+    prob_grad = dot(head_grad[...], values[...], ((1,), (1,)))
+    row_dot = jnp.sum(prob_rows * prob_grad, axis=1, keepdims=True)
     score_grad = (prob_rows * (prob_grad - row_dot)).astype(bf16)
-    query_grad = (
-        jnp.einsum("hqk,kd->qhd", score_grad, keys, preferred_element_type=f32) * score_scale
-    )
-    key_grad = (
-        jnp.einsum("hqk,qhd->kd", score_grad, queries, preferred_element_type=f32) * score_scale
-    )
-    value_grad = jnp.einsum(
-        "hqk,qhd->kd", prob_rows.astype(bf16), head_grad, preferred_element_type=f32
-    )
-    return (query_grad, key_grad, value_grad)
+    grad = dot(score_grad, keys[...], ((1,), (0,))) * scale
+    query_grad[...] = turned(grad, cosine[...], -sine[...]).astype(bf16)
+    key_grad[...] += dot(score_grad, queries[...], ((0,), (0,))) * scale
+    value_grad[...] += dot(prob_rows.astype(bf16), head_grad[...], ((0,), (0,)))
+
+
+def attend_backward(queries, head_grad, table, bias, turn):
+    rows = queries.shape[0]
+    key_rows = table.shape[0]
+    heads = HEADS // CORES
+    per_head = pl.BlockSpec((rows, HEAD), lambda h: (0, h))
+    fixed = pl.BlockSpec((rows, HEAD), lambda h: (0, 0))
+    table_grad = pl.BlockSpec((key_rows, HEAD), lambda h: (0, 0))
+    return pl.pallas_call(
+        backward_kernel,
+        grid=(heads,),
+        in_specs=[
+            per_head,
+            per_head,
+            pl.BlockSpec((key_rows, HEAD), lambda h: (0, 0)),
+            pl.BlockSpec((key_rows, HEAD), lambda h: (0, 1)),
+            pl.BlockSpec((rows, key_rows), lambda h: (0, 0)),
+            fixed,
+            fixed,
+        ],
+        out_specs=[per_head, table_grad, table_grad],
+        out_shape=[
+            jax.ShapeDtypeStruct((rows, heads * HEAD), bf16),
+            jax.ShapeDtypeStruct((key_rows, HEAD), f32),
+            jax.ShapeDtypeStruct((key_rows, HEAD), f32),
+        ],
+        compiler_params=pltpu.CompilerParams(vmem_limit_bytes=KERNEL_BYTES),
+        cost_estimate=pl.CostEstimate(
+            flops=10 * heads * rows * key_rows * HEAD,
+            bytes_accessed=4 * rows * key_rows + 8 * rows * heads * HEAD,
+            transcendentals=heads * rows * key_rows,
+        ),
+        name="attend_backward",
+    )(queries, head_grad, table, table, bias, turn[0], turn[1])
 
 
 def expert_gates(normed, router, routes, expert_ids):
@@ -328,17 +391,14 @@
     key_index = chip_index_of(wires.chip - depth, depth + 1)
     query_label, query_valid, position = doc_labels(query_index, doc_lengths, seq_length)
     key_label = doc_labels(key_index, doc_lengths, seq_length)[0]
-    keep_mask = keep_rule(query_index, key_index, query_label, key_label)
+    bias = jnp.where(
+        keep_rule(query_index, key_index, query_label, key_label), 0.0, HIDDEN_SCORE
+    ).astype(f32)
+    turn = turn_tables(position)
+    valid = jnp.broadcast_to(query_valid[:, None], (chip_tokens, HEAD))
     expert_ids = jnp.arange(expert_count, dtype=jnp.int32)
     my_expert = (expert_ids == wires.dp_index)[None, :]
-    all_routes = lax.all_gather(routes, "dp", axis=0)
-    block_routes = [
-        jnp.concatenate(
-            [lax.dynamic_index_in_dim(all_routes, owner, 0, keepdims=False) for owner in owners]
-        )
-        for owners in wires.token_owner()
-    ]
-
+    route_names = jnp.pad(routes.astype(bf16), ((0, 0), (0, 128 - routes.shape[1])))
     small_width = -(-(expert_count + 2) // 128) * 128
 
     def packed_weights(layer_index):
@@ -360,19 +420,30 @@
                 )
             )
             backs.append(out_rows[:, c * q_width : (c + 1) * q_width])
-        result = []
-        for first, second in (fronts, backs):
+        def per_chip(first, second):
             kept = jnp.where(core == 0, first, second)
             sent = jnp.where(core == 0, second, first)
             block = wires.ordered(core, kept, wires.to_core(sent), 0)
-            result.append(block.reshape(2 * kept.shape[0], kept.shape[1]))
-        return result
-
+            return block.reshape(2 * kept.shape[0], kept.shape[1])
+
+        return per_chip(*fronts), per_chip(*backs)
+
+    packed = [packed_weights(layer_index) for layer_index in range(layer_count)]
+    cut = (q_width // 2) // 128 * 128 + 256
+    fronts = [
+        jnp.concatenate(wires.chip_gather(packed[0][0][:, :cut], packed[0][0][:, cut:]), axis=1)
+    ]
+    rest_front = jnp.concatenate([front for front, _ in packed[1:]], axis=1)
+    rest_back = jnp.concatenate([back for _, back in packed], axis=1)
+    rest_front, rest_back, fronts[0] = lax.optimization_barrier((rest_front, rest_back, fronts[0]))
+    rest_front, rest_back = wires.chip_gather(rest_front, rest_back)
+    front_width = qkv_width + small_width
     held_weights = []
     for layer_index in range(layer_count):
-        front, back = packed_weights(layer_index)
-        front = wires.chip_gather(front)
-        back = wires.chip_gather(back)
+        if layer_index > 0:
+            fronts.append(rest_front[:, (layer_index - 1) * front_width :][:, :front_width])
+        front = fronts[layer_index]
+        back = rest_back[:, layer_index * q_width : (layer_index + 1) * q_width]
         small = front[:, qkv_width:]
         held_weights.append(
             (
@@ -391,23 +462,24 @@
         scale_one = norm_scale(stream)
         normed_one = wires.chip_rows((stream * scale_one * gain_rows[0]).astype(bf16))
         mixed = dot(normed_one, qkv_here, ((1,), (0,)))
-        queries = rope_turn(
-            mixed[:, :q_width].reshape(chip_tokens, heads_here, HEAD), position, 1.0
-        ).astype(bf16)
-        own_keys = rope_turn(mixed[:, None, q_width : q_width + HEAD], position, 1.0)[:, 0]
+        own_keys = rope_turn(mixed[:, q_width : q_width + HEAD], turn, 1.0)
         own_pair = jnp.concatenate([own_keys, mixed[:, q_width + HEAD :]], axis=1).astype(bf16)
         table = jnp.concatenate(
             [wires.chips_on(own_pair, step) for step in range(depth, 0, -1)] + [own_pair], axis=0
         )
-        keys, values = table[:, :HEAD], table[:, HEAD:]
-        attended, log_total = attend_forward(queries, keys, values, keep_mask)
-        attended = (
-            (attended * query_valid[:, None, None]).astype(bf16).reshape(chip_tokens, q_width)
-        )
+        attended, queries = attend_forward(mixed, table, bias, turn, valid)
         stream_mid = stream + wires.chip_sum(dot(attended, out_here, ((1,), (1,))))
         scale_two = norm_scale(stream_mid)
         normed_two = (stream_mid * scale_two * gain_rows[1]).astype(bf16)
-        blocks = wires.token_gather(normed_two)
+        if layer_index == 0:
+            blocks = wires.token_gather(jnp.concatenate([normed_two, route_names], axis=1))
+            block_routes = [
+                block[:, model_width : model_width + routes.shape[1]].astype(jnp.int32)
+                for block in blocks
+            ]
+            blocks = [block[:, :model_width] for block in blocks]
+        else:
+            blocks = wires.token_gather(normed_two)
         block_gates, up_gates, block_outs = [], [], []
         for block, route_rows in zip(blocks, block_routes):
             gates = expert_gates(block, router, route_rows, expert_ids)[0]
@@ -427,9 +499,7 @@
                 normed_one,
                 normed_two,
                 queries,
-                keys,
-                values,
-                log_total,
+                table,
                 attended,
                 blocks,
                 block_gates,
@@ -449,9 +519,7 @@
             normed_one,
             normed_two,
             queries,
-            keys,
-            values,
-            log_total,
+            table,
             attended,
             blocks,
             block_gates,
@@ -506,20 +574,19 @@
         mid_grad = stream_grad + mid_grad
         attn_grad = wires.chip_rows(mid_grad.astype(bf16))
         head_grad = dot(attn_grad, out_here, ((1,), (0,))) * query_valid[:, None]
-        head_grad = head_grad.astype(bf16).reshape(chip_tokens, heads_here, HEAD)
+        head_grad = head_grad.astype(bf16)
         out_grad = dot(attn_grad, attended, ((0,), (0,))).astype(bf16)
-        query_grad, key_grad, value_grad = attend_backward(
-            queries, keys, values, head_grad, log_total, keep_mask
-        )
+        query_lin, key_grad, value_grad = attend_backward(queries, head_grad, table, bias, turn)
         pair_sums = jnp.concatenate([key_grad, value_grad], axis=1)
         own_grad = pair_sums[depth * chip_tokens :]
         for step in range(depth, 0, -1):
             first = (depth - step) * chip_tokens
             part = pair_sums[first : first + chip_tokens].astype(bf16)
             own_grad = own_grad + wires.chips_on(part, -step).astype(f32)
-        query_lin = rope_turn(query_grad, position, -1.0).reshape(chip_tokens, q_width)
-        key_lin = rope_turn(own_grad[:, None, :HEAD], position, -1.0)[:, 0]
-        mixed_grad = jnp.concatenate([query_lin, key_lin, own_grad[:, HEAD:]], axis=1).astype(bf16)
+        key_lin = rope_turn(own_grad[:, :HEAD], turn, -1.0)
+        mixed_grad = jnp.concatenate(
+            [query_lin, key_lin.astype(bf16), own_grad[:, HEAD:].astype(bf16)], axis=1
+        )
         normed_one_grad = wires.chip_sum(dot(mixed_grad, qkv_here, ((1,), (1,))))
         gain_one_grad, front_grad = norm_back(stream, scale_one, gain_rows[0], normed_one_grad)
         stream_grad = mid_grad + front_grad
@@ -532,10 +599,20 @@
             kept, sent = wires.picked(core, value.reshape(2, rows, value.shape[1]), 0)
             return kept, wires.to_core(sent.astype(bf16)).astype(f32)
 
-        back_own, back_other = shared(wires.chip_scatter(out_grad))
-        front_own, front_other = shared(
-            wires.chip_scatter(jnp.concatenate([qkv_grad, small], axis=1))
-        )
+        half = q_width // 2
+        if layer_index > 0:
+            front, back = wires.chip_scatter(jnp.concatenate([qkv_grad, small], axis=1), out_grad)
+        else:
+            back = jnp.concatenate(wires.chip_scatter(out_grad[:, :half], out_grad[:, half:]), axis=1)
+            cut = qkv_width // 2
+            front = jnp.concatenate(
+                wires.chip_scatter(
+                    qkv_grad[:, :cut], jnp.concatenate([qkv_grad[:, cut:], small], axis=1)
+                ),
+                axis=1,
+            )
+        back_own, back_other = shared(back)
+        front_own, front_other = shared(front)
         out_sum = wires.ordered(core, back_own, back_other, 1)
         out_sum = out_sum.reshape(out_sum.shape[0], HEADS * HEAD).T
         small_sum = (front_own + front_other)[:, qkv_width:]

time: 1460 us -> 1040 us (0.71)
  starting transfers between devices: 494 us -> 228 us
  other arithmetic: 177 us -> 104 us
  local copies, waits for them, and re-layouts: 132 us -> 77.9 us
  matrix products: 164 us -> 125 us
  Pallas kernels: 0 us -> 32.2 us
  blocking collectives: 28.4 us -> 0 us
    ppermute x96 -> x39, starting transfers between devices: 242 us -> 112 us  [along(): lax.ppermute(value, 'dp', [(i, (i + 2 * steps) % count) for i in range(co...]
    ppermute x96 -> x34, waiting for transfers between devices: 153 us -> 83.9 us  [to_side(): return lax.ppermute(value, 'dp', [(i, i ^ 1) for i in range(self.dp_count)])]
    ppermute x68 -> x14, starting transfers between devices: 82.8 us -> 16.4 us  [to_pair(): lax.ppermute(value, 'seq', [(i, i ^ 2) for i in range(self.seq_count)])]
    ppermute x96 -> x34, starting transfers between devices: 99.4 us -> 44 us  [to_side(): return lax.ppermute(value, 'dp', [(i, i ^ 1) for i in range(self.dp_count)])]
    ppermute x16, waiting for transfers between devices: 5.9 us -> 60.3 us  [chips_on(): lax.ppermute(value, ALL, [(i, i + offset) for i in range(first, last)])]
    ppermute x96 -> x39, waiting for transfers between devices: 174 us -> 227 us  [along(): lax.ppermute(value, 'dp', [(i, (i + 2 * steps) % count) for i in range(co...]
    dot_general x12 -> x0, matrix products: 37.7 us -> none  [the longest x2 11.4 us: attend_backward(): jnp.einsum('hqk,qhd->kd', prob_rows.astype(bf16), head_grad, preferred_el...]
    pallas_call x0 -> x4, Pallas kernels: none -> 32.2 us  [the longest x2 18.9 us: attend_backward(): pl.pallas_call(backward_kernel, grid=(heads,), in_specs=[per_head, per_he...]
  transfers between devices with their start and end apart: 298 -> 125, of which waited for: 129 -> 57; matrix products, arithmetic and copies ran while one was open for 31% -> 25% of each run, Pallas kernels for 0% -> 3%
where the time goes in v2:
time: 1040 us; the launch traced here: 1030 us
  waiting for transfers between devices  455 us (44%)
  starting transfers between devices  228 us (22%)
  matrix products  125 us (12%)
  other arithmetic  104 us (10%)
  local copies, waits for them, and re-layouts  77.9 us (7%)
  Pallas kernels  32.2 us (3%)
    ppermute x39, waiting for transfers between devices, along(): lax.ppermute(value, 'dp', [(i, (i + 2 * steps) % count) for i in range(co...  227 us
    dot_general x52, matrix products, dot(): lax.dot_general(left, right, (dims, ((), ())), preferred_element_type=f32)  125 us
    ppermute x39, starting transfers between devices, along(): lax.ppermute(value, 'dp', [(i, (i + 2 * steps) % count) for i in range(co...  112 us
    ppermute x34, waiting for transfers between devices, to_side(): return lax.ppermute(value, 'dp', [(i, i ^ 1) for i in range(self.dp_count)])  83.9 us
    ppermute x14, waiting for transfers between devices, to_pair(): lax.ppermute(value, 'seq', [(i, i ^ 2) for i in range(self.seq_count)])  79.6 us
    ppermute x16, waiting for transfers between devices, chips_on(): lax.ppermute(value, ALL, [(i, i + offset) for i in range(first, last)])  60.3 us
    ppermute x16, starting transfers between devices, chips_on(): lax.ppermute(value, ALL, [(i, i + offset) for i in range(first, last)])  44.2 us
    ppermute x34, starting transfers between devices, to_side(): return lax.ppermute(value, 'dp', [(i, i ^ 1) for i in range(self.dp_count)])  44 us
  transfers between devices with their start and end apart: 125, of which 57 were waited for; matrix products, arithmetic and copies ran while one was open for 25% of the time, Pallas kernels for 3%

profile of v2, /device:TPU:0, one launch (start us, length us, event | category | flops | bytes accessed | tf_op | source)
XLA Modules:
  0.0 1027.6 jit_solution(6995119336482169201)
XLA Ops:
  18.6 10.6 %collective-permute-done.4 = bf16[96,1152]{1,0:T(8,128)(2,1)S(1)} collective-permute-done((bf16[96,1152]{1,0:T(8,128)(2,1)S(1)}, bf16[96,1152]{1,0:T(8,128)(2,1)S(1)}, u32[]{:S(2)}, u32[]{:S(2)}) %collective-permute-start.4) | collective-permute-done | bytes 221216 | tf_op jit(solution)/shard_map/ppermute | solution.py:60
  30.0 7.8 collective-permute-done.5
  43.3 5.7 collective-permute-done.9
  50.7 5.2 collective-permute-done.7
  56.3 13.0 %collective-permute-done.10 = bf16[4,2,96,512]{3,2,0,1:T(8,128)(2,1)S(1)} collective-permute-done((bf16[4,2,96,512]{3,2,0,1:T(8,128)(2,1)S(1)}, bf16[4,2,96,512]{3,2,0,1:T(8,128)(2,1)S(1)}, u32[]{:S(2)}, u32[]{:S(2)}) %collective-permute-start.10) | collective-permute-done | bytes 786464 | tf_op jit(solution)/shard_map/ppermute | solution.py:56
  73.9 8.6 collective-permute-start.16
  86.0 9.4 collective-permute-done.16
  95.4 18.2 %collective-permute-done.17 = bf16[96,2688]{1,0:T(8,128)(2,1)S(1)} collective-permute-done((bf16[96,2688]{1,0:T(8,128)(2,1)S(1)}, bf16[96,2688]{1,0:T(8,128)(2,1)S(1)}, u32[]{:S(2)}, u32[]{:S(2)}) %collective-permute-start.17) | collective-permute-done | bytes 516128 | tf_op jit(solution)/shard_map/ppermute | solution.py:60
  118.8 22.9 %collective-permute-done.19 = bf16[4,96,1536]{2,1,0:T(8,128)(2,1)S(1)} collective-permute-done((bf16[4,96,1536]{2,1,0:T(8,128)(2,1)S(1)}, bf16[4,96,1536]{2,1,0:T(8,128)(2,1)S(1)}, u32[]{:S(2)}, u32[]{:S(2)}) %collective-permute-start.19) | collective-permute-done | bytes 1179680 | tf_op jit(solution)/shard_map/ppermute | solution.py:53
  147.3 14.2 %collective-permute-start.12 = (bf16[256,256]{1,0:T(8,128)(2,1)}, bf16[256,256]{1,0:T(8,128)(2,1)}, u32[]{:S(2)}, u32[]{:S(2)}) collective-permute-start(bf16[256,256]{1,0:T(8,128)(2,1)} %pad_maximum_fusion.46), channel_id=1, source_target_pairs={{0,8},{1,9},{2,10},{3,11},{4,12},{5,13},{6,14},{7,15},{8,16},{9,17... | collective-permute-start | bytes 393224 | tf_op jit(solution)/shard_map/ppermute | solution.py:66
  179.2 48.1 %collective-permute-done.14 = bf16[256,256]{1,0:T(8,128)(2,1)S(1)} collective-permute-done((bf16[256,256]{1,0:T(8,128)(2,1)}, bf16[256,256]{1,0:T(8,128)(2,1)S(1)}, u32[]{:S(2)}, u32[]{:S(2)}) %collective-permute-start.14) | collective-permute-done | bytes 131104 | tf_op jit(solution)/shard_map/ppermute | solution.py:66
  228.4 6.7 attend_forward.2
  247.6 11.7 %collective-permute-start.58 = (bf16[128,1536]{1,0:T(8,128)(2,1)}, bf16[128,1536]{1,0:T(8,128)(2,1)S(1)}, u32[]{:S(2)}, u32[]{:S(2)}) collective-permute-start(bf16[128,1536]{1,0:T(8,128)(2,1)} %param.11), channel_id=1, source_target_pairs={{0,16},{4,20},{8,24},{12,28},{16,0},{20,4},{24,8},{28,12},{1,17},{... | collective-permute-start | bytes 1179656 | tf_op jit(solution)/shard_map/ppermute | solution.py:60
  260.6 14.3 %collective-permute-done.35 = bf16[4,2,96,1152]{3,2,0,1:T(8,128)(2,1)S(1)} collective-permute-done((bf16[4,2,96,1152]{3,2,0,1:T(8,128)(2,1)S(1)}, bf16[4,2,96,1152]{3,2,0,1:T(8,128)(2,1)S(1)}, u32[]{:S(2)}, u32[]{:S(2)}) %collective-permute-start.35) | collective-permute-done | bytes 1769504 | tf_op jit(solution)/shard_map/ppermute | solution.py:53
  275.4 12.0 %collective-permute-start.24 = (bf16[128,1664]{0,1:T(8,128)(2,1)S(1)}, bf16[128,1664]{0,1:T(8,128)(2,1)S(1)}, u32[]{:S(2)}, u32[]{:S(2)}) collective-permute-start(bf16[128,1664]{0,1:T(8,128)(2,1)S(1)} %pad_maximum_fusion.34), channel_id=1, source_target_pairs={{0,8},{4,12},{8,16},{12,20},{16,24},{20,28},{24,0},{28,4},{1,9},{5... | collective-permute-start | bytes 1277960 | tf_op jit(solution)/shard_map/ppermute | solution.py:60
  290.5 9.7 collective-permute-done.24
  314.7 11.3 %collective-permute-done.26 = bf16[128,1664]{0,1:T(8,128)(2,1)S(1)} collective-permute-done((bf16[128,1664]{0,1:T(8,128)(2,1)S(1)}, bf16[128,1664]{0,1:T(8,128)(2,1)S(1)}, u32[]{:S(2)}, u32[]{:S(2)}) %collective-permute-start.26) | collective-permute-done | bytes 426016 | tf_op jit(solution)/shard_map/ppermute | solution.py:60
  328.5 9.8 collective-permute-done.27
  344.9 5.5 fusion.20
  362.3 13.3 %collective-permute-done.30 = bf16[256,1536]{0,1:T(8,128)(2,1)S(1)} collective-permute-done((bf16[256,1536]{0,1:T(8,128)(2,1)S(1)}, bf16[256,1536]{0,1:T(8,128)(2,1)S(1)}, u32[]{:S(2)}, u32[]{:S(2)}) %collective-permute-start.30) | collective-permute-done | bytes 786464 | tf_op jit(solution)/shard_map/ppermute | solution.py:56
  376.0 8.1 collective-permute-done.28
  384.6 9.8 collective-permute-done.32
  395.3 15.9 %collective-permute-done.33 = bf16[128,1536]{0,1:T(8,128)(2,1)S(1)} collective-permute-done((bf16[128,1536]{0,1:T(8,128)(2,1)S(1)}, bf16[128,1536]{0,1:T(8,128)(2,1)S(1)}, u32[]{:S(2)}, u32[]{:S(2)}) %collective-permute-start.33) | collective-permute-done | bytes 393248 | tf_op jit(solution)/shard_map/ppermute | solution.py:60
  429.9 6.7 attend_forward.3
  450.5 7.3 collective-permute-done.44
  457.8 7.5 collective-permute-done.45
  470.1 16.3 %collective-permute-done.46 = bf16[128,1536]{0,1:T(8,128)(2,1)S(1)} collective-permute-done((bf16[128,1536]{0,1:T(8,128)(2,1)S(1)}, bf16[128,1536]{0,1:T(8,128)(2,1)S(1)}, u32[]{:S(2)}, u32[]{:S(2)}) %collective-permute-start.46) | collective-permute-done | bytes 393248 | tf_op jit(solution)/shard_map/ppermute | solution.py:60
  546.4 14.1 %convolution_convert_fusion = bf16[1536,1536]{1,0:T(8,128)(2,1)S(1)} fusion(bf16[1024,1536]{0,1:T(8,128)(2,1)S(1)} %copy-done.142, bf16[256,768]{1,0:T(8,128)(2,1)S(1)} %copy-done.191, bf16[256,768]{1,0:T(8,128)(2,1)S(1)} %copy-done.190, bf16[512,768]{1,0:T(8,128)(2,1)S(1)} %copy-done.197, bf16[512,768]{1,0:T(8,128)(2,1)S(1)} %copy-done.196, ...), kind=kOutput, calls=%fused_computation | convolution fusion | flops 4853071872 | bytes 11010048 | tf_op jit(solution)/shard_map/dot_general | solution.py:29
  584.0 8.8 collective-permute-done.50
  599.3 7.4 collective-permute-done.64
  606.7 9.0 collective-permute-start.65
  616.6 7.0 collective-permute-done.52
  624.0 12.8 %collective-permute-start.53 = (bf16[128,1536]{0,1:T(8,128)(2,1)S(1)}, bf16[128,1536]{0,1:T(8,128)(2,1)S(1)}, u32[]{:S(2)}, u32[]{:S(2)}) collective-permute-start(bf16[128,1536]{0,1:T(8,128)(2,1)S(1)} %add_convert_fusion.7), channel_id=1, source_target_pairs={{0,16},{4,20},{8,24},{12,28},{16,0},{20,4},{24,8},{28,12},{1,17},{... | collective-permute-start | bytes 1179656 | tf_op jit(solution)/shard_map/ppermute | solution.py:60
  636.8 8.9 collective-permute-done.65
  648.1 5.1 collective-permute-done.53
  662.5 9.4 attend_backward.2
  706.0 5.8 copy.316
  770.7 5.1 fusion.57
  777.1 5.2 convolution_convert_fusion.1
  807.3 9.2 collective-permute-done.81
  818.0 7.2 collective-permute-done.82
  828.0 8.8 collective-permute-done.99
  842.2 19.7 %collective-permute-done.83 = bf16[128,1536]{0,1:T(8,128)(2,1)S(1)} collective-permute-done((bf16[128,1536]{0,1:T(8,128)(2,1)S(1)}, bf16[128,1536]{0,1:T(8,128)(2,1)S(1)}, u32[]{:S(2)}, u32[]{:S(2)}) %collective-permute-start.83) | collective-permute-done | bytes 393248 | tf_op jit(solution)/shard_map/ppermute | solution.py:60
  869.9 6.7 collective-permute-done.102
  884.3 9.4 attend_backward.3
  940.2 29.9 %collective-permute-done.109 = bf16[4,96,384]{2,1,0:T(8,128)(2,1)} collective-permute-done((bf16[4,96,384]{2,1,0:T(8,128)(2,1)}, bf16[4,96,384]{2,1,0:T(8,128)(2,1)}, u32[]{:S(2)}, u32[]{:S(2)}) %collective-permute-start.109) | collective-permute-done | bytes 294944 | tf_op jit(solution)/shard_map/ppermute | solution.py:53
  991.4 7.4 collective-permute-done.91
  1014.0 8.1 collective-permute-done.95
  (1064 shorter events, 487.5 us)
Async XLA Ops:
  0.7 163.0 %collective-permute-start.56 = (bf16[128,1536]{1,0:T(8,128)(2,1)}, bf16[128,1536]{1,0:T(8,128)(2,1)S(1)}, u32[]{:S(2)}, u32[]{:S(2)}) collective-permute-start(bf16[128,1536]{1,0:T(8,128)(2,1)} %param.11), channel_id=1, source_target_pairs={{0,8},{4,12},{8,16},{12,20},{16,24},{20,28},{24,0},{28,4},{1,9},{5... | collective-permute-start | bytes 1179656 | tf_op jit(solution)/shard_map/ppermute | solution.py:60
  3.7 168.2 %collective-permute-start.57 = (bf16[128,1536]{1,0:T(8,128)(2,1)}, bf16[128,1536]{1,0:T(8,128)(2,1)}, u32[]{:S(2)}, u32[]{:S(2)}) collective-permute-start(bf16[128,1536]{1,0:T(8,128)(2,1)} %param.11), channel_id=1, source_target_pairs={{0,24},{4,28},{8,0},{12,4},{16,8},{20,12},{24,16},{28,20},{1,25},{... | collective-permute-start | bytes 1179656 | tf_op jit(solution)/shard_map/ppermute | solution.py:60
  8.5 47.7 %collective-permute-start = (bf16[48,1152]{1,0:T(8,128)(2,1)S(1)}, bf16[48,1152]{1,0:T(8,128)(2,1)S(1)}, u32[]{:S(2)}, u32[]{:S(2)}) collective-permute-start(bf16[48,1152]{1,0:T(8,128)(2,1)S(1)} %broadcast_select_fusion.2), channel_id=1, source_target_pairs={{0,1},{1,0},{2,3},{3,2},{4,5},{5,4},{6,7},{7,6},{8,9},{9,8},{10,11... | collective-permute-start | bytes 331784 | tf_op jit(solution)/shard_map/ppermute | solution.py:50
  82.4 31.2 %collective-permute-start.17 = (bf16[96,2688]{1,0:T(8,128)(2,1)S(1)}, bf16[96,2688]{1,0:T(8,128)(2,1)S(1)}, u32[]{:S(2)}, u32[]{:S(2)}) collective-permute-start(bf16[96,2688]{1,0:T(8,128)(2,1)S(1)} %constant_dynamic-update-slice_fusion.5), channel_id=1, source_target_pairs={{0,16},{4,20},{8,24},{12,28},{16,0},{20,4},{24,8},{28,12},{1,17},{... | collective-permute-start | bytes 1548296 | tf_op jit(solution)/shard_map/ppermute | solution.py:60
  83.2 32.0 %collective-permute-start.18 = (bf16[96,2688]{1,0:T(8,128)(2,1)S(1)}, bf16[96,2688]{1,0:T(8,128)(2,1)S(1)}, u32[]{:S(2)}, u32[]{:S(2)}) collective-permute-start(bf16[96,2688]{1,0:T(8,128)(2,1)S(1)} %constant_dynamic-update-slice_fusion.5), channel_id=1, source_target_pairs={{0,24},{4,28},{8,0},{12,4},{16,8},{20,12},{24,16},{28,20},{1,25},{... | collective-permute-start | bytes 1548296 | tf_op jit(solution)/shard_map/ppermute | solution.py:60
  115.3 26.4 %collective-permute-start.19 = (bf16[4,96,1536]{2,1,0:T(8,128)(2,1)S(1)}, bf16[4,96,1536]{2,1,0:T(8,128)(2,1)S(1)}, u32[]{:S(2)}, u32[]{:S(2)}) collective-permute-start(bf16[4,96,1536]{2,1,0:T(8,128)(2,1)S(1)} %slice.962), channel_id=1, source_target_pairs={{0,2},{1,3},{2,0},{3,1},{4,6},{5,7},{6,4},{7,5},{8,10},{9,11},{10,... | collective-permute-start | bytes 3538952 | tf_op jit(solution)/shard_map/ppermute | solution.py:53
  144.2 94.6 %collective-permute-start.20 = (bf16[4,2,96,1536]{3,2,1,0:T(8,128)(2,1)}, bf16[4,2,96,1536]{3,2,1,0:T(8,128)(2,1)}, u32[]{:S(2)}, u32[]{:S(2)}) collective-permute-start(bf16[4,2,96,1536]{3,2,1,0:T(8,128)(2,1)} %pad_maximum_fusion.4), channel_id=1, source_target_pairs={{0,4},{4,0},{8,12},{12,8},{16,20},{20,16},{24,28},{28,24},{1,5},{5... | collective-permute-start | bytes 7077896 | tf_op jit(solution)/shard_map/ppermute | solution.py:56
  162.5 72.6 %collective-permute-start.34 = (bf16[4,96,1152]{2,1,0:T(8,128)(2,1)}, bf16[4,96,1152]{2,1,0:T(8,128)(2,1)}, u32[]{:S(2)}, u32[]{:S(2)}) collective-permute-start(bf16[4,96,1152]{2,1,0:T(8,128)(2,1)} %slice.986), channel_id=1, source_target_pairs={{0,4},{4,0},{8,12},{12,8},{16,20},{20,16},{24,28},{28,24},{1,5},{5... | collective-permute-start | bytes 2654216 | tf_op jit(solution)/shard_map/ppermute | solution.py:56
  171.9 87.3 %collective-permute-start.54 = (bf16[128,1536]{1,0:T(8,128)(2,1)}, bf16[128,1536]{1,0:T(8,128)(2,1)S(1)}, u32[]{:S(2)}, u32[]{:S(2)}) collective-permute-start(bf16[128,1536]{1,0:T(8,128)(2,1)} %param.11), channel_id=1, source_target_pairs={{0,4},{4,0},{8,12},{12,8},{16,20},{20,16},{24,28},{28,24},{1,5},{5... | collective-permute-start | bytes 1179656 | tf_op jit(solution)/shard_map/ppermute | solution.py:56
  171.9 55.3 %collective-permute-start.14 = (bf16[256,256]{1,0:T(8,128)(2,1)}, bf16[256,256]{1,0:T(8,128)(2,1)S(1)}, u32[]{:S(2)}, u32[]{:S(2)}) collective-permute-start(bf16[256,256]{1,0:T(8,128)(2,1)} %pad_maximum_fusion.46), channel_id=1, source_target_pairs={{0,4},{1,5},{2,6},{3,7},{4,8},{5,9},{6,10},{7,11},{8,12},{9,13},{1... | collective-permute-start | bytes 393224 | tf_op jit(solution)/shard_map/ppermute | solution.py:66
  176.8 50.5 %collective-permute-start.15 = (bf16[256,256]{1,0:T(8,128)(2,1)}, bf16[256,256]{1,0:T(8,128)(2,1)S(1)}, u32[]{:S(2)}, u32[]{:S(2)}) collective-permute-start(bf16[256,256]{1,0:T(8,128)(2,1)} %pad_maximum_fusion.46), channel_id=1, source_target_pairs={{0,2},{1,3},{2,4},{3,5},{4,6},{5,7},{6,8},{7,9},{8,10},{9,11},{10,... | collective-permute-start | bytes 393224 | tf_op jit(solution)/shard_map/ppermute | solution.py:66
  237.0 38.0 %collective-permute-start.35 = (bf16[4,2,96,1152]{3,2,0,1:T(8,128)(2,1)S(1)}, bf16[4,2,96,1152]{3,2,0,1:T(8,128)(2,1)S(1)}, u32[]{:S(2)}, u32[]{:S(2)}) collective-permute-start(bf16[4,2,96,1152]{3,2,0,1:T(8,128)(2,1)S(1)} %pad_maximum_fusion.6), channel_id=1, source_target_pairs={{0,2},{1,3},{2,0},{3,1},{4,6},{5,7},{6,4},{7,5},{8,10},{9,11},{10,... | collective-permute-start | bytes 5308424 | tf_op jit(solution)/shard_map/ppermute | solution.py:53
  245.1 174.6 %collective-permute-start.61 = (bf16[256,1536]{1,0:T(8,128)(2,1)S(1)}, bf16[256,1536]{1,0:T(8,128)(2,1)S(1)}, u32[]{:S(2)}, u32[]{:S(2)}) collective-permute-start(bf16[256,1536]{1,0:T(8,128)(2,1)S(1)} %pad_maximum_fusion.16), channel_id=1, source_target_pairs={{0,4},{4,0},{8,12},{12,8},{16,20},{20,16},{24,28},{28,24},{1,5},{5... | collective-permute-start | bytes 2359304 | tf_op jit(solution)/shard_map/ppermute | solution.py:56
  247.6 166.0 %collective-permute-start.58 = (bf16[128,1536]{1,0:T(8,128)(2,1)}, bf16[128,1536]{1,0:T(8,128)(2,1)S(1)}, u32[]{:S(2)}, u32[]{:S(2)}) collective-permute-start(bf16[128,1536]{1,0:T(8,128)(2,1)} %param.11), channel_id=1, source_target_pairs={{0,16},{4,20},{8,24},{12,28},{16,0},{20,4},{24,8},{28,12},{1,17},{... | collective-permute-start | bytes 1179656 | tf_op jit(solution)/shard_map/ppermute | solution.py:60
  260.5 30.0 %collective-permute-start.22 = (bf16[128,1664]{0,1:T(8,128)(2,1)S(1)}, bf16[128,1664]{0,1:T(8,128)(2,1)S(1)}, u32[]{:S(2)}, u32[]{:S(2)}) collective-permute-start(bf16[128,1664]{0,1:T(8,128)(2,1)S(1)} %pad_maximum_fusion.34), channel_id=1, source_target_pairs={{0,4},{4,0},{8,12},{12,8},{16,20},{20,16},{24,28},{28,24},{1,5},{5... | collective-permute-start | bytes 1277960 | tf_op jit(solution)/shard_map/ppermute | solution.py:56
  306.8 37.9 %collective-permute-start.29 = (bf16[256,1664]{0,1:T(8,128)(2,1)S(1)}, bf16[256,1664]{0,1:T(8,128)(2,1)S(1)}, u32[]{:S(2)}, u32[]{:S(2)}) collective-permute-start(bf16[256,1664]{0,1:T(8,128)(2,1)S(1)} %pad_maximum_fusion.10), channel_id=1, source_target_pairs={{0,4},{4,0},{8,12},{12,8},{16,20},{20,16},{24,28},{28,24},{1,5},{5... | collective-permute-start | bytes 2555912 | tf_op jit(solution)/shard_map/ppermute | solution.py:56
  358.1 26.0 %collective-permute-start.28 = (bf16[128,1536]{0,1:T(8,128)(2,1)S(1)}, bf16[128,1536]{0,1:T(8,128)(2,1)S(1)}, u32[]{:S(2)}, u32[]{:S(2)}) collective-permute-start(bf16[128,1536]{0,1:T(8,128)(2,1)S(1)} %slice.977), channel_id=1, source_target_pairs={{0,4},{4,0},{8,12},{12,8},{16,20},{20,16},{24,28},{28,24},{1,5},{5... | collective-permute-start | bytes 1179656 | tf_op jit(solution)/shard_map/ppermute | solution.py:56
  360.5 34.7 %collective-permute-start.23 = (bf16[128,1536]{0,1:T(8,128)(2,1)S(1)}, bf16[128,1536]{0,1:T(8,128)(2,1)S(1)}, u32[]{:S(2)}, u32[]{:S(2)}) collective-permute-start(bf16[128,1536]{0,1:T(8,128)(2,1)S(1)} %slice.971), channel_id=1, source_target_pairs={{0,4},{4,0},{8,12},{12,8},{16,20},{20,16},{24,28},{28,24},{1,5},{5... | collective-permute-start | bytes 1179656 | tf_op jit(solution)/shard_map/ppermute | solution.py:56
  521.4 50.7 %all-to-all-start = ((f32[8,1,128]{2,1,0:T(1,128)}), f32[8,1,128]{2,1,0:T(1,128)}, u32[]{:S(2)}, u32[]{:S(2)}) async-start(f32[8,1,128]{2,1,0:T(1,128)} %constant_dynamic-update-slice_fusion.55), calls=%async_computation | async-start | bytes 8192 | tf_op jit(solution)/shard_map/all_to_all | solution.py:558
  530.3 45.7 %collective-permute-start.60 = (bf16[128,1536]{0,1:T(8,128)(2,1)}, bf16[128,1536]{0,1:T(8,128)(2,1)}, u32[]{:S(2)}, u32[]{:S(2)}) collective-permute-start(bf16[128,1536]{0,1:T(8,128)(2,1)} %slice.1016), channel_id=1, source_target_pairs={{0,4},{4,0},{8,12},{12,8},{16,20},{20,16},{24,28},{28,24},{1,5},{5... | collective-permute-start | bytes 1179656 | tf_op jit(solution)/shard_map/ppermute | solution.py:56
  538.3 40.5 %collective-permute-start.62 = (bf16[256,1536]{0,1:T(8,128)(2,1)}, bf16[256,1536]{0,1:T(8,128)(2,1)}, u32[]{:S(2)}, u32[]{:S(2)}) collective-permute-start(bf16[256,1536]{0,1:T(8,128)(2,1)} %slice.1018), channel_id=1, source_target_pairs={{0,4},{4,0},{8,12},{12,8},{16,20},{20,16},{24,28},{28,24},{1,5},{5... | collective-permute-start | bytes 2359304 | tf_op jit(solution)/shard_map/ppermute | solution.py:56
  540.9 83.1 %collective-permute-start.55 = (bf16[128,1536]{0,1:T(8,128)(2,1)}, bf16[128,1536]{0,1:T(8,128)(2,1)}, u32[]{:S(2)}, u32[]{:S(2)}) collective-permute-start(bf16[128,1536]{0,1:T(8,128)(2,1)} %slice.1014), channel_id=1, source_target_pairs={{0,4},{4,0},{8,12},{12,8},{16,20},{20,16},{24,28},{28,24},{1,5},{5... | collective-permute-start | bytes 1179656 | tf_op jit(solution)/shard_map/ppermute | solution.py:56
  543.4 34.0 %collective-permute-start.48 = (bf16[128,1536]{0,1:T(8,128)(2,1)}, bf16[128,1536]{0,1:T(8,128)(2,1)}, u32[]{:S(2)}, u32[]{:S(2)}) collective-permute-start(bf16[128,1536]{0,1:T(8,128)(2,1)} %slice.1006), channel_id=1, source_target_pairs={{0,4},{4,0},{8,12},{12,8},{16,20},{20,16},{24,28},{28,24},{1,5},{5... | collective-permute-start | bytes 1179656 | tf_op jit(solution)/shard_map/ppermute | solution.py:56
  544.6 48.2 %collective-permute-start.50 = (bf16[256,1536]{0,1:T(8,128)(2,1)}, bf16[256,1536]{0,1:T(8,128)(2,1)}, u32[]{:S(2)}, u32[]{:S(2)}) collective-permute-start(bf16[256,1536]{0,1:T(8,128)(2,1)} %slice.1010), channel_id=1, source_target_pairs={{0,4},{4,0},{8,12},{12,8},{16,20},{20,16},{24,28},{28,24},{1,5},{5... | collective-permute-start | bytes 2359304 | tf_op jit(solution)/shard_map/ppermute | solution.py:56
  576.0 72.1 %collective-permute-start.43 = (bf16[128,1536]{0,1:T(8,128)(2,1)}, bf16[128,1536]{0,1:T(8,128)(2,1)S(1)}, u32[]{:S(2)}, u32[]{:S(2)}) collective-permute-start(bf16[128,1536]{0,1:T(8,128)(2,1)} %slice.1002), channel_id=1, source_target_pairs={{0,4},{4,0},{8,12},{12,8},{16,20},{20,16},{24,28},{28,24},{1,5},{5... | collective-permute-start | bytes 1179656 | tf_op jit(solution)/shard_map/ppermute | solution.py:56
  606.7 39.0 %collective-permute-start.65 = (bf16[128,1536]{0,1:T(8,128)(2,1)S(1)}, bf16[128,1536]{0,1:T(8,128)(2,1)S(1)}, u32[]{:S(2)}, u32[]{:S(2)}) collective-permute-start(bf16[128,1536]{0,1:T(8,128)(2,1)S(1)} %add_convert_fusion.5), channel_id=1, source_target_pairs={{0,16},{4,20},{8,24},{12,28},{16,0},{20,4},{24,8},{28,12},{1,17},{... | collective-permute-start | bytes 1179656 | tf_op jit(solution)/shard_map/ppermute | solution.py:60
  616.5 74.9 %collective-permute-start.117 = (bf16[2,384,1536]{2,1,0:T(8,128)(2,1)}, bf16[2,384,1536]{2,1,0:T(8,128)(2,1)}, u32[]{:S(2)}, u32[]{:S(2)}) collective-permute-start(bf16[2,384,1536]{2,1,0:T(8,128)(2,1)} %select_bitcast_fusion), channel_id=1, source_target_pairs={{0,1},{1,0},{2,3},{3,2},{4,5},{5,4},{6,7},{7,6},{8,9},{9,8},{10,11... | collective-permute-start | bytes 7077896 | tf_op jit(solution)/shard_map/ppermute | solution.py:50
  623.6 33.7 %collective-permute-start.122 = (bf16[192,1536]{1,0:T(8,128)(2,1)}, bf16[192,1536]{1,0:T(8,128)(2,1)}, u32[]{:S(2)}, u32[]{:S(2)}) collective-permute-start(bf16[192,1536]{1,0:T(8,128)(2,1)} %select_bitcast_fusion.23), channel_id=1, source_target_pairs={{0,2},{1,3},{2,0},{3,1},{4,6},{5,7},{6,4},{7,5},{8,10},{9,11},{10,... | collective-permute-start | bytes 1769480 | tf_op jit(solution)/shard_map/ppermute | solution.py:53
  624.0 29.3 %collective-permute-start.53 = (bf16[128,1536]{0,1:T(8,128)(2,1)S(1)}, bf16[128,1536]{0,1:T(8,128)(2,1)S(1)}, u32[]{:S(2)}, u32[]{:S(2)}) collective-permute-start(bf16[128,1536]{0,1:T(8,128)(2,1)S(1)} %add_convert_fusion.7), channel_id=1, source_target_pairs={{0,16},{4,20},{8,24},{12,28},{16,0},{20,4},{24,8},{28,12},{1,17},{... | collective-permute-start | bytes 1179656 | tf_op jit(solution)/shard_map/ppermute | solution.py:60
  680.0 54.9 %collective-permute-start.100 = (bf16[4,2,96,768]{3,2,0,1:T(8,128)(2,1)}, bf16[4,2,96,768]{3,2,0,1:T(8,128)(2,1)}, u32[]{:S(2)}, u32[]{:S(2)}) collective-permute-start(bf16[4,2,96,768]{3,2,0,1:T(8,128)(2,1)} %select_bitcast_fusion.11), channel_id=1, source_target_pairs={{0,4},{4,0},{8,12},{12,8},{16,20},{20,16},{24,28},{28,24},{1,5},{5... | collective-permute-start | bytes 3538952 | tf_op jit(solution)/shard_map/ppermute | solution.py:56
  695.8 47.1 %collective-permute-start.118 = (bf16[384,1536]{1,0:T(8,128)(2,1)}, bf16[384,1536]{1,0:T(8,128)(2,1)}, u32[]{:S(2)}, u32[]{:S(2)}) collective-permute-start(bf16[384,1536]{1,0:T(8,128)(2,1)} %select_bitcast_fusion.9), channel_id=1, source_target_pairs={{0,2},{1,3},{2,0},{3,1},{4,6},{5,7},{6,4},{7,5},{8,10},{9,11},{10,... | collective-permute-start | bytes 3538952 | tf_op jit(solution)/shard_map/ppermute | solution.py:53
  716.9 82.7 %collective-permute-start.98 = (bf16[4,2,96,1152]{3,2,0,1:T(8,128)(2,1)}, bf16[4,2,96,1152]{3,2,0,1:T(8,128)(2,1)}, u32[]{:S(2)}, u32[]{:S(2)}) collective-permute-start(bf16[4,2,96,1152]{3,2,0,1:T(8,128)(2,1)} %select_bitcast_fusion.4), channel_id=1, source_target_pairs={{0,2},{1,3},{2,0},{3,1},{4,6},{5,7},{6,4},{7,5},{8,10},{9,11},{10,... | collective-permute-start | bytes 5308424 | tf_op jit(solution)/shard_map/ppermute | solution.py:53
  720.3 26.0 %collective-permute-start.79 = (bf16[256,1536]{0,1:T(8,128)(2,1)S(1)}, bf16[256,1536]{0,1:T(8,128)(2,1)S(1)}, u32[]{:S(2)}, u32[]{:S(2)}) collective-permute-start(bf16[256,1536]{0,1:T(8,128)(2,1)S(1)} %pad_maximum_fusion.18), channel_id=1, source_target_pairs={{0,4},{4,0},{8,12},{12,8},{16,20},{20,16},{24,28},{28,24},{1,5},{5... | collective-permute-start | bytes 2359304 | tf_op jit(solution)/shard_map/ppermute | solution.py:56
  734.9 103.1 %collective-permute-start.73 = (bf16[128,1536]{0,1:T(8,128)(2,1)}, bf16[128,1536]{0,1:T(8,128)(2,1)}, u32[]{:S(2)}, u32[]{:S(2)}) collective-permute-start(bf16[128,1536]{0,1:T(8,128)(2,1)} %slice.1033), channel_id=1, source_target_pairs={{0,4},{4,0},{8,12},{12,8},{16,20},{20,16},{24,28},{28,24},{1,5},{5... | collective-permute-start | bytes 1179656 | tf_op jit(solution)/shard_map/ppermute | solution.py:56
  741.8 54.4 %collective-permute-start.101 = (bf16[4,96,768]{2,1,0:T(8,128)(2,1)}, bf16[4,96,768]{2,1,0:T(8,128)(2,1)}, u32[]{:S(2)}, u32[]{:S(2)}) collective-permute-start(bf16[4,96,768]{2,1,0:T(8,128)(2,1)} %select_bitcast_fusion.27), channel_id=1, source_target_pairs={{0,2},{1,3},{2,0},{3,1},{4,6},{5,7},{6,4},{7,5},{8,10},{9,11},{10,... | collective-permute-start | bytes 1769480 | tf_op jit(solution)/shard_map/ppermute | solution.py:53
  759.2 34.7 %all-to-all-start.1 = ((f32[8,1,128]{2,1,0:T(1,128)}), f32[8,1,128]{2,1,0:T(1,128)S(1)}, u32[]{:S(2)}, u32[]{:S(2)}) async-start(f32[8,1,128]{2,1,0:T(1,128)} %constant_dynamic-update-slice_fusion.47), calls=%async_computation.1 | async-start | bytes 8192 | tf_op jit(solution)/shard_map/all_to_all | solution.py:558
  768.6 29.4 %collective-permute-start.78 = (bf16[128,1536]{0,1:T(8,128)(2,1)}, bf16[128,1536]{0,1:T(8,128)(2,1)}, u32[]{:S(2)}, u32[]{:S(2)}) collective-permute-start(bf16[128,1536]{0,1:T(8,128)(2,1)} %slice.1035), channel_id=1, source_target_pairs={{0,4},{4,0},{8,12},{12,8},{16,20},{20,16},{24,28},{28,24},{1,5},{5... | collective-permute-start | bytes 1179656 | tf_op jit(solution)/shard_map/ppermute | solution.py:56
  776.9 25.0 %collective-permute-start.80 = (bf16[256,1536]{0,1:T(8,128)(2,1)}, bf16[256,1536]{0,1:T(8,128)(2,1)}, u32[]{:S(2)}, u32[]{:S(2)}) collective-permute-start(bf16[256,1536]{0,1:T(8,128)(2,1)} %slice.1037), channel_id=1, source_target_pairs={{0,4},{4,0},{8,12},{12,8},{16,20},{20,16},{24,28},{28,24},{1,5},{5... | collective-permute-start | bytes 2359304 | tf_op jit(solution)/shard_map/ppermute | solution.py:56
  796.2 121.4 %collective-permute-start.115 = (bf16[2,384,1536]{2,1,0:T(8,128)(2,1)}, bf16[2,384,1536]{2,1,0:T(8,128)(2,1)}, u32[]{:S(2)}, u32[]{:S(2)}) collective-permute-start(bf16[2,384,1536]{2,1,0:T(8,128)(2,1)} %select_bitcast_fusion.1), channel_id=1, source_target_pairs={{0,1},{1,0},{2,3},{3,2},{4,5},{5,4},{6,7},{7,6},{8,9},{9,8},{10,11... | collective-permute-start | bytes 7077896 | tf_op jit(solution)/shard_map/ppermute | solution.py:50
  798.0 28.2 %collective-permute-start.119 = (bf16[2,192,1536]{2,1,0:T(8,128)(2,1)S(1)}, bf16[2,192,1536]{2,1,0:T(8,128)(2,1)S(1)}, u32[]{:S(2)}, u32[]{:S(2)}) collective-permute-start(bf16[2,192,1536]{2,1,0:T(8,128)(2,1)S(1)} %copy-done.89), channel_id=1, source_target_pairs={{0,1},{1,0},{2,3},{3,2},{4,5},{5,4},{6,7},{7,6},{8,9},{9,8},{10,11... | collective-permute-start | bytes 3538952 | tf_op jit(solution)/shard_map/ppermute | solution.py:50
  825.2 36.7 %collective-permute-start.83 = (bf16[128,1536]{0,1:T(8,128)(2,1)S(1)}, bf16[128,1536]{0,1:T(8,128)(2,1)S(1)}, u32[]{:S(2)}, u32[]{:S(2)}) collective-permute-start(bf16[128,1536]{0,1:T(8,128)(2,1)S(1)} %add_convert_fusion.4), channel_id=1, source_target_pairs={{0,16},{4,20},{8,24},{12,28},{16,0},{20,4},{24,8},{28,12},{1,17},{... | collective-permute-start | bytes 1179656 | tf_op jit(solution)/shard_map/ppermute | solution.py:60
  826.7 38.3 %collective-permute-start.120 = (bf16[192,1536]{1,0:T(8,128)(2,1)S(1)}, bf16[192,1536]{1,0:T(8,128)(2,1)S(1)}, u32[]{:S(2)}, u32[]{:S(2)}) collective-permute-start(bf16[192,1536]{1,0:T(8,128)(2,1)S(1)} %select_bitcast_fusion.24), channel_id=1, source_target_pairs={{0,2},{1,3},{2,0},{3,1},{4,6},{5,7},{6,4},{7,5},{8,10},{9,11},{10,... | collective-permute-start | bytes 1769480 | tf_op jit(solution)/shard_map/ppermute | solution.py:53
  837.3 30.6 %collective-permute-start.104 = (bf16[96,1920]{1,0:T(8,128)(2,1)S(1)}, bf16[96,1920]{1,0:T(8,128)(2,1)S(1)}, u32[]{:S(2)}, u32[]{:S(2)}) collective-permute-start(bf16[96,1920]{1,0:T(8,128)(2,1)S(1)} %get-tuple-element.207), channel_id=1, source_target_pairs={{0,8},{4,12},{8,16},{12,20},{16,24},{20,28},{24,0},{28,4},{1,9},{5... | collective-permute-start | bytes 1105928 | tf_op jit(solution)/shard_map/ppermute | solution.py:60
  838.0 31.9 %collective-permute-start.103 = (bf16[96,1920]{1,0:T(8,128)(2,1)S(1)}, bf16[96,1920]{1,0:T(8,128)(2,1)S(1)}, u32[]{:S(2)}, u32[]{:S(2)}) collective-permute-start(bf16[96,1920]{1,0:T(8,128)(2,1)S(1)} %get-tuple-element.206), channel_id=1, source_target_pairs={{0,16},{4,20},{8,24},{12,28},{16,0},{20,4},{24,8},{28,12},{1,17},{... | collective-permute-start | bytes 1105928 | tf_op jit(solution)/shard_map/ppermute | solution.py:60
  916.6 62.2 %collective-permute-start.90 = (bf16[4,2,96,512]{3,2,0,1:T(8,128)(2,1)}, bf16[4,2,96,512]{3,2,0,1:T(8,128)(2,1)}, u32[]{:S(2)}, u32[]{:S(2)}) collective-permute-start(bf16[4,2,96,512]{3,2,0,1:T(8,128)(2,1)} %select_bitcast_fusion.20), channel_id=1, source_target_pairs={{0,2},{1,3},{2,0},{3,1},{4,6},{5,7},{6,4},{7,5},{8,10},{9,11},{10,... | collective-permute-start | bytes 2359304 | tf_op jit(solution)/shard_map/ppermute | solution.py:53
  921.4 87.4 %collective-permute-start.116 = (bf16[384,1536]{1,0:T(8,128)(2,1)}, bf16[384,1536]{1,0:T(8,128)(2,1)}, u32[]{:S(2)}, u32[]{:S(2)}) collective-permute-start(bf16[384,1536]{1,0:T(8,128)(2,1)} %select_bitcast_fusion.10), channel_id=1, source_target_pairs={{0,2},{1,3},{2,0},{3,1},{4,6},{5,7},{6,4},{7,5},{8,10},{9,11},{10,... | collective-permute-start | bytes 3538952 | tf_op jit(solution)/shard_map/ppermute | solution.py:53
  932.0 38.2 %collective-permute-start.109 = (bf16[4,96,384]{2,1,0:T(8,128)(2,1)}, bf16[4,96,384]{2,1,0:T(8,128)(2,1)}, u32[]{:S(2)}, u32[]{:S(2)}) collective-permute-start(bf16[4,96,384]{2,1,0:T(8,128)(2,1)} %select_bitcast_fusion.34), channel_id=1, source_target_pairs={{0,2},{1,3},{2,0},{3,1},{4,6},{5,7},{6,4},{7,5},{8,10},{9,11},{10,... | collective-permute-start | bytes 884744 | tf_op jit(solution)/shard_map/ppermute | solution.py:53
  936.4 52.2 %collective-permute-start.92 = (bf16[4,2,96,640]{3,2,0,1:T(8,128)(2,1)}, bf16[4,2,96,640]{3,2,0,1:T(8,128)(2,1)S(1)}, u32[]{:S(2)}, u32[]{:S(2)}) collective-permute-start(bf16[4,2,96,640]{3,2,0,1:T(8,128)(2,1)} %select_bitcast_fusion.14), channel_id=1, source_target_pairs={{0,4},{4,0},{8,12},{12,8},{16,20},{20,16},{24,28},{28,24},{1,5},{5... | collective-permute-start | bytes 2949128 | tf_op jit(solution)/shard_map/ppermute | solution.py:56
  (297 other events, 4785.2 us)

commit v3 on v2

--- a/solution.py
+++ b/solution.py
@@ -27,6 +27,51 @@
 
 def dot(left, right, dims):
     return lax.dot_general(left, right, (dims, ((), ())), preferred_element_type=f32)
+
+
+def after(value, *events):
+    there = None
+    for event in events:
+        if event is None:
+            continue
+        sample = lax.slice(event, (0,) * event.ndim, (1,) * event.ndim).reshape(())
+        same = sample == sample
+        there = same if there is None else there & same
+    return value if there is None else jnp.where(there, value, jnp.zeros_like(value))
+
+
+class Task:
+    def __init__(self, legs):
+        self.legs = legs
+        self.marks = []
+        self.result = None
+        self.running = True
+        self.go()
+
+    def go(self, *events):
+        if not self.running:
+            return
+        try:
+            self.marks = self.legs.send(events) if self.marks else next(self.legs)
+        except StopIteration as end:
+            self.running = False
+            self.marks = []
+            self.result = end.value
+
+    def finish(self):
+        while self.running:
+            self.go(*self.marks)
+        return self.result
+
+
+def phase(*tasks):
+    events = [mark for task in tasks for mark in task.marks]
+    for task in tasks:
+        task.go(*events)
+
+
+def place_of(stacked, index, axis):
+    return lax.dynamic_index_in_dim(stacked, index, axis, keepdims=False)
 
 
 class Wires:
@@ -70,35 +115,53 @@
             [jnp.where(flag == 0, own, other), jnp.where(flag == 0, other, own)], axis=axis
         )
 
-    def token_gather(self, value):
+    def token_gather(self, value, slowly=False):
         if not self.by_line:
             return [lax.all_gather(value, "dp", axis=0, tiled=True)]
         side = self.to_side(value)
-        one, three = self.along(value, 1), self.along(value, 3)
-        held, one, three = lax.optimization_barrier((value, one, three))
-        two = self.along(held, 2)
-        odd = jnp.concatenate([one, three], axis=0)
+        if slowly:
+            events = yield [side]
+            held = after(value, *events)
+            one, three = self.along(held, 1), self.along(held, 3)
+            events = yield [one, three]
+            two = self.along(after(value, *events), 2)
+            events = yield [two]
+            odd = after(jnp.concatenate([one, three], axis=0), *events)
+            odd_side = self.to_side(odd)
+            events = yield [odd_side]
+            two = after(two, *events)
+        else:
+            one, three = self.along(value, 1), self.along(value, 3)
+            events = yield [side, one, three]
+            odd = jnp.concatenate([one, three], axis=0)
+            odd_side = self.to_side(odd)
+            two = self.along(after(value, *events), 2)
+            events = yield [odd_side, two]
+            two = after(two, *[event for event in events if event is not two])
+        two_side = self.to_side(two)
+        events = yield [two_side]
         return [
             jnp.concatenate([value, side], axis=0),
-            jnp.concatenate([odd, self.to_side(odd)], axis=0),
-            jnp.concatenate([two, self.to_side(two)], axis=0),
+            jnp.concatenate([odd, odd_side], axis=0),
+            jnp.concatenate([two, two_side], axis=0),
         ]
 
     def token_scatter(self, blocks):
         if not self.by_line:
             return lax.psum_scatter(blocks[0], "dp", scatter_dimension=0, tiled=True).astype(f32)
         rows = blocks[0].shape[0] // 2
-
-        def folded(block):
-            half = block.shape[0] // 2
-            return block[:half].astype(f32) + self.to_side(block[half:]).astype(f32)
-
-        odd = folded(blocks[1]).astype(bf16)
+        odd = self.to_side(blocks[1][2 * rows :])
+        events = yield [odd]
+        odd = (blocks[1][: 2 * rows].astype(f32) + odd.astype(f32)).astype(bf16)
         one, three = self.along(odd[:rows], -1), self.along(odd[rows:], -3)
-        two = folded(blocks[2]).astype(bf16)
-        held, one, three = lax.optimization_barrier((two, one, three))
-        two = self.along(held, -2)
-        return folded(blocks[0]) + one.astype(f32) + three.astype(f32) + two.astype(f32)
+        two = self.to_side(after(blocks[2][rows:], *events))
+        events = yield [one, three, two]
+        two = (blocks[2][:rows].astype(f32) + two.astype(f32)).astype(bf16)
+        two = self.along(after(two, *events), -2)
+        side = self.to_side(after(blocks[0][rows:], *events))
+        events = yield [two, side]
+        total = blocks[0][:rows].astype(f32) + side.astype(f32)
+        return total + one.astype(f32) + three.astype(f32) + two.astype(f32)
 
     def token_owner(self):
         if not self.by_line:
@@ -109,71 +172,132 @@
             for members in ((0,), (1, 3), (2,))
         ]
 
+    def key_gather(self, own, depth):
+        earlier = [self.chips_on(own, step) for step in range(depth, 0, -1)]
+        events = yield earlier
+        return jnp.concatenate(earlier + [own], axis=0)
+
+    def key_scatter(self, sums, depth):
+        rows = sums.shape[0] // (depth + 1)
+        earlier = [
+            self.chips_on(sums[k * rows : (k + 1) * rows].astype(bf16), k - depth)
+            for k in range(depth)
+        ]
+        events = yield earlier
+        return sum(
+            (value.astype(f32) for value in earlier), sums[depth * rows :]
+        )
+
+    def expert_sums(self, pairs):
+        if not self.by_line:
+            totals = [dot(inputs, grads, ((0,), (0,))).astype(bf16) for inputs, grads in pairs]
+            return [
+                lax.psum_scatter(total, "seq", scatter_dimension=0, tiled=True).astype(f32)
+                for total in totals
+            ]
+        kept, crossed = [], []
+        for inputs, grads in pairs:
+            whole = dot(inputs, grads, ((0,), (0,))).astype(bf16)
+            whole = whole.reshape(2, 2, whole.shape[0] // 4, -1)
+            kept.append(place_of(whole, self.core, 1))
+            crossed.append(self.to_core(place_of(whole, 1 - self.core, 1)))
+        events = yield crossed
+
+        def half(k, pair):
+            return place_of(kept[k], pair, 0).astype(f32) + place_of(
+                crossed[k], pair, 0
+            ).astype(f32)
+
+        others = [
+            self.to_pair(after(half(k, 1 - self.pair).astype(bf16), *events))
+            for k in range(len(pairs))
+        ]
+        events = yield others
+        return [half(k, self.pair) + other.astype(f32) for k, other in enumerate(others)]
+
     def core_groups(self):
         count = self.dp_count * self.seq_count
         return [list(range(core, count, CORES)) for core in range(CORES)]
 
-    def chip_gather(self, one, two):
+    def chip_gather_whole(self, block):
+        return lax.all_gather(
+            block, ALL, axis=0, tiled=True, axis_index_groups=self.core_groups()
+        )
+
+    def chip_scatter_whole(self, whole):
+        return lax.psum_scatter(
+            whole, ALL, scatter_dimension=0, tiled=True, axis_index_groups=self.core_groups()
+        ).astype(f32)
+
+    def chip_gather(self, one, two, slowly=False):
         rows, width = one.shape
+        block = jnp.concatenate([one, two], axis=1)
         if not self.by_line:
-            whole = lax.all_gather(
-                jnp.concatenate([one, two], axis=1),
-                ALL,
-                axis=0,
-                tiled=True,
-                axis_index_groups=self.core_groups(),
-            )
-            return whole[:, :width], whole[:, width:]
-        block = jnp.concatenate([one, two], axis=1)
+            return self.chip_gather_whole(block)
+        pieces = [block, self.along(block, 1), None, self.along(block, 3)]
+        if slowly:
+            events = yield [pieces[1], pieces[3]]
+            pieces[2] = self.along(after(block, *events), 2)
+            events = yield [pieces[2]]
+        else:
+            pieces[2] = self.along(block, 2)
+            events = yield pieces[1:]
         lines = jnp.zeros((LINE,) + block.shape, block.dtype)
-        for k in range(LINE):
-            piece = block if k == 0 else self.along(block, k)
+        for k, piece in enumerate(pieces):
             place = lax.rem(self.line - k + self.length, self.length)
             lines = lax.dynamic_update_slice(lines, piece[None], (place, 0, 0))
+        lines = lines if not slowly else after(lines, *events)
         one, two = lines[:, :, :width], lines[:, :, width:]
-        one = self.ordered(self.side, one, self.to_side(one), 1)
-        two = self.ordered(self.pair, two, self.to_pair(two), 1)
-        one = self.ordered(self.pair, one, self.to_pair(one), 2)
-        two = self.ordered(self.side, two, self.to_side(two), 1)
-        return one.reshape(self.chips * rows, -1), two.reshape(self.chips * rows, -1)
-
-    def picked(self, flag, stacked, axis):
-        first, second = (
-            lax.index_in_dim(stacked, 0, axis, keepdims=False),
-            lax.index_in_dim(stacked, 1, axis, keepdims=False),
-        )
-        return jnp.where(flag == 0, first, second), jnp.where(flag == 0, second, first)
-
-    def chip_scatter(self, one, two):
+        side, pair = self.to_side(one), self.to_pair(two)
+        events = yield [side, pair]
+        one = self.ordered(self.side, one, after(side, *events), 1)
+        two = self.ordered(self.pair, two, after(pair, *events), 1)
+        pair, side = self.to_pair(one), self.to_side(two)
+        events = yield [pair, side]
+        one = self.ordered(self.pair, one, pair, 2)
+        two = self.ordered(self.side, two, side, 1)
+        return jnp.concatenate(
+            [part.reshape(self.chips * rows, -1) for part in (one, two)], axis=1
+        )
+
+    def chip_scatter(self, one, two, slowly=False):
         width = one.shape[1]
         rows = one.shape[0] // self.chips
         if not self.by_line:
-            total = lax.psum_scatter(
-                jnp.concatenate([one, two], axis=1),
-                ALL,
-                scatter_dimension=0,
-                tiled=True,
-                axis_index_groups=self.core_groups(),
-            ).astype(f32)
+            total = self.chip_scatter_whole(jnp.concatenate([one, two], axis=1))
             return total[:, :width], total[:, width:]
 
-        def step(flag, stacked, axis, move):
-            kept, sent = self.picked(flag, stacked, axis)
-            return (kept.astype(f32) + move(sent).astype(f32)).astype(bf16)
+        def added(flag, stacked, axis, got, events):
+            kept = place_of(stacked, flag, axis).astype(f32)
+            return (kept + after(got, *events).astype(f32)).astype(bf16)
 
         one = one.reshape(LINE, 2, 2, rows, -1)
         two = two.reshape(LINE, 2, 2, rows, -1)
-        one = step(self.pair, one, 2, self.to_pair)
-        two = step(self.side, two, 1, self.to_side)
-        one = step(self.side, one, 1, self.to_side)
-        two = step(self.pair, two, 1, self.to_pair)
+        got_one = self.to_pair(place_of(one, 1 - self.pair, 2))
+        got_two = self.to_side(place_of(two, 1 - self.side, 1))
+        events = yield [got_one, got_two]
+        one = added(self.pair, one, 2, got_one, events)
+        two = added(self.side, two, 1, got_two, events)
+        got_one = self.to_side(place_of(one, 1 - self.side, 1))
+        got_two = self.to_pair(place_of(two, 1 - self.pair, 1))
+        events = yield [got_one, got_two]
+        one = added(self.side, one, 1, got_one, events)
+        two = added(self.pair, two, 1, got_two, events)
         both = jnp.concatenate([one, two], axis=2)
-        total = None
-        for k in range(LINE):
-            place = lax.rem(self.line - k + self.length, self.length)
-            piece = lax.dynamic_index_in_dim(both, place, 0, keepdims=False)
-            piece = (piece if k == 0 else self.along(piece, -k)).astype(f32)
-            total = piece if k == 0 else total + piece
+        pieces = [
+            place_of(both, lax.rem(self.line - k + self.length, self.length), 0)
+            for k in range(LINE)
+        ]
+        for k in (1, 3):
+            pieces[k] = self.along(pieces[k], -k)
+        if slowly:
+            events = yield [pieces[1], pieces[3]]
+            pieces[2] = self.along(after(pieces[2], *events), -2)
+            events = yield [pieces[2]]
+        else:
+            pieces[2] = self.along(pieces[2], -2)
+            events = yield pieces[1:]
+        total = sum(piece.astype(f32) for piece in pieces)
         return total[:, :width], total[:, width:]
 
     def chip_rows(self, value):
@@ -182,16 +306,6 @@
     def chip_sum(self, value):
         rows = value.shape[0] // 2
         return value[:rows] + self.to_core(value[rows:].astype(bf16)).astype(f32)
-
-    def seq_scatter(self, value):
-        rows, columns = value.shape
-        if self.pairs != 2:
-            return lax.psum_scatter(value, "seq", scatter_dimension=0, tiled=True).astype(f32)
-        piece = value.reshape(2, 2, rows // 4, columns)
-        kept, sent = self.picked(self.core, piece, 1)
-        piece = (kept.astype(f32) + self.to_core(sent).astype(f32)).astype(bf16)
-        kept, sent = self.picked(self.pair, piece, 0)
-        return kept.astype(f32) + self.to_pair(sent).astype(f32)
 
 
 def doc_labels(token_index, doc_lengths, seq_length):
@@ -399,6 +513,8 @@
     expert_ids = jnp.arange(expert_count, dtype=jnp.int32)
     my_expert = (expert_ids == wires.dp_index)[None, :]
     route_names = jnp.pad(routes.astype(bf16), ((0, 0), (0, 128 - routes.shape[1])))
+    lane = jnp.arange(128, dtype=jnp.int32)[None, :]
+
     small_width = -(-(expert_count + 2) // 128) * 128
 
     def packed_weights(layer_index):
@@ -428,68 +544,77 @@
 
         return per_chip(*fronts), per_chip(*backs)
 
+    def split_front(front):
+        small = front[:, qkv_width:]
+        return (
+            small[:, expert_count : expert_count + 2].astype(f32).T,
+            front[:, :qkv_width],
+            small[:, :expert_count],
+        )
+
     packed = [packed_weights(layer_index) for layer_index in range(layer_count)]
-    cut = (q_width // 2) // 128 * 128 + 256
-    fronts = [
-        jnp.concatenate(wires.chip_gather(packed[0][0][:, :cut], packed[0][0][:, cut:]), axis=1)
-    ]
-    rest_front = jnp.concatenate([front for front, _ in packed[1:]], axis=1)
-    rest_back = jnp.concatenate([back for _, back in packed], axis=1)
-    rest_front, rest_back, fronts[0] = lax.optimization_barrier((rest_front, rest_back, fronts[0]))
-    rest_front, rest_back = wires.chip_gather(rest_front, rest_back)
-    front_width = qkv_width + small_width
-    held_weights = []
-    for layer_index in range(layer_count):
-        if layer_index > 0:
-            fronts.append(rest_front[:, (layer_index - 1) * front_width :][:, :front_width])
-        front = fronts[layer_index]
-        back = rest_back[:, layer_index * q_width : (layer_index + 1) * q_width]
-        small = front[:, qkv_width:]
-        held_weights.append(
-            (
-                small[:, expert_count : expert_count + 2].astype(f32).T,
-                front[:, :qkv_width],
-                back,
-                small[:, :expert_count],
-            )
-        )
+    front_width = packed[0][0].shape[1]
+    first = jnp.concatenate(packed[0], axis=1)
+    cut = first.shape[1] // 256 * 128
+    weights = Task(wires.chip_gather(first[:, :cut], first[:, cut:]))
+    gradient = Task(wires.token_gather(cotangent, slowly=True))
+    phase(weights)
+    phase(weights)
+    phase(weights, gradient)
+    held_weights = [weights.finish()]
     stream = activations.astype(f32)
     stored = []
     for layer_index in range(layer_count):
-        gain_rows, qkv_here, out_here, router = held_weights[layer_index]
-        gate_up_here = w_gate_up[layer_index, 0]
-        down_here = w_down[layer_index, 0]
+        front = held_weights[layer_index][:, :front_width]
+        out_here = held_weights[layer_index][:, front_width:]
+        gain_rows, qkv_here, router = split_front(front)
+        gate_up_here, down_here = w_gate_up[layer_index, 0], w_down[layer_index, 0]
+        more = layer_index + 1 < layer_count
         scale_one = norm_scale(stream)
-        normed_one = wires.chip_rows((stream * scale_one * gain_rows[0]).astype(bf16))
+        normed_own = (stream * scale_one * gain_rows[0]).astype(bf16)
+        if more:
+            held_weights.append(
+                wires.chip_gather_whole(
+                    after(jnp.concatenate(packed[layer_index + 1], axis=1), normed_own)
+                )
+            )
+        normed_one = wires.chip_rows(normed_own)
         mixed = dot(normed_one, qkv_here, ((1,), (0,)))
         own_keys = rope_turn(mixed[:, q_width : q_width + HEAD], turn, 1.0)
         own_pair = jnp.concatenate([own_keys, mixed[:, q_width + HEAD :]], axis=1).astype(bf16)
-        table = jnp.concatenate(
-            [wires.chips_on(own_pair, step) for step in range(depth, 0, -1)] + [own_pair], axis=0
-        )
+        keys = Task(wires.key_gather(own_pair, depth))
+        phase(keys)
+        table = keys.finish()
         attended, queries = attend_forward(mixed, table, bias, turn, valid)
         stream_mid = stream + wires.chip_sum(dot(attended, out_here, ((1,), (1,))))
         scale_two = norm_scale(stream_mid)
         normed_two = (stream_mid * scale_two * gain_rows[1]).astype(bf16)
+        sent = normed_two
+        if more:
+            gradient.go(sent, *gradient.marks)
+        else:
+            gradient.go(sent, *gradient.marks)
         if layer_index == 0:
-            blocks = wires.token_gather(jnp.concatenate([normed_two, route_names], axis=1))
+            sent = jnp.concatenate([sent, route_names], axis=1)
+        tokens = Task(wires.token_gather(sent))
+        phase(tokens)
+        phase(tokens)
+        blocks = tokens.finish()
+        if layer_index == 0:
             block_routes = [
                 block[:, model_width : model_width + routes.shape[1]].astype(jnp.int32)
                 for block in blocks
             ]
             blocks = [block[:, :model_width] for block in blocks]
-        else:
-            blocks = wires.token_gather(normed_two)
         block_gates, up_gates, block_outs = [], [], []
         for block, route_rows in zip(blocks, block_routes):
             gates = expert_gates(block, router, route_rows, expert_ids)[0]
             gate = jnp.sum(jnp.where(my_expert, gates, 0.0), axis=1, keepdims=True)
             up_gate = dot(block, gate_up_here, ((1,), (0,)))
-            hidden = (jax.nn.silu(up_gate[:, :ff_width]) * up_gate[:, ff_width:]).astype(bf16)
-            out = dot(hidden, down_here, ((1,), (0,)))
+            hidden = jax.nn.silu(up_gate[:, :ff_width]) * up_gate[:, ff_width:] * gate
             block_gates.append(gate)
             up_gates.append(up_gate)
-            block_outs.append((out * gate).astype(bf16))
+            block_outs.append(dot(hidden.astype(bf16), down_here, ((1,), (0,))).astype(bf16))
         stored.append(
             (
                 stream,
@@ -504,12 +629,28 @@
                 blocks,
                 block_gates,
                 up_gates,
+                gain_rows,
+                qkv_here,
+                out_here,
+                router,
             )
         )
-        stream = stream_mid + wires.token_scatter(block_outs)
-    layer_out = stream.astype(bf16)
+        outs = Task(wires.token_scatter(block_outs))
+        if more:
+            phase(outs)
+            phase(outs)
+            stream = stream_mid + outs.finish()
+    last_mid = stream_mid
     stream_grad = cotangent.astype(f32)
-    grad_layers = []
+    grad_layers = [None] * layer_count
+    held_sums = []
+
+    def shared(value):
+        rows = value.shape[0] // 2
+        value = value.reshape(2, rows, value.shape[1])
+        crossed = wires.to_core(place_of(value, 1 - core, 0).astype(bf16))
+        return place_of(value, core, 0), crossed.astype(f32)
+
     for layer_index in range(layer_count - 1, -1, -1):
         (
             stream,
@@ -524,48 +665,77 @@
             blocks,
             block_gates,
             up_gates,
+            gain_rows,
+            qkv_here,
+            out_here,
+            router,
         ) = stored[layer_index]
-        gain_rows, qkv_here, out_here, router = held_weights[layer_index]
-        gate_up_here = w_gate_up[layer_index, 0]
-        down_here = w_down[layer_index, 0]
-        grad_blocks = wires.token_gather(stream_grad.astype(bf16))
-        pair_grads, hiddens, in_grads, gate_grads = [], [], [], []
+        gate_up_here, down_here = w_gate_up[layer_index, 0], w_down[layer_index, 0]
+        last = layer_index + 1 == layer_count
+        if last:
+            grad_blocks = gradient.finish()
+        else:
+            gradient = Task(wires.token_gather(held_grad))
+            phase(gradient)
+            phase(gradient)
+            grad_blocks = gradient.finish()
+        in_grads, pair_grads, hiddens = [], [], []
         for grad_block, gate, up_gate in zip(grad_blocks, block_gates, up_gates):
+            back = dot(grad_block, down_here, ((1,), (1,)))
             gate_part = up_gate[:, :ff_width]
             up_part = up_gate[:, ff_width:]
             sigmoid_gate = jax.nn.sigmoid(gate_part)
             activated = gate_part * sigmoid_gate
             hidden = activated * up_part
-            back = dot(grad_block, down_here, ((1,), (1,)))
-            gate_grads.append(jnp.sum(hidden * back, axis=1))
+            gate_grad = jnp.sum(hidden * back, axis=1, keepdims=True)
+            high = gate_grad.astype(bf16).astype(f32)
+            tail = jnp.where(
+                lane == wires.dp_index,
+                high,
+                jnp.where(lane == wires.dp_index + 64, gate_grad - high, 0.0),
+            ).astype(bf16)
             hidden_grad = back * gate
             pair_grad = jnp.concatenate(
                 [
-                    hidden_grad * up_part * sigmoid_gate * (1.0 + gate_part * (1.0 - sigmoid_gate)),
+                    hidden_grad
+                    * up_part
+                    * sigmoid_gate
+                    * (1.0 + gate_part * (1.0 - sigmoid_gate)),
                     hidden_grad * activated,
                 ],
                 axis=1,
             ).astype(bf16)
             pair_grads.append(pair_grad)
             hiddens.append((hidden * gate).astype(bf16))
-            in_grads.append(dot(pair_grad, gate_up_here, ((1,), (1,))).astype(bf16))
-        gate_rows = jnp.zeros((wires.dp_count, tok_rows), f32)
-        for owners, gate_grad in zip(wires.token_owner(), gate_grads):
-            for place, owner in enumerate(owners):
-                gate_rows = lax.dynamic_update_slice(
-                    gate_rows, gate_grad[place * tok_rows :][None, :tok_rows], (owner, 0)
-                )
-        gate_rows = lax.all_to_all(gate_rows, "dp", split_axis=0, concat_axis=0, tiled=True)
-        normed_grad = wires.token_scatter(in_grads)
-        pair_all = jnp.concatenate(pair_grads, axis=0)
-        gate_up_grad = dot(jnp.concatenate(blocks, axis=0), pair_all, ((0,), (0,))).astype(bf16)
-        down_grad = dot(
-            jnp.concatenate(hiddens, axis=0), jnp.concatenate(grad_blocks, axis=0), ((0,), (0,))
-        ).astype(bf16)
-        gate_up_sum = wires.seq_scatter(gate_up_grad)
-        down_sum = wires.seq_scatter(down_grad)
+            in_grad = dot(pair_grad, gate_up_here, ((1,), (1,))).astype(bf16)
+            in_grads.append(jnp.concatenate([in_grad, tail], axis=1))
+        earlier = [outs] if last else []
+        in_grads = [after(block, *[m for task in earlier for m in task.marks]) for block in in_grads]
+        back_sums = Task(wires.token_scatter(in_grads))
+        phase(back_sums)
+        expert_grads = Task(
+            wires.expert_sums(
+                [
+                    (
+                        jnp.concatenate(blocks, axis=0),
+                        after(jnp.concatenate(pair_grads, axis=0), *in_grads),
+                    ),
+                    (
+                        after(jnp.concatenate(hiddens, axis=0), *in_grads),
+                        jnp.concatenate(grad_blocks, axis=0),
+                    ),
+                ]
+            )
+        )
+        phase(back_sums, expert_grads)
+        normed_grad = back_sums.finish()
+        for task in earlier:
+            task.go(normed_grad, *task.marks)
+        gate_rows = normed_grad[:, model_width:]
+        gate_rows = gate_rows[:, :expert_count] + gate_rows[:, 64 : 64 + expert_count]
+        normed_grad = normed_grad[:, :model_width]
         gates, named = expert_gates(normed_two, router, routes, expert_ids)
-        gate_grad = jnp.where(named, gate_rows.T, 0.0)
+        gate_grad = jnp.where(named, gate_rows, 0.0)
         logit_grad = gates * (gate_grad - jnp.sum(gates * gate_grad, axis=1, keepdims=True))
         logit_grad = logit_grad.astype(bf16)
         router_grad = dot(normed_two, logit_grad, ((0,), (0,)))
@@ -576,13 +746,19 @@
         head_grad = dot(attn_grad, out_here, ((1,), (0,))) * query_valid[:, None]
         head_grad = head_grad.astype(bf16)
         out_grad = dot(attn_grad, attended, ((0,), (0,))).astype(bf16)
+        background = earlier
+        if not last:
+            half = q_width // 2
+            out_sums = Task(wires.chip_scatter(out_grad[:, :half], out_grad[:, half:]))
+            background = [out_sums]
         query_lin, key_grad, value_grad = attend_backward(queries, head_grad, table, bias, turn)
-        pair_sums = jnp.concatenate([key_grad, value_grad], axis=1)
-        own_grad = pair_sums[depth * chip_tokens :]
-        for step in range(depth, 0, -1):
-            first = (depth - step) * chip_tokens
-            part = pair_sums[first : first + chip_tokens].astype(bf16)
-            own_grad = own_grad + wires.chips_on(part, -step).astype(f32)
+        events = [mark for task in background for mark in task.marks]
+        pair_sums = after(jnp.concatenate([key_grad, value_grad], axis=1), *events)
+        for task in background:
+            task.go(query_lin, *events)
+        key_sums = Task(wires.key_scatter(pair_sums, depth))
+        phase(key_sums, *([expert_grads] if last else [out_sums]))
+        own_grad = key_sums.finish()
         key_lin = rope_turn(own_grad[:, :HEAD], turn, -1.0)
         mixed_grad = jnp.concatenate(
             [query_lin, key_lin.astype(bf16), own_grad[:, HEAD:].astype(bf16)], axis=1
@@ -590,27 +766,28 @@
         normed_one_grad = wires.chip_sum(dot(mixed_grad, qkv_here, ((1,), (1,))))
         gain_one_grad, front_grad = norm_back(stream, scale_one, gain_rows[0], normed_one_grad)
         stream_grad = mid_grad + front_grad
-        qkv_grad = dot(normed_one, mixed_grad, ((0,), (0,))).astype(bf16)
+        query_lin_grad = dot(normed_one, query_lin, ((0,), (0,))).astype(bf16)
+        pair_lin_grad = dot(normed_one, mixed_grad[:, q_width:], ((0,), (0,))).astype(bf16)
         small = jnp.concatenate([router_grad, jnp.stack([gain_one_grad, gain_two_grad]).T], axis=1)
         small = jnp.pad(small, ((0, 0), (0, small_width - small.shape[1]))).astype(bf16)
-
-        def shared(value):
-            rows = value.shape[0] // 2
-            kept, sent = wires.picked(core, value.reshape(2, rows, value.shape[1]), 0)
-            return kept, wires.to_core(sent.astype(bf16)).astype(f32)
-
-        half = q_width // 2
-        if layer_index > 0:
-            front, back = wires.chip_scatter(jnp.concatenate([qkv_grad, small], axis=1), out_grad)
+        if last:
+            held_grad = after(stream_grad.astype(bf16), *outs.marks)
+            outs.finish()
+            front = jnp.concatenate([query_lin_grad, pair_lin_grad, small], axis=1)
+            total = wires.chip_scatter_whole(jnp.concatenate([front, out_grad], axis=1))
+            held_sums.append((layer_index, total, None, expert_grads))
         else:
-            back = jnp.concatenate(wires.chip_scatter(out_grad[:, :half], out_grad[:, half:]), axis=1)
-            cut = qkv_width // 2
-            front = jnp.concatenate(
-                wires.chip_scatter(
-                    qkv_grad[:, :cut], jnp.concatenate([qkv_grad[:, cut:], small], axis=1)
-                ),
-                axis=1,
+            front_sums = Task(
+                wires.chip_scatter(query_lin_grad, jnp.concatenate([pair_lin_grad, small], axis=1))
             )
+            held_sums.append((layer_index, front_sums, out_sums, expert_grads))
+    for layer_index, front_sums, out_sums, expert_grads in held_sums:
+        if out_sums is None:
+            front, back = front_sums[:, :front_width], front_sums[:, front_width:]
+        else:
+            front, back = front_sums.finish()
+            front = jnp.concatenate([front, back], axis=1)
+            back = jnp.concatenate(out_sums.finish(), axis=1)
         back_own, back_other = shared(back)
         front_own, front_other = shared(front)
         out_sum = wires.ordered(core, back_own, back_other, 1)
@@ -628,8 +805,16 @@
         )
         gain_sum = small_sum[:, expert_count : expert_count + 2].T
         router_sum = small_sum[:, :expert_count]
-        grad_layers.append((gain_sum, qkv_sum, out_sum, router_sum, gate_up_sum, down_sum))
-    grad_layers = grad_layers[::-1]
+        gate_up_sum, down_sum = expert_grads.finish()
+        grad_layers[layer_index] = (
+            gain_sum,
+            qkv_sum,
+            out_sum,
+            router_sum,
+            gate_up_sum,
+            down_sum,
+        )
+    layer_out = (last_mid + outs.finish()).astype(bf16)
     stacked = [jnp.stack([grad_entry[member] for grad_entry in grad_layers]) for member in range(6)]
     return (
         layer_out,

time: 1040 us -> 946 us (0.910)
  waiting for transfers between devices: 455 us -> 304 us
  between operations: 5.31 us -> 107 us
  starting transfers between devices: 228 us -> 175 us
  local copies, waits for them, and re-layouts: 77.9 us -> 101 us
  other arithmetic: 104 us -> 92.4 us
    ppermute x39 -> x33, waiting for transfers between devices: 227 us -> 140 us  [along(): lax.ppermute(value, 'dp', [(i, (i + 2 * steps) % count) for i in range(co...]
    ppermute x14 -> x10, waiting for transfers between devices: 79.6 us -> 8.4 us  [to_pair(): lax.ppermute(value, 'seq', [(i, i ^ 2) for i in range(self.seq_count)])]
    ppermute x39 -> x33, starting transfers between devices: 112 us -> 66.4 us  [along(): lax.ppermute(value, 'dp', [(i, (i + 2 * steps) % count) for i in range(co...]
    ppermute x34 -> x30, waiting for transfers between devices: 83.9 us -> 124 us  [to_side(): return lax.ppermute(value, 'dp', [(i, i ^ 1) for i in range(self.dp_count)])]
    slice x22 -> x76, local copies, waits for them, and re-layouts: 12.7 us -> 48.5 us  [the longest x67 46.1 us: after(): sample = lax.slice(event, (0,) * event.ndim, (1,) * event.ndim).reshape(())]
    ppermute x16, waiting for transfers between devices: 60.3 us -> 29 us  [chips_on(): lax.ppermute(value, ALL, [(i, i + offset) for i in range(first, last)])]
    convert_element_type x37 -> x30, other arithmetic: 32.4 us -> 8.8 us  [the longest x8 4.86 us: added(): return (kept + after(got, *events).astype(f32)).astype(bf16)]
    unnamed x472 -> x454, local copies, waits for them, and re-layouts: 35.2 us -> 29.1 us
  transfers between devices with their start and end apart: 125 -> 111, of which waited for: 57 -> 41; matrix products, arithmetic and copies ran while one was open for 25% -> 30% of each run, Pallas kernels for 3% -> 3%
where the time goes in v3:
time: 946 us; the launch traced here: 934 us
  waiting for transfers between devices  304 us (32%)
  starting transfers between devices  175 us (18%)
  matrix products  121 us (13%)
  between operations  107 us (11%)
  local copies, waits for them, and re-layouts  101 us (11%)
  other arithmetic  92.4 us (10%)
  Pallas kernels  32.2 us (3%)
    ppermute x33, waiting for transfers between devices, along(): lax.ppermute(value, 'dp', [(i, (i + 2 * steps) % count) for i in range(co...  140 us
    ppermute x30, waiting for transfers between devices, to_side(): return lax.ppermute(value, 'dp', [(i, i ^ 1) for i in range(self.dp_count)])  124 us
    dot_general x54, matrix products, dot(): lax.dot_general(left, right, (dims, ((), ())), preferred_element_type=f32)  121 us
    ppermute x33, starting transfers between devices, along(): lax.ppermute(value, 'dp', [(i, (i + 2 * steps) % count) for i in range(co...  66.4 us
    ppermute x16, starting transfers between devices, chips_on(): lax.ppermute(value, ALL, [(i, i + offset) for i in range(first, last)])  50.2 us
    slice x67, local copies, waits for them, and re-layouts, after(): sample = lax.slice(event, (0,) * event.ndim, (1,) * event.ndim).reshape(())  46.1 us
    ppermute x30, starting transfers between devices, to_side(): return lax.ppermute(value, 'dp', [(i, i ^ 1) for i in range(self.dp_count)])  41.2 us
    unnamed x454, local copies, waits for them, and re-layouts  29.1 us
  transfers between devices with their start and end apart: 111, of which 41 were waited for; matrix products, arithmetic and copies ran while one was open for 30% of the time, Pallas kernels for 3%

profile of v3, /device:TPU:0, one launch (start us, length us, event | category | flops | bytes accessed | tf_op | source)
XLA Modules:
  0.0 933.7 jit_solution(11422615657121634236)
XLA Ops:
  23.8 8.3 collective-permute-done.2
  33.0 13.7 %collective-permute-done.3 = bf16[96,1920]{1,0:T(8,128)(2,1)S(1)} collective-permute-done((bf16[96,1920]{1,0:T(8,128)(2,1)}, bf16[96,1920]{1,0:T(8,128)(2,1)S(1)}, u32[]{:S(2)}, u32[]{:S(2)}) %collective-permute-start.3) | collective-permute-done | bytes 368672 | tf_op jit(solution)/shard_map/ppermute | solution.py:105
  46.7 5.7 collective-permute-done.4
  55.1 10.8 %collective-permute-done.5 = bf16[4,96,896]{2,1,0:T(8,128)(2,1)S(1)} collective-permute-done((bf16[4,96,896]{2,1,0:T(8,128)(2,1)S(1)}, bf16[4,96,896]{2,1,0:T(8,128)(2,1)S(1)}, u32[]{:S(2)}, u32[]{:S(2)}) %collective-permute-start.5) | collective-permute-done | bytes 688160 | tf_op jit(solution)/shard_map/ppermute | solution.py:101
  72.8 26.5 %collective-permute-done.7 = bf16[4,2,96,1024]{3,2,1,0:T(8,128)(2,1)S(1)} collective-permute-done((bf16[4,2,96,1024]{3,2,1,0:T(8,128)(2,1)S(1)}, bf16[4,2,96,1024]{3,2,1,0:T(8,128)(2,1)S(1)}, u32[]{:S(2)}, u32[]{:S(2)}) %collective-permute-start.7) | collective-permute-done | bytes 1572896 | tf_op jit(solution)/shard_map/ppermute | solution.py:101
  104.1 10.2 %collective-permute-start.10 = (bf16[256,256]{1,0:T(8,128)(2,1)S(1)}, bf16[256,256]{1,0:T(8,128)(2,1)S(1)}, u32[]{:S(2)}, u32[]{:S(2)}) collective-permute-start(bf16[256,256]{1,0:T(8,128)(2,1)S(1)} %pad_maximum_fusion.45), channel_id=1, source_target_pairs={{0,8},{1,9},{2,10},{3,11},{4,12},{5,13},{6,14},{7,15},{8,16},{9,17... | collective-permute-start | bytes 393224 | tf_op jit(solution)/shard_map/ppermute | solution.py:111
  123.1 4.3 collective-permute-done.12
  127.6 6.7 attend_forward.2
  138.9 6.4 collective-permute-start.16
  158.2 6.4 collective-permute-done.17
  182.6 10.1 %collective-permute-done.18 = bf16[256,1664]{0,1:T(8,128)(2,1)S(1)} collective-permute-done((bf16[256,1664]{0,1:T(8,128)(2,1)S(1)}, bf16[256,1664]{0,1:T(8,128)(2,1)S(1)}, u32[]{:S(2)}, u32[]{:S(2)}) %collective-permute-start.18) | collective-permute-done | bytes 852000 | tf_op jit(solution)/shard_map/ppermute | solution.py:101
  198.9 4.7 fusion.20
  213.0 20.6 %collective-permute-done.19 = bf16[256,1536]{0,1:T(8,128)(2,1)S(1)} collective-permute-done((bf16[256,1536]{0,1:T(8,128)(2,1)S(1)}, bf16[256,1536]{0,1:T(8,128)(2,1)S(1)}, u32[]{:S(2)}, u32[]{:S(2)}) %collective-permute-start.19) | collective-permute-done | bytes 786464 | tf_op jit(solution)/shard_map/ppermute | solution.py:101
  235.9 7.0 collective-permute-start.21
  244.2 9.8 %collective-permute-done.24 = bf16[128,1536]{0,1:T(8,128)(2,1)S(1)} collective-permute-done((bf16[128,1536]{0,1:T(8,128)(2,1)S(1)}, bf16[128,1536]{0,1:T(8,128)(2,1)S(1)}, u32[]{:S(2)}, u32[]{:S(2)}) %collective-permute-start.24) | collective-permute-done | bytes 393248 | tf_op jit(solution)/shard_map/ppermute | solution.py:101
  269.5 19.0 %collective-permute-done.26 = bf16[128,1536]{0,1:T(8,128)(2,1)S(1)} collective-permute-done((bf16[128,1536]{0,1:T(8,128)(2,1)S(1)}, bf16[128,1536]{0,1:T(8,128)(2,1)S(1)}, u32[]{:S(2)}, u32[]{:S(2)}) %collective-permute-start.26) | collective-permute-done | bytes 393248 | tf_op jit(solution)/shard_map/ppermute | solution.py:105
  303.1 4.3 collective-permute-start.31
  307.4 12.2 %collective-permute-start.30 = (bf16[256,256]{1,0:T(8,128)(2,1)S(1)}, bf16[256,256]{1,0:T(8,128)(2,1)S(1)}, u32[]{:S(2)}, u32[]{:S(2)}) collective-permute-start(bf16[256,256]{1,0:T(8,128)(2,1)S(1)} %pad_maximum_fusion.46), channel_id=1, source_target_pairs={{0,8},{1,9},{2,10},{3,11},{4,12},{5,13},{6,14},{7,15},{8,16},{9,17... | collective-permute-start | bytes 393224 | tf_op jit(solution)/shard_map/ppermute | solution.py:111
  329.1 6.7 attend_forward.3
  348.1 5.6 collective-permute-start.37
  356.6 5.3 collective-permute-start.35
  368.9 15.0 %collective-permute-done.36 = bf16[128,1536]{0,1:T(8,128)(2,1)S(1)} collective-permute-done((bf16[128,1536]{0,1:T(8,128)(2,1)S(1)}, bf16[128,1536]{0,1:T(8,128)(2,1)S(1)}, u32[]{:S(2)}, u32[]{:S(2)}) %collective-permute-start.36) | collective-permute-done | bytes 393248 | tf_op jit(solution)/shard_map/ppermute | solution.py:105
  397.7 10.6 %collective-permute-done.38 = bf16[256,1536]{0,1:T(8,128)(2,1)S(1)} collective-permute-done((bf16[256,1536]{0,1:T(8,128)(2,1)S(1)}, bf16[256,1536]{0,1:T(8,128)(2,1)S(1)}, u32[]{:S(2)}, u32[]{:S(2)}) %collective-permute-start.38) | collective-permute-done | bytes 786464 | tf_op jit(solution)/shard_map/ppermute | solution.py:101
  410.3 4.8 fusion.8
  422.7 5.0 fusion.54
  438.0 4.0 fusion.67
  442.3 4.0 fusion.70
  458.6 6.9 convolution_convert_fusion.1
  519.5 9.4 %collective-permute-done.55 = bf16[128,1664]{0,1:T(8,128)(2,1)S(1)} collective-permute-done((bf16[128,1664]{0,1:T(8,128)(2,1)S(1)}, bf16[128,1664]{0,1:T(8,128)(2,1)S(1)}, u32[]{:S(2)}, u32[]{:S(2)}) %collective-permute-start.55) | collective-permute-done | bytes 426016 | tf_op jit(solution)/shard_map/ppermute | solution.py:105
  547.7 9.4 %attend_backward.2 = (bf16[256,768]{1,0:T(8,128)(2,1)S(1)}, f32[1280,128]{1,0:T(8,128)S(1)}, f32[1280,128]{1,0:T(8,128)S(1)}) custom-call(bf16[256,768]{1,0:T(8,128)(2,1)S(1)} %copy-done.11, bf16[256,768]{1,0:T(8,128)(2,1)S(1)} %fusion.155.head_grad, bf16[1280,256]{1,0:T(8,128)(2,1)S(1)} %constant_dynamic-update-slice_fusion.8.keys.values, ...), custom_call_target="tpu_custom_call" | custom-call | flops 2516582400 | bytes 2883584 | tf_op jit(solution)/shard_map/attend_backward/pallas_call | solution.py:436
  574.1 4.8 collective-permute-start.60
  578.9 4.7 collective-permute-start.61
  595.0 5.5 collective-permute-done.61
  614.3 7.8 collective-permute-done.67
  642.7 10.1 %collective-permute-done.70 = bf16[256,1536]{0,1:T(8,128)(2,1)S(1)} collective-permute-done((bf16[256,1536]{0,1:T(8,128)(2,1)S(1)}, bf16[256,1536]{0,1:T(8,128)(2,1)S(1)}, u32[]{:S(2)}, u32[]{:S(2)}) %collective-permute-start.70) | collective-permute-done | bytes 786464 | tf_op jit(solution)/shard_map/ppermute | solution.py:101
  664.5 4.3 collective-permute-done.75
  679.7 5.1 convolution_convert_fusion
  700.9 8.7 copy.275
  735.2 27.2 %collective-permute-done.80 = bf16[128,1664]{0,1:T(8,128)(2,1)S(1)} collective-permute-done((bf16[128,1664]{0,1:T(8,128)(2,1)S(1)}, bf16[128,1664]{0,1:T(8,128)(2,1)S(1)}, u32[]{:S(2)}, u32[]{:S(2)}) %collective-permute-start.80) | collective-permute-done | bytes 426016 | tf_op jit(solution)/shard_map/ppermute | solution.py:105
  772.5 4.3 collective-permute-start.82
  779.8 9.4 %attend_backward.3 = (bf16[256,768]{1,0:T(8,128)(2,1)S(1)}, f32[1280,128]{1,0:T(8,128)S(1)}, f32[1280,128]{1,0:T(8,128)S(1)}) custom-call(bf16[256,768]{1,0:T(8,128)(2,1)S(1)} %copy-done.9, bf16[256,768]{1,0:T(8,128)(2,1)S(1)} %fusion.158.head_grad, bf16[1280,256]{1,0:T(8,128)(2,1)S(1)} %copy-done.1, bf16[1280,256]{1,0:T(8,128)(2,1)S(1)} %copy-done.1, ...), custom_call_target="tpu_custom_call" | custom-call | flops 2516582400 | bytes 2883584 | tf_op jit(solution)/shard_map/attend_backward/pallas_call | solution.py:436
  812.8 20.3 %collective-permute-done.87 = bf16[256,256]{1,0:T(8,128)(2,1)S(1)} collective-permute-done((bf16[256,256]{1,0:T(8,128)(2,1)S(1)}, bf16[256,256]{1,0:T(8,128)(2,1)S(1)}, u32[]{:S(2)}, u32[]{:S(2)}) %collective-permute-start.87) | collective-permute-done | bytes 131104 | tf_op jit(solution)/shard_map/ppermute | solution.py:111
  858.5 4.9 maximum_bitcast_fusion
  863.4 8.6 collective-permute-done.101
  881.4 7.7 collective-permute-done.92
  890.9 4.2 collective-permute-done.91
  900.1 5.2 collective-permute-done.93
  905.4 12.3 %collective-permute-done.94 = bf16[96,1152]{1,0:T(8,128)(2,1)S(1)} collective-permute-done((bf16[96,1152]{1,0:T(8,128)(2,1)S(1)}, bf16[96,1152]{1,0:T(8,128)(2,1)S(1)}, u32[]{:S(2)}, u32[]{:S(2)}) %collective-permute-start.94) | collective-permute-done | bytes 221216 | tf_op jit(solution)/shard_map/ppermute | solution.py:105
  (1056 shorter events, 397.8 us)
Async XLA Ops:
  7.2 283.2 %all-gather.2.cloned.1.call-start = ((), (), s32[]{:S(2)}) async-start(), calls=%async_computation.1 | async-start | bytes 6266880 | tf_op jit(solution)/shard_map/all_gather | solution.py:223
  9.5 104.9 %collective-permute-start.28 = (bf16[48,768]{1,0:T(8,128)(2,1)}, bf16[48,768]{1,0:T(8,128)(2,1)}, u32[]{:S(2)}, u32[]{:S(2)}) collective-permute-start(bf16[48,768]{1,0:T(8,128)(2,1)} %broadcast_select_fusion.15), channel_id=1, source_target_pairs={{0,1},{1,0},{2,3},{3,2},{4,5},{5,4},{6,7},{7,6},{8,9},{9,8},{10,11... | collective-permute-start | bytes 221192 | tf_op jit(solution)/shard_map/ppermute | solution.py:95
  12.2 123.1 %collective-permute-start.27 = (bf16[48,1152]{1,0:T(8,128)(2,1)}, bf16[48,1152]{1,0:T(8,128)(2,1)}, u32[]{:S(2)}, u32[]{:S(2)}) collective-permute-start(bf16[48,1152]{1,0:T(8,128)(2,1)} %broadcast_select_fusion.11), channel_id=1, source_target_pairs={{0,1},{1,0},{2,3},{3,2},{4,5},{5,4},{6,7},{7,6},{8,9},{9,8},{10,11... | collective-permute-start | bytes 331784 | tf_op jit(solution)/shard_map/ppermute | solution.py:95
  13.2 134.1 %collective-permute-start.40 = (bf16[128,1536]{0,1:T(8,128)(2,1)}, bf16[128,1536]{0,1:T(8,128)(2,1)}, u32[]{:S(2)}, u32[]{:S(2)}) collective-permute-start(bf16[128,1536]{0,1:T(8,128)(2,1)} %copy.213), channel_id=1, source_target_pairs={{0,4},{4,0},{8,12},{12,8},{16,20},{20,16},{24,28},{28,24},{1,5},{5... | collective-permute-start | bytes 1179656 | tf_op jit(solution)/shard_map/ppermute | solution.py:101
  21.1 25.5 %collective-permute-start.3 = (bf16[96,1920]{1,0:T(8,128)(2,1)}, bf16[96,1920]{1,0:T(8,128)(2,1)S(1)}, u32[]{:S(2)}, u32[]{:S(2)}) collective-permute-start(bf16[96,1920]{1,0:T(8,128)(2,1)} %get-tuple-element.108), channel_id=1, source_target_pairs={{0,16},{4,20},{8,24},{12,28},{16,0},{20,4},{24,8},{28,12},{1,17},{... | collective-permute-start | bytes 1105928 | tf_op jit(solution)/shard_map/ppermute | solution.py:105
  32.1 20.4 %collective-permute-start.4 = (bf16[96,1920]{1,0:T(8,128)(2,1)}, bf16[96,1920]{1,0:T(8,128)(2,1)S(1)}, u32[]{:S(2)}, u32[]{:S(2)}) collective-permute-start(bf16[96,1920]{1,0:T(8,128)(2,1)} %get-tuple-element.108), channel_id=1, source_target_pairs={{0,24},{4,28},{8,0},{12,4},{16,8},{20,12},{24,16},{28,20},{1,25},{... | collective-permute-start | bytes 1105928 | tf_op jit(solution)/shard_map/ppermute | solution.py:105
  69.8 29.4 %collective-permute-start.7 = (bf16[4,2,96,1024]{3,2,1,0:T(8,128)(2,1)S(1)}, bf16[4,2,96,1024]{3,2,1,0:T(8,128)(2,1)S(1)}, u32[]{:S(2)}, u32[]{:S(2)}) collective-permute-start(bf16[4,2,96,1024]{3,2,1,0:T(8,128)(2,1)S(1)} %pad_maximum_fusion.4), channel_id=1, source_target_pairs={{0,4},{4,0},{8,12},{12,8},{16,20},{20,16},{24,28},{28,24},{1,5},{5... | collective-permute-start | bytes 4718600 | tf_op jit(solution)/shard_map/ppermute | solution.py:101
  72.3 28.7 %collective-permute-start.9 = (bf16[4,2,96,896]{3,2,1,0:T(8,128)(2,1)S(1)}, bf16[4,2,96,896]{3,2,1,0:T(8,128)(2,1)S(1)}, u32[]{:S(2)}, u32[]{:S(2)}) collective-permute-start(bf16[4,2,96,896]{3,2,1,0:T(8,128)(2,1)S(1)} %pad_maximum_fusion.5), channel_id=1, source_target_pairs={{0,2},{1,3},{2,0},{3,1},{4,6},{5,7},{6,4},{7,5},{8,10},{9,11},{10,... | collective-permute-start | bytes 4128776 | tf_op jit(solution)/shard_map/ppermute | solution.py:98
  145.4 21.7 %collective-permute-start.15 = (bf16[128,1664]{0,1:T(8,128)(2,1)}, bf16[128,1664]{0,1:T(8,128)(2,1)}, u32[]{:S(2)}, u32[]{:S(2)}) collective-permute-start(bf16[128,1664]{0,1:T(8,128)(2,1)} %pad_maximum_fusion.32), channel_id=1, source_target_pairs={{0,4},{4,0},{8,12},{12,8},{16,20},{20,16},{24,28},{28,24},{1,5},{5... | collective-permute-start | bytes 1277960 | tf_op jit(solution)/shard_map/ppermute | solution.py:101
  156.1 763.7 %reduce-scatter.4.cloned.1.call-start = ((), (), s32[]{:S(2)}) async-start(), calls=%async_computation.2 | async-start | bytes 6266880 | tf_op jit(solution)/shard_map/reduce_scatter | solution.py:228
  170.4 24.3 %collective-permute-start.22 = (bf16[128,1664]{0,1:T(8,128)(2,1)S(1)}, bf16[128,1664]{0,1:T(8,128)(2,1)S(1)}, u32[]{:S(2)}, u32[]{:S(2)}) collective-permute-start(bf16[128,1664]{0,1:T(8,128)(2,1)S(1)} %broadcast_select_fusion.2), channel_id=1, source_target_pairs={{0,16},{4,20},{8,24},{12,28},{16,0},{20,4},{24,8},{28,12},{1,17},{... | collective-permute-start | bytes 1277960 | tf_op jit(solution)/shard_map/ppermute | solution.py:105
  172.2 20.6 %collective-permute-start.18 = (bf16[256,1664]{0,1:T(8,128)(2,1)S(1)}, bf16[256,1664]{0,1:T(8,128)(2,1)S(1)}, u32[]{:S(2)}, u32[]{:S(2)}) collective-permute-start(bf16[256,1664]{0,1:T(8,128)(2,1)S(1)} %pad_maximum_fusion.9), channel_id=1, source_target_pairs={{0,4},{4,0},{8,12},{12,8},{16,20},{20,16},{24,28},{28,24},{1,5},{5... | collective-permute-start | bytes 2555912 | tf_op jit(solution)/shard_map/ppermute | solution.py:101
  206.9 26.8 %collective-permute-start.19 = (bf16[256,1536]{0,1:T(8,128)(2,1)S(1)}, bf16[256,1536]{0,1:T(8,128)(2,1)S(1)}, u32[]{:S(2)}, u32[]{:S(2)}) collective-permute-start(bf16[256,1536]{0,1:T(8,128)(2,1)S(1)} %slice.1067), channel_id=1, source_target_pairs={{0,4},{4,0},{8,12},{12,8},{16,20},{20,16},{24,28},{28,24},{1,5},{5... | collective-permute-start | bytes 2359304 | tf_op jit(solution)/shard_map/ppermute | solution.py:101
  261.2 27.4 %collective-permute-start.26 = (bf16[128,1536]{0,1:T(8,128)(2,1)S(1)}, bf16[128,1536]{0,1:T(8,128)(2,1)S(1)}, u32[]{:S(2)}, u32[]{:S(2)}) collective-permute-start(bf16[128,1536]{0,1:T(8,128)(2,1)S(1)} %fusion.259), channel_id=1, source_target_pairs={{0,16},{4,20},{8,24},{12,28},{16,0},{20,4},{24,8},{28,12},{1,17},{... | collective-permute-start | bytes 1179656 | tf_op jit(solution)/shard_map/ppermute | solution.py:105
  266.8 25.8 %collective-permute-start.42 = (bf16[128,1536]{0,1:T(8,128)(2,1)}, bf16[128,1536]{0,1:T(8,128)(2,1)}, u32[]{:S(2)}, u32[]{:S(2)}) collective-permute-start(bf16[128,1536]{0,1:T(8,128)(2,1)} %broadcast_select_fusion.10), channel_id=1, source_target_pairs={{0,24},{4,28},{8,0},{12,4},{16,8},{20,12},{24,16},{28,20},{1,25},{... | collective-permute-start | bytes 1179656 | tf_op jit(solution)/shard_map/ppermute | solution.py:105
  269.1 26.2 %collective-permute-start.41 = (bf16[128,1536]{0,1:T(8,128)(2,1)}, bf16[128,1536]{0,1:T(8,128)(2,1)}, u32[]{:S(2)}, u32[]{:S(2)}) collective-permute-start(bf16[128,1536]{0,1:T(8,128)(2,1)} %broadcast_select_fusion.10), channel_id=1, source_target_pairs={{0,8},{4,12},{8,16},{12,20},{16,24},{20,28},{24,0},{28,4},{1,9},{5... | collective-permute-start | bytes 1179656 | tf_op jit(solution)/shard_map/ppermute | solution.py:105
  303.1 23.0 %collective-permute-start.31 = (bf16[256,256]{1,0:T(8,128)(2,1)S(1)}, bf16[256,256]{1,0:T(8,128)(2,1)S(1)}, u32[]{:S(2)}, u32[]{:S(2)}) collective-permute-start(bf16[256,256]{1,0:T(8,128)(2,1)S(1)} %pad_maximum_fusion.46), channel_id=1, source_target_pairs={{0,6},{1,7},{2,8},{3,9},{4,10},{5,11},{6,12},{7,13},{8,14},{9,15},... | collective-permute-start | bytes 393224 | tf_op jit(solution)/shard_map/ppermute | solution.py:111
  353.6 30.3 %collective-permute-start.36 = (bf16[128,1536]{0,1:T(8,128)(2,1)S(1)}, bf16[128,1536]{0,1:T(8,128)(2,1)S(1)}, u32[]{:S(2)}, u32[]{:S(2)}) collective-permute-start(bf16[128,1536]{0,1:T(8,128)(2,1)S(1)} %get-tuple-element.94), channel_id=1, source_target_pairs={{0,8},{4,12},{8,16},{12,20},{16,24},{20,28},{24,0},{28,4},{1,9},{5... | collective-permute-start | bytes 1179656 | tf_op jit(solution)/shard_map/ppermute | solution.py:105
  356.6 29.2 %collective-permute-start.35 = (bf16[128,1536]{0,1:T(8,128)(2,1)S(1)}, bf16[128,1536]{0,1:T(8,128)(2,1)S(1)}, u32[]{:S(2)}, u32[]{:S(2)}) collective-permute-start(bf16[128,1536]{0,1:T(8,128)(2,1)S(1)} %get-tuple-element.94), channel_id=1, source_target_pairs={{0,4},{4,0},{8,12},{12,8},{16,20},{20,16},{24,28},{28,24},{1,5},{5... | collective-permute-start | bytes 1179656 | tf_op jit(solution)/shard_map/ppermute | solution.py:101
  364.5 29.1 %collective-permute-start.44 = (bf16[256,1536]{0,1:T(8,128)(2,1)S(1)}, bf16[256,1536]{0,1:T(8,128)(2,1)S(1)}, u32[]{:S(2)}, u32[]{:S(2)}) collective-permute-start(bf16[256,1536]{0,1:T(8,128)(2,1)S(1)} %get-tuple-element.90), channel_id=1, source_target_pairs={{0,4},{4,0},{8,12},{12,8},{16,20},{20,16},{24,28},{28,24},{1,5},{5... | collective-permute-start | bytes 2359304 | tf_op jit(solution)/shard_map/ppermute | solution.py:101
  387.6 29.1 %collective-permute-start.49 = (bf16[128,1536]{0,1:T(8,128)(2,1)S(1)}, bf16[128,1536]{0,1:T(8,128)(2,1)S(1)}, u32[]{:S(2)}, u32[]{:S(2)}) collective-permute-start(bf16[128,1536]{0,1:T(8,128)(2,1)S(1)} %broadcast_select_fusion.6), channel_id=1, source_target_pairs={{0,16},{4,20},{8,24},{12,28},{16,0},{20,4},{24,8},{28,12},{1,17},{... | collective-permute-start | bytes 1179656 | tf_op jit(solution)/shard_map/ppermute | solution.py:105
  387.8 20.5 %collective-permute-start.38 = (bf16[256,1536]{0,1:T(8,128)(2,1)S(1)}, bf16[256,1536]{0,1:T(8,128)(2,1)S(1)}, u32[]{:S(2)}, u32[]{:S(2)}) collective-permute-start(bf16[256,1536]{0,1:T(8,128)(2,1)S(1)} %pad_maximum_fusion.13), channel_id=1, source_target_pairs={{0,4},{4,0},{8,12},{12,8},{16,20},{20,16},{24,28},{28,24},{1,5},{5... | collective-permute-start | bytes 2359304 | tf_op jit(solution)/shard_map/ppermute | solution.py:101
  395.7 32.2 %collective-permute-start.48 = (bf16[128,1536]{0,1:T(8,128)(2,1)S(1)}, bf16[128,1536]{0,1:T(8,128)(2,1)S(1)}, u32[]{:S(2)}, u32[]{:S(2)}) collective-permute-start(bf16[128,1536]{0,1:T(8,128)(2,1)S(1)} %get-tuple-element.88), channel_id=1, source_target_pairs={{0,4},{4,0},{8,12},{12,8},{16,20},{20,16},{24,28},{28,24},{1,5},{5... | collective-permute-start | bytes 1179656 | tf_op jit(solution)/shard_map/ppermute | solution.py:101
  420.7 25.6 %collective-permute-start.39 = (bf16[256,1536]{0,1:T(8,128)(2,1)S(1)}, bf16[256,1536]{0,1:T(8,128)(2,1)S(1)}, u32[]{:S(2)}, u32[]{:S(2)}) collective-permute-start(bf16[256,1536]{0,1:T(8,128)(2,1)S(1)} %slice.1111), channel_id=1, source_target_pairs={{0,4},{4,0},{8,12},{12,8},{16,20},{20,16},{24,28},{28,24},{1,5},{5... | collective-permute-start | bytes 2359304 | tf_op jit(solution)/shard_map/ppermute | solution.py:101
  453.4 27.0 %collective-permute-start.58 = (bf16[128,1536]{0,1:T(8,128)(2,1)S(1)}, bf16[128,1536]{0,1:T(8,128)(2,1)S(1)}, u32[]{:S(2)}, u32[]{:S(2)}) collective-permute-start(bf16[128,1536]{0,1:T(8,128)(2,1)S(1)} %get-tuple-element.157), channel_id=1, source_target_pairs={{0,8},{4,12},{8,16},{12,20},{16,24},{20,28},{24,0},{28,4},{1,9},{5... | collective-permute-start | bytes 1179656 | tf_op jit(solution)/shard_map/ppermute | solution.py:105
  455.9 25.2 %collective-permute-start.57 = (bf16[128,1536]{0,1:T(8,128)(2,1)S(1)}, bf16[128,1536]{0,1:T(8,128)(2,1)S(1)}, u32[]{:S(2)}, u32[]{:S(2)}) collective-permute-start(bf16[128,1536]{0,1:T(8,128)(2,1)S(1)} %get-tuple-element.158), channel_id=1, source_target_pairs={{0,24},{4,28},{8,0},{12,4},{16,8},{20,12},{24,16},{28,20},{1,25},{... | collective-permute-start | bytes 1179656 | tf_op jit(solution)/shard_map/ppermute | solution.py:105
  468.4 34.8 %collective-permute-start.52 = (bf16[2,384,1536]{2,1,0:T(8,128)(2,1)}, bf16[2,384,1536]{2,1,0:T(8,128)(2,1)}, u32[]{:S(2)}, u32[]{:S(2)}) collective-permute-start(bf16[2,384,1536]{2,1,0:T(8,128)(2,1)} %dynamic-slice_bitcast_fusion.1), channel_id=1, source_target_pairs={{0,1},{1,0},{2,3},{3,2},{4,5},{5,4},{6,7},{7,6},{8,9},{9,8},{10,11... | collective-permute-start | bytes 7077896 | tf_op jit(solution)/shard_map/ppermute | solution.py:95
  508.4 20.6 %collective-permute-start.55 = (bf16[128,1664]{0,1:T(8,128)(2,1)S(1)}, bf16[128,1664]{0,1:T(8,128)(2,1)S(1)}, u32[]{:S(2)}, u32[]{:S(2)}) collective-permute-start(bf16[128,1664]{0,1:T(8,128)(2,1)S(1)} %fusion.253), channel_id=1, source_target_pairs={{0,16},{4,20},{8,24},{12,28},{16,0},{20,4},{24,8},{28,12},{1,17},{... | collective-permute-start | bytes 1277960 | tf_op jit(solution)/shard_map/ppermute | solution.py:105
  514.4 27.9 %collective-permute-start.108 = (bf16[192,1536]{1,0:T(8,128)(2,1)}, bf16[192,1536]{1,0:T(8,128)(2,1)}, u32[]{:S(2)}, u32[]{:S(2)}) collective-permute-start(bf16[192,1536]{1,0:T(8,128)(2,1)} %fusion.235), channel_id=1, source_target_pairs={{0,2},{1,3},{2,0},{3,1},{4,6},{5,7},{6,4},{7,5},{8,10},{9,11},{10,... | collective-permute-start | bytes 1769480 | tf_op jit(solution)/shard_map/ppermute | solution.py:98
  519.3 69.9 %collective-permute-start.106 = (bf16[384,1536]{1,0:T(8,128)(2,1)}, bf16[384,1536]{1,0:T(8,128)(2,1)}, u32[]{:S(2)}, u32[]{:S(2)}) collective-permute-start(bf16[384,1536]{1,0:T(8,128)(2,1)} %fusion.162), channel_id=1, source_target_pairs={{0,2},{1,3},{2,0},{3,1},{4,6},{5,7},{6,4},{7,5},{8,10},{9,11},{10,... | collective-permute-start | bytes 3538952 | tf_op jit(solution)/shard_map/ppermute | solution.py:98
  539.0 20.8 %collective-permute-start.59 = (bf16[128,1536]{0,1:T(8,128)(2,1)}, bf16[128,1536]{0,1:T(8,128)(2,1)}, u32[]{:S(2)}, u32[]{:S(2)}) collective-permute-start(bf16[128,1536]{0,1:T(8,128)(2,1)} %slice_select_fusion.3), channel_id=1, source_target_pairs={{0,4},{4,0},{8,12},{12,8},{16,20},{20,16},{24,28},{28,24},{1,5},{5... | collective-permute-start | bytes 1179656 | tf_op jit(solution)/shard_map/ppermute | solution.py:101
  578.9 21.5 %collective-permute-start.61 = (bf16[128,1536]{0,1:T(8,128)(2,1)S(1)}, bf16[128,1536]{0,1:T(8,128)(2,1)S(1)}, u32[]{:S(2)}, u32[]{:S(2)}) collective-permute-start(bf16[128,1536]{0,1:T(8,128)(2,1)S(1)} %fusion.260), channel_id=1, source_target_pairs={{0,16},{4,20},{8,24},{12,28},{16,0},{20,4},{24,8},{28,12},{1,17},{... | collective-permute-start | bytes 1179656 | tf_op jit(solution)/shard_map/ppermute | solution.py:105
  632.4 24.9 %collective-permute-start.74 = (bf16[128,1536]{0,1:T(8,128)(2,1)S(1)}, bf16[128,1536]{0,1:T(8,128)(2,1)S(1)}, u32[]{:S(2)}, u32[]{:S(2)}) collective-permute-start(bf16[128,1536]{0,1:T(8,128)(2,1)S(1)} %broadcast_select_fusion.4), channel_id=1, source_target_pairs={{0,16},{4,20},{8,24},{12,28},{16,0},{20,4},{24,8},{28,12},{1,17},{... | collective-permute-start | bytes 1179656 | tf_op jit(solution)/shard_map/ppermute | solution.py:105
  664.0 23.8 %collective-permute-start.71 = (bf16[256,1664]{0,1:T(8,128)(2,1)S(1)}, bf16[256,1664]{0,1:T(8,128)(2,1)S(1)}, u32[]{:S(2)}, u32[]{:S(2)}) collective-permute-start(bf16[256,1664]{0,1:T(8,128)(2,1)S(1)} %pad_maximum_fusion.7), channel_id=1, source_target_pairs={{0,4},{4,0},{8,12},{12,8},{16,20},{20,16},{24,28},{28,24},{1,5},{5... | collective-permute-start | bytes 2555912 | tf_op jit(solution)/shard_map/ppermute | solution.py:101
  678.6 39.2 %collective-permute-start.78 = (bf16[2,192,1536]{2,1,0:T(8,128)(2,1)}, bf16[2,192,1536]{2,1,0:T(8,128)(2,1)}, u32[]{:S(2)}, u32[]{:S(2)}) collective-permute-start(bf16[2,192,1536]{2,1,0:T(8,128)(2,1)} %dynamic-slice_bitcast_fusion.2), channel_id=1, source_target_pairs={{0,1},{1,0},{2,3},{3,2},{4,5},{5,4},{6,7},{7,6},{8,9},{9,8},{10,11... | collective-permute-start | bytes 3538952 | tf_op jit(solution)/shard_map/ppermute | solution.py:95
  687.7 32.6 %collective-permute-start.77 = (bf16[2,384,1536]{2,1,0:T(8,128)(2,1)}, bf16[2,384,1536]{2,1,0:T(8,128)(2,1)}, u32[]{:S(2)}, u32[]{:S(2)}) collective-permute-start(bf16[2,384,1536]{2,1,0:T(8,128)(2,1)} %dynamic-slice_bitcast_fusion), channel_id=1, source_target_pairs={{0,1},{1,0},{2,3},{3,2},{4,5},{5,4},{6,7},{7,6},{8,9},{9,8},{10,11... | collective-permute-start | bytes 7077896 | tf_op jit(solution)/shard_map/ppermute | solution.py:95
  693.9 21.4 %collective-permute-start.72 = (bf16[128,1664]{0,1:T(8,128)(2,1)}, bf16[128,1664]{0,1:T(8,128)(2,1)}, u32[]{:S(2)}, u32[]{:S(2)}) collective-permute-start(bf16[128,1664]{0,1:T(8,128)(2,1)} %get-tuple-element.154), channel_id=1, source_target_pairs={{0,24},{4,28},{8,0},{12,4},{16,8},{20,12},{24,16},{28,20},{1,25},{... | collective-permute-start | bytes 1277960 | tf_op jit(solution)/shard_map/ppermute | solution.py:105
  724.6 37.8 %collective-permute-start.80 = (bf16[128,1664]{0,1:T(8,128)(2,1)S(1)}, bf16[128,1664]{0,1:T(8,128)(2,1)S(1)}, u32[]{:S(2)}, u32[]{:S(2)}) collective-permute-start(bf16[128,1664]{0,1:T(8,128)(2,1)S(1)} %fusion.254), channel_id=1, source_target_pairs={{0,16},{4,20},{8,24},{12,28},{16,0},{20,4},{24,8},{28,12},{1,17},{... | collective-permute-start | bytes 1277960 | tf_op jit(solution)/shard_map/ppermute | solution.py:105
  728.4 38.0 %collective-permute-start.107 = (bf16[192,1536]{1,0:T(8,128)(2,1)S(1)}, bf16[192,1536]{1,0:T(8,128)(2,1)S(1)}, u32[]{:S(2)}, u32[]{:S(2)}) collective-permute-start(bf16[192,1536]{1,0:T(8,128)(2,1)S(1)} %fusion.234), channel_id=1, source_target_pairs={{0,2},{1,3},{2,0},{3,1},{4,6},{5,7},{6,4},{7,5},{8,10},{9,11},{10,... | collective-permute-start | bytes 1769480 | tf_op jit(solution)/shard_map/ppermute | solution.py:98
  733.7 60.6 %collective-permute-start.105 = (bf16[384,1536]{1,0:T(8,128)(2,1)S(1)}, bf16[384,1536]{1,0:T(8,128)(2,1)S(1)}, u32[]{:S(2)}, u32[]{:S(2)}) collective-permute-start(bf16[384,1536]{1,0:T(8,128)(2,1)S(1)} %fusion.161), channel_id=1, source_target_pairs={{0,2},{1,3},{2,0},{3,1},{4,6},{5,7},{6,4},{7,5},{8,10},{9,11},{10,... | collective-permute-start | bytes 3538952 | tf_op jit(solution)/shard_map/ppermute | solution.py:98
  772.5 25.2 %collective-permute-start.82 = (bf16[4,2,96,384]{3,2,0,1:T(8,128)(2,1)S(1)}, bf16[4,2,96,384]{3,2,0,1:T(8,128)(2,1)S(1)}, u32[]{:S(2)}, u32[]{:S(2)}) collective-permute-start(bf16[4,2,96,384]{3,2,0,1:T(8,128)(2,1)S(1)} %bitcast.530), channel_id=1, source_target_pairs={{0,2},{1,3},{2,0},{3,1},{4,6},{5,7},{6,4},{7,5},{8,10},{9,11},{10,... | collective-permute-start | bytes 1769480 | tf_op jit(solution)/shard_map/ppermute | solution.py:98
  776.9 22.7 %collective-permute-start.83 = (bf16[4,2,96,384]{3,2,0,1:T(8,128)(2,1)S(1)}, bf16[4,2,96,384]{3,2,0,1:T(8,128)(2,1)S(1)}, u32[]{:S(2)}, u32[]{:S(2)}) collective-permute-start(bf16[4,2,96,384]{3,2,0,1:T(8,128)(2,1)S(1)} %bitcast.529), channel_id=1, source_target_pairs={{0,4},{4,0},{8,12},{12,8},{16,20},{20,16},{24,28},{28,24},{1,5},{5... | collective-permute-start | bytes 1769480 | tf_op jit(solution)/shard_map/ppermute | solution.py:101
  794.2 79.1 %collective-permute-start.89 = (bf16[4,2,96,768]{3,2,0,1:T(8,128)(2,1)}, bf16[4,2,96,768]{3,2,0,1:T(8,128)(2,1)}, u32[]{:S(2)}, u32[]{:S(2)}) collective-permute-start(bf16[4,2,96,768]{3,2,0,1:T(8,128)(2,1)} %bitcast.476), channel_id=1, source_target_pairs={{0,2},{1,3},{2,0},{3,1},{4,6},{5,7},{6,4},{7,5},{8,10},{9,11},{10,... | collective-permute-start | bytes 3538952 | tf_op jit(solution)/shard_map/ppermute | solution.py:98
  803.4 29.6 %collective-permute-start.87 = (bf16[256,256]{1,0:T(8,128)(2,1)S(1)}, bf16[256,256]{1,0:T(8,128)(2,1)S(1)}, u32[]{:S(2)}, u32[]{:S(2)}) collective-permute-start(bf16[256,256]{1,0:T(8,128)(2,1)S(1)} %get-tuple-element.164), channel_id=1, source_target_pairs={{2,0},{3,1},{4,2},{5,3},{6,4},{7,5},{8,6},{9,7},{10,8},{11,9},{12,... | collective-permute-start | bytes 393224 | tf_op jit(solution)/shard_map/ppermute | solution.py:111
  804.7 30.2 %collective-permute-start.86 = (bf16[256,256]{1,0:T(8,128)(2,1)S(1)}, bf16[256,256]{1,0:T(8,128)(2,1)S(1)}, u32[]{:S(2)}, u32[]{:S(2)}) collective-permute-start(bf16[256,256]{1,0:T(8,128)(2,1)S(1)} %get-tuple-element.165), channel_id=1, source_target_pairs={{4,0},{5,1},{6,2},{7,3},{8,4},{9,5},{10,6},{11,7},{12,8},{13,9},{1... | collective-permute-start | bytes 393224 | tf_op jit(solution)/shard_map/ppermute | solution.py:111
  806.0 30.7 %collective-permute-start.85 = (bf16[256,256]{1,0:T(8,128)(2,1)S(1)}, bf16[256,256]{1,0:T(8,128)(2,1)S(1)}, u32[]{:S(2)}, u32[]{:S(2)}) collective-permute-start(bf16[256,256]{1,0:T(8,128)(2,1)S(1)} %get-tuple-element.166), channel_id=1, source_target_pairs={{6,0},{7,1},{8,2},{9,3},{10,4},{11,5},{12,6},{13,7},{14,8},{15,9},... | collective-permute-start | bytes 393224 | tf_op jit(solution)/shard_map/ppermute | solution.py:111
  809.6 33.6 %collective-permute-start.99 = (bf16[4,96,384]{2,1,0:T(8,128)(2,1)S(1)}, bf16[4,96,384]{2,1,0:T(8,128)(2,1)S(1)}, u32[]{:S(2)}, u32[]{:S(2)}) collective-permute-start(bf16[4,96,384]{2,1,0:T(8,128)(2,1)S(1)} %dynamic-slice_bitcast_fusion.5), channel_id=1, source_target_pairs={{0,2},{1,3},{2,0},{3,1},{4,6},{5,7},{6,4},{7,5},{8,10},{9,11},{10,... | collective-permute-start | bytes 884744 | tf_op jit(solution)/shard_map/ppermute | solution.py:98
  897.4 20.2 %collective-permute-start.94 = (bf16[96,1152]{1,0:T(8,128)(2,1)S(1)}, bf16[96,1152]{1,0:T(8,128)(2,1)S(1)}, u32[]{:S(2)}, u32[]{:S(2)}) collective-permute-start(bf16[96,1152]{1,0:T(8,128)(2,1)S(1)} %get-tuple-element.151), channel_id=1, source_target_pairs={{0,16},{4,20},{8,24},{12,28},{16,0},{20,4},{24,8},{28,12},{1,17},{... | collective-permute-start | bytes 663560 | tf_op jit(solution)/shard_map/ppermute | solution.py:105
  (278 other events, 4422.8 us)
Sparse Core Ops, SparseCore 0:
  156.2 125.6 all-gather.1
  709.8 177.3 reduce-scatter.3

commit v4 on v3

--- a/solution.py
+++ b/solution.py
@@ -30,14 +30,17 @@
 
 
 def after(value, *events):
-    there = None
+    total = None
     for event in events:
         if event is None:
             continue
-        sample = lax.slice(event, (0,) * event.ndim, (1,) * event.ndim).reshape(())
-        same = sample == sample
-        there = same if there is None else there & same
-    return value if there is None else jnp.where(there, value, jnp.zeros_like(value))
+        sample = lax.slice(event, (0,) * event.ndim, (1,) * event.ndim).reshape(1, 1)
+        sample = sample.astype(f32)
+        total = sample if total is None else total + sample
+    if total is None:
+        return value
+    there = jnp.broadcast_to((total == total).reshape((1,) * value.ndim), value.shape)
+    return jnp.where(there, value, jnp.zeros_like(value))
 
 
 class Task:
@@ -754,11 +757,11 @@
         query_lin, key_grad, value_grad = attend_backward(queries, head_grad, table, bias, turn)
         events = [mark for task in background for mark in task.marks]
         pair_sums = after(jnp.concatenate([key_grad, value_grad], axis=1), *events)
+        key_sums = Task(wires.key_scatter(pair_sums, depth))
+        phase(key_sums, *([expert_grads] if last else []))
+        own_grad = key_sums.finish()
         for task in background:
-            task.go(query_lin, *events)
-        key_sums = Task(wires.key_scatter(pair_sums, depth))
-        phase(key_sums, *([expert_grads] if last else [out_sums]))
-        own_grad = key_sums.finish()
+            task.go(own_grad, *events)
         key_lin = rope_turn(own_grad[:, :HEAD], turn, -1.0)
         mixed_grad = jnp.concatenate(
             [query_lin, key_lin.astype(bf16), own_grad[:, HEAD:].astype(bf16)], axis=1

time: 946 us -> 929 us (0.982)
  waiting for transfers between devices: 304 us -> 360 us
  between operations: 107 us -> 69.7 us
  other arithmetic: 92.4 us -> 72.6 us
  starting transfers between devices: 175 us -> 163 us
    ppermute x33, waiting for transfers between devices: 140 us -> 175 us  [along(): lax.ppermute(value, 'dp', [(i, (i + 2 * steps) % count) for i in range(co...]
    ppermute x30, waiting for transfers between devices: 124 us -> 139 us  [to_side(): return lax.ppermute(value, 'dp', [(i, i ^ 1) for i in range(self.dp_count)])]
    select_n x26, other arithmetic: 22.5 us -> 8.72 us  [after(): return jnp.where(there, value, jnp.zeros_like(value))]
    ppermute x16, starting transfers between devices: 50.2 us -> 38.6 us  [chips_on(): lax.ppermute(value, ALL, [(i, i + offset) for i in range(first, last)])]
    slice x67 -> x63, local copies, waits for them, and re-layouts: 46.1 us -> 41.5 us  [after(): lax.slice(event, (0,) * event.ndim, (1,) * event.ndim).reshape(1, 1)]
    unnamed x454 -> x350, local copies, waits for them, and re-layouts: 29.1 us -> 28.8 us
  transfers between devices with their start and end apart: 111 -> 111, of which waited for: 41 -> 50; matrix products, arithmetic and copies ran while one was open for 30% -> 29% of each run, Pallas kernels for 3% -> 4%
where the time goes in v4:
time: 929 us; the launch traced here: 918 us
  waiting for transfers between devices  360 us (39%)
  starting transfers between devices  163 us (18%)
  matrix products  128 us (14%)
  local copies, waits for them, and re-layouts  91.7 us (10%)
  other arithmetic  72.6 us (8%)
  between operations  69.7 us (8%)
  Pallas kernels  32.5 us (3%)
    ppermute x33, waiting for transfers between devices, along(): lax.ppermute(value, 'dp', [(i, (i + 2 * steps) % count) for i in range(co...  175 us
    ppermute x30, waiting for transfers between devices, to_side(): return lax.ppermute(value, 'dp', [(i, i ^ 1) for i in range(self.dp_count)])  139 us
    dot_general x54, matrix products, dot(): lax.dot_general(left, right, (dims, ((), ())), preferred_element_type=f32)  128 us
    ppermute x33, starting transfers between devices, along(): lax.ppermute(value, 'dp', [(i, (i + 2 * steps) % count) for i in range(co...  73.4 us
    slice x63, local copies, waits for them, and re-layouts, after(): lax.slice(event, (0,) * event.ndim, (1,) * event.ndim).reshape(1, 1)  41.5 us
    ppermute x16, starting transfers between devices, chips_on(): lax.ppermute(value, ALL, [(i, i + offset) for i in range(first, last)])  38.6 us
    ppermute x30, starting transfers between devices, to_side(): return lax.ppermute(value, 'dp', [(i, i ^ 1) for i in range(self.dp_count)])  38 us
    ppermute x16, waiting for transfers between devices, chips_on(): lax.ppermute(value, ALL, [(i, i + offset) for i in range(first, last)])  33.2 us
  transfers between devices with their start and end apart: 111, of which 50 were waited for; matrix products, arithmetic and copies ran while one was open for 29% of the time, Pallas kernels for 4%

profile of v4, /device:TPU:0, one launch (start us, length us, event | category | flops | bytes accessed | tf_op | source)
XLA Modules:
  0.0 917.9 jit_solution(13651765533548084305)
XLA Ops:
  21.5 8.2 collective-permute-done.2
  30.6 13.7 %collective-permute-done.3 = bf16[96,1920]{1,0:T(8,128)(2,1)S(1)} collective-permute-done((bf16[96,1920]{1,0:T(8,128)(2,1)S(1)}, bf16[96,1920]{1,0:T(8,128)(2,1)S(1)}, u32[]{:S(2)}, u32[]{:S(2)}) %collective-permute-start.3) | collective-permute-done | bytes 368672 | tf_op jit(solution)/shard_map/ppermute | solution.py:108
  44.3 5.4 collective-permute-done.4
  52.8 12.1 %collective-permute-done.5 = bf16[4,96,896]{2,1,0:T(8,128)(2,1)S(1)} collective-permute-done((bf16[4,96,896]{2,1,0:T(8,128)(2,1)S(1)}, bf16[4,96,896]{2,1,0:T(8,128)(2,1)S(1)}, u32[]{:S(2)}, u32[]{:S(2)}) %collective-permute-start.5) | collective-permute-done | bytes 688160 | tf_op jit(solution)/shard_map/ppermute | solution.py:104
  70.0 27.3 %collective-permute-done.7 = bf16[4,2,96,1024]{3,2,1,0:T(8,128)(2,1)S(1)} collective-permute-done((bf16[4,2,96,1024]{3,2,1,0:T(8,128)(2,1)S(1)}, bf16[4,2,96,1024]{3,2,1,0:T(8,128)(2,1)S(1)}, u32[]{:S(2)}, u32[]{:S(2)}) %collective-permute-start.7) | collective-permute-done | bytes 1572896 | tf_op jit(solution)/shard_map/ppermute | solution.py:104
  102.5 8.8 collective-permute-start.10
  125.3 6.7 attend_forward.2
  136.6 5.8 collective-permute-start.16
  157.5 5.8 collective-permute-done.17
  166.8 7.5 collective-permute-start.22
  182.5 4.9 fusion.22
  199.3 5.0 fusion.20
  220.1 22.8 %collective-permute-done.19 = bf16[256,1536]{1,0:T(8,128)(2,1)} collective-permute-done((bf16[256,1536]{1,0:T(8,128)(2,1)}, bf16[256,1536]{1,0:T(8,128)(2,1)}, u32[]{:S(2)}, u32[]{:S(2)}) %collective-permute-start.19) | collective-permute-done | bytes 786464 | tf_op jit(solution)/shard_map/ppermute | solution.py:104
  247.9 6.3 collective-permute-start.21
  255.3 12.4 %collective-permute-done.21 = bf16[128,1536]{1,0:T(8,128)(2,1)S(1)} collective-permute-done((bf16[128,1536]{1,0:T(8,128)(2,1)S(1)}, bf16[128,1536]{1,0:T(8,128)(2,1)S(1)}, u32[]{:S(2)}, u32[]{:S(2)}) %collective-permute-start.21) | collective-permute-done | bytes 393248 | tf_op jit(solution)/shard_map/ppermute | solution.py:108
  268.1 6.8 collective-permute-done.20
  286.3 18.8 %collective-permute-done.26 = bf16[128,1536]{1,0:T(8,128)(2,1)S(1)} collective-permute-done((bf16[128,1536]{1,0:T(8,128)(2,1)S(1)}, bf16[128,1536]{1,0:T(8,128)(2,1)S(1)}, u32[]{:S(2)}, u32[]{:S(2)}) %collective-permute-start.26) | collective-permute-done | bytes 393248 | tf_op jit(solution)/shard_map/ppermute | solution.py:108
  335.7 6.7 attend_forward.3
  361.0 5.0 collective-permute-start.37
  368.7 6.1 collective-permute-start.35
  379.3 17.7 %collective-permute-done.36 = bf16[128,1536]{1,0:T(8,128)(2,1)} collective-permute-done((bf16[128,1536]{1,0:T(8,128)(2,1)}, bf16[128,1536]{1,0:T(8,128)(2,1)}, u32[]{:S(2)}, u32[]{:S(2)}) %collective-permute-start.36) | collective-permute-done | bytes 393248 | tf_op jit(solution)/shard_map/ppermute | solution.py:108
  417.8 6.6 collective-permute-done.38
  426.3 13.2 %fusion.8 = f32[512,1536]{1,0:T(8,128)S(1)} fusion(bf16[512,1536]{1,0:T(8,128)(2,1)S(1)} %get-tuple-element.185, bf16[2,1,1536,1536]{3,2,1,0:T(8,128)(2,1)} %param.18), kind=kOutput, calls=%fused_computation.12 | convolution fusion | flops 2415919104 | bytes 9437184 | tf_op jit(solution)/shard_map/dot_general | solution.py:29
  447.0 5.0 fusion.54
  464.5 4.9 fusion.70
  479.6 7.8 convolution_convert_fusion.1
  491.6 5.1 collective-permute-done.47
  527.4 5.1 collective-permute-done.56
  532.6 10.2 %collective-permute-done.57 = bf16[128,1664]{1,0:T(8,128)(2,1)S(1)} collective-permute-done((bf16[128,1664]{1,0:T(8,128)(2,1)S(1)}, bf16[128,1664]{1,0:T(8,128)(2,1)S(1)}, u32[]{:S(2)}, u32[]{:S(2)}) %collective-permute-start.57) | collective-permute-done | bytes 426016 | tf_op jit(solution)/shard_map/ppermute | solution.py:108
  550.9 5.3 collective-permute-done.58
  558.2 9.4 %attend_backward.2 = (bf16[256,768]{1,0:T(8,128)(2,1)S(1)}, f32[1280,128]{1,0:T(8,128)S(1)}, f32[1280,128]{1,0:T(8,128)S(1)}) custom-call(bf16[256,768]{1,0:T(8,128)(2,1)S(1)} %get-tuple-element.20.queries, bf16[256,768]{1,0:T(8,128)(2,1)S(1)} %fusion.155.head_grad, bf16[1280,256]{1,0:T(8,128)(2,1)S(1)} %constant_dynamic-update-slice_fusion.8.keys.values, ...), custom_call_target="tpu_custom_call" | custom-call | flops 2516582400 | bytes 2883584 | tf_op jit(solution)/shard_map/attend_backward/pallas_call | solution.py:439
  589.6 5.3 collective-permute-start.65
  600.1 12.7 %collective-permute-done.65 = bf16[128,1536]{1,0:T(8,128)(2,1)S(1)} collective-permute-done((bf16[128,1536]{1,0:T(8,128)(2,1)S(1)}, bf16[128,1536]{1,0:T(8,128)(2,1)S(1)}, u32[]{:S(2)}, u32[]{:S(2)}) %collective-permute-start.65) | collective-permute-done | bytes 393248 | tf_op jit(solution)/shard_map/ppermute | solution.py:108
  621.6 8.6 copy.246
  645.9 13.3 %collective-permute-done.70 = bf16[256,1536]{1,0:T(8,128)(2,1)S(1)} collective-permute-done((bf16[256,1536]{1,0:T(8,128)(2,1)S(1)}, bf16[256,1536]{1,0:T(8,128)(2,1)S(1)}, u32[]{:S(2)}, u32[]{:S(2)}) %collective-permute-start.70) | collective-permute-done | bytes 786464 | tf_op jit(solution)/shard_map/ppermute | solution.py:104
  665.4 7.6 collective-permute-done.74
  680.4 7.1 collective-permute-done.75
  694.5 6.5 convolution_convert_fusion
  702.1 8.0 collective-permute-done.71
  721.3 9.6 %collective-permute-done.73 = bf16[128,1664]{1,0:T(8,128)(2,1)S(1)} collective-permute-done((bf16[128,1664]{1,0:T(8,128)(2,1)S(1)}, bf16[128,1664]{1,0:T(8,128)(2,1)S(1)}, u32[]{:S(2)}, u32[]{:S(2)}) %collective-permute-start.73) | collective-permute-done | bytes 426016 | tf_op jit(solution)/shard_map/ppermute | solution.py:108
  746.2 10.8 %collective-permute-done.79 = bf16[128,1664]{1,0:T(8,128)(2,1)S(1)} collective-permute-done((bf16[128,1664]{1,0:T(8,128)(2,1)S(1)}, bf16[128,1664]{1,0:T(8,128)(2,1)S(1)}, u32[]{:S(2)}, u32[]{:S(2)}) %collective-permute-start.79) | collective-permute-done | bytes 426016 | tf_op jit(solution)/shard_map/ppermute | solution.py:104
  757.0 19.0 %collective-permute-done.80 = bf16[128,1664]{1,0:T(8,128)(2,1)S(1)} collective-permute-done((bf16[128,1664]{1,0:T(8,128)(2,1)S(1)}, bf16[128,1664]{1,0:T(8,128)(2,1)S(1)}, u32[]{:S(2)}, u32[]{:S(2)}) %collective-permute-start.80) | collective-permute-done | bytes 426016 | tf_op jit(solution)/shard_map/ppermute | solution.py:108
  784.2 9.7 %attend_backward.3 = (bf16[256,768]{1,0:T(8,128)(2,1)S(1)}, f32[1280,128]{1,0:T(8,128)S(1)}, f32[1280,128]{1,0:T(8,128)S(1)}) custom-call(bf16[256,768]{1,0:T(8,128)(2,1)S(1)} %get-tuple-element.24.queries, bf16[256,768]{1,0:T(8,128)(2,1)S(1)} %fusion.158.head_grad, bf16[1280,256]{1,0:T(8,128)(2,1)S(1)} %copy-done.1, bf16[1280,256]{1,0:T(8,128)(2,1)S(1)} %copy-done.1, ...), custom_call_target="tpu_custom_call" | custom-call | flops 2516582400 | bytes 2883584 | tf_op jit(solution)/shard_map/attend_backward/pallas_call | solution.py:439
  798.3 6.1 collective-permute-done.82
  814.9 17.6 %collective-permute-done.87 = bf16[256,256]{1,0:T(8,128)(2,1)S(1)} collective-permute-done((bf16[256,256]{1,0:T(8,128)(2,1)S(1)}, bf16[256,256]{1,0:T(8,128)(2,1)S(1)}, u32[]{:S(2)}, u32[]{:S(2)}) %collective-permute-start.87) | collective-permute-done | bytes 131104 | tf_op jit(solution)/shard_map/ppermute | solution.py:114
  858.3 7.6 collective-permute-done.90
  888.0 5.4 collective-permute-done.93
  893.4 9.1 collective-permute-done.94
  (960 shorter events, 398.1 us)
Async XLA Ops:
  7.2 299.7 %all-gather.2.cloned.1.call-start = ((), (), s32[]{:S(2)}) async-start(), calls=%async_computation.1 | async-start | bytes 6266880 | tf_op jit(solution)/shard_map/all_gather | solution.py:226
  9.5 101.8 %collective-permute-start.28 = (bf16[48,768]{1,0:T(8,128)(2,1)}, bf16[48,768]{1,0:T(8,128)(2,1)}, u32[]{:S(2)}, u32[]{:S(2)}) collective-permute-start(bf16[48,768]{1,0:T(8,128)(2,1)} %broadcast_select_fusion.15), channel_id=1, source_target_pairs={{0,1},{1,0},{2,3},{3,2},{4,5},{5,4},{6,7},{7,6},{8,9},{9,8},{10,11... | collective-permute-start | bytes 221192 | tf_op jit(solution)/shard_map/ppermute | solution.py:98
  12.2 120.9 %collective-permute-start.27 = (bf16[48,1152]{1,0:T(8,128)(2,1)}, bf16[48,1152]{1,0:T(8,128)(2,1)}, u32[]{:S(2)}, u32[]{:S(2)}) collective-permute-start(bf16[48,1152]{1,0:T(8,128)(2,1)} %broadcast_select_fusion.11), channel_id=1, source_target_pairs={{0,1},{1,0},{2,3},{3,2},{4,5},{5,4},{6,7},{7,6},{8,9},{9,8},{10,11... | collective-permute-start | bytes 331784 | tf_op jit(solution)/shard_map/ppermute | solution.py:98
  12.2 132.2 %collective-permute-start.42 = (bf16[128,1536]{1,0:T(8,128)(2,1)}, bf16[128,1536]{1,0:T(8,128)(2,1)}, u32[]{:S(2)}, u32[]{:S(2)}) collective-permute-start(bf16[128,1536]{1,0:T(8,128)(2,1)} %param.11), channel_id=1, source_target_pairs={{0,4},{4,0},{8,12},{12,8},{16,20},{20,16},{24,28},{28,24},{1,5},{5... | collective-permute-start | bytes 1179656 | tf_op jit(solution)/shard_map/ppermute | solution.py:104
  18.8 25.5 %collective-permute-start.3 = (bf16[96,1920]{1,0:T(8,128)(2,1)S(1)}, bf16[96,1920]{1,0:T(8,128)(2,1)S(1)}, u32[]{:S(2)}, u32[]{:S(2)}) collective-permute-start(bf16[96,1920]{1,0:T(8,128)(2,1)S(1)} %get-tuple-element.134), channel_id=1, source_target_pairs={{0,16},{4,20},{8,24},{12,28},{16,0},{20,4},{24,8},{28,12},{1,17},{... | collective-permute-start | bytes 1105928 | tf_op jit(solution)/shard_map/ppermute | solution.py:108
  67.5 29.8 %collective-permute-start.7 = (bf16[4,2,96,1024]{3,2,1,0:T(8,128)(2,1)S(1)}, bf16[4,2,96,1024]{3,2,1,0:T(8,128)(2,1)S(1)}, u32[]{:S(2)}, u32[]{:S(2)}) collective-permute-start(bf16[4,2,96,1024]{3,2,1,0:T(8,128)(2,1)S(1)} %pad_maximum_fusion.4), channel_id=1, source_target_pairs={{0,4},{4,0},{8,12},{12,8},{16,20},{20,16},{24,28},{28,24},{1,5},{5... | collective-permute-start | bytes 4718600 | tf_op jit(solution)/shard_map/ppermute | solution.py:104
  69.9 29.5 %collective-permute-start.9 = (bf16[4,2,96,896]{3,2,0,1:T(8,128)(2,1)S(1)}, bf16[4,2,96,896]{3,2,0,1:T(8,128)(2,1)S(1)}, u32[]{:S(2)}, u32[]{:S(2)}) collective-permute-start(bf16[4,2,96,896]{3,2,0,1:T(8,128)(2,1)S(1)} %pad_maximum_fusion.5), channel_id=1, source_target_pairs={{0,2},{1,3},{2,0},{3,1},{4,6},{5,7},{6,4},{7,5},{8,10},{9,11},{10,... | collective-permute-start | bytes 4128776 | tf_op jit(solution)/shard_map/ppermute | solution.py:101
  142.4 20.9 %collective-permute-start.17 = (bf16[128,1664]{1,0:T(8,128)(2,1)}, bf16[128,1664]{1,0:T(8,128)(2,1)}, u32[]{:S(2)}, u32[]{:S(2)}) collective-permute-start(bf16[128,1664]{1,0:T(8,128)(2,1)} %pad_maximum_fusion.32), channel_id=1, source_target_pairs={{0,24},{4,28},{8,0},{12,4},{16,8},{20,12},{24,16},{28,20},{1,25},{... | collective-permute-start | bytes 1277960 | tf_op jit(solution)/shard_map/ppermute | solution.py:108
  151.2 753.3 %reduce-scatter.4.cloned.1.call-start = ((), (), s32[]{:S(2)}) async-start(), calls=%async_computation.2 | async-start | bytes 6266880 | tf_op jit(solution)/shard_map/reduce_scatter | solution.py:231
  166.8 24.4 %collective-permute-start.22 = (bf16[128,1664]{1,0:T(8,128)(2,1)}, bf16[128,1664]{1,0:T(8,128)(2,1)S(1)}, u32[]{:S(2)}, u32[]{:S(2)}) collective-permute-start(bf16[128,1664]{1,0:T(8,128)(2,1)} %broadcast_select_fusion.2), channel_id=1, source_target_pairs={{0,16},{4,20},{8,24},{12,28},{16,0},{20,4},{24,8},{28,12},{1,17},{... | collective-permute-start | bytes 1277960 | tf_op jit(solution)/shard_map/ppermute | solution.py:108
  209.5 33.3 %collective-permute-start.19 = (bf16[256,1536]{1,0:T(8,128)(2,1)}, bf16[256,1536]{1,0:T(8,128)(2,1)}, u32[]{:S(2)}, u32[]{:S(2)}) collective-permute-start(bf16[256,1536]{1,0:T(8,128)(2,1)} %slice.1047), channel_id=1, source_target_pairs={{0,4},{4,0},{8,12},{12,8},{16,20},{20,16},{24,28},{28,24},{1,5},{5... | collective-permute-start | bytes 2359304 | tf_op jit(solution)/shard_map/ppermute | solution.py:104
  245.4 31.4 %collective-permute-start.24 = (bf16[128,1536]{1,0:T(8,128)(2,1)S(1)}, bf16[128,1536]{1,0:T(8,128)(2,1)S(1)}, u32[]{:S(2)}, u32[]{:S(2)}) collective-permute-start(bf16[128,1536]{1,0:T(8,128)(2,1)S(1)} %slice_select_fusion.5), channel_id=1, source_target_pairs={{0,4},{4,0},{8,12},{12,8},{16,20},{20,16},{24,28},{28,24},{1,5},{5... | collective-permute-start | bytes 1179656 | tf_op jit(solution)/shard_map/ppermute | solution.py:104
  254.2 20.7 %collective-permute-start.20 = (bf16[128,1536]{1,0:T(8,128)(2,1)S(1)}, bf16[128,1536]{1,0:T(8,128)(2,1)S(1)}, u32[]{:S(2)}, u32[]{:S(2)}) collective-permute-start(bf16[128,1536]{1,0:T(8,128)(2,1)S(1)} %get-tuple-element.188), channel_id=1, source_target_pairs={{0,24},{4,28},{8,0},{12,4},{16,8},{20,12},{24,16},{28,20},{1,25},{... | collective-permute-start | bytes 1179656 | tf_op jit(solution)/shard_map/ppermute | solution.py:108
  279.8 25.3 %collective-permute-start.26 = (bf16[128,1536]{1,0:T(8,128)(2,1)S(1)}, bf16[128,1536]{1,0:T(8,128)(2,1)S(1)}, u32[]{:S(2)}, u32[]{:S(2)}) collective-permute-start(bf16[128,1536]{1,0:T(8,128)(2,1)S(1)} %fusion.259), channel_id=1, source_target_pairs={{0,16},{4,20},{8,24},{12,28},{16,0},{20,4},{24,8},{28,12},{1,17},{... | collective-permute-start | bytes 1179656 | tf_op jit(solution)/shard_map/ppermute | solution.py:108
  284.3 25.1 %collective-permute-start.44 = (bf16[128,1536]{1,0:T(8,128)(2,1)}, bf16[128,1536]{1,0:T(8,128)(2,1)}, u32[]{:S(2)}, u32[]{:S(2)}) collective-permute-start(bf16[128,1536]{1,0:T(8,128)(2,1)} %broadcast_select_fusion.10), channel_id=1, source_target_pairs={{0,24},{4,28},{8,0},{12,4},{16,8},{20,12},{24,16},{28,20},{1,25},{... | collective-permute-start | bytes 1179656 | tf_op jit(solution)/shard_map/ppermute | solution.py:108
  284.3 26.3 %collective-permute-start.43 = (bf16[128,1536]{1,0:T(8,128)(2,1)}, bf16[128,1536]{1,0:T(8,128)(2,1)}, u32[]{:S(2)}, u32[]{:S(2)}) collective-permute-start(bf16[128,1536]{1,0:T(8,128)(2,1)} %broadcast_select_fusion.10), channel_id=1, source_target_pairs={{0,8},{4,12},{8,16},{12,20},{16,24},{20,28},{24,0},{28,4},{1,9},{5... | collective-permute-start | bytes 1179656 | tf_op jit(solution)/shard_map/ppermute | solution.py:108
  326.7 22.8 %collective-permute-start.45 = (bf16[128,1536]{1,0:T(8,128)(2,1)}, bf16[128,1536]{1,0:T(8,128)(2,1)}, u32[]{:S(2)}, u32[]{:S(2)}) collective-permute-start(bf16[128,1536]{1,0:T(8,128)(2,1)} %get-tuple-element.212), channel_id=1, source_target_pairs={{0,16},{4,20},{8,24},{12,28},{16,0},{20,4},{24,8},{28,12},{1,17},{... | collective-permute-start | bytes 1179656 | tf_op jit(solution)/shard_map/ppermute | solution.py:108
  361.0 39.7 %collective-permute-start.37 = (bf16[128,1536]{1,0:T(8,128)(2,1)}, bf16[128,1536]{1,0:T(8,128)(2,1)}, u32[]{:S(2)}, u32[]{:S(2)}) collective-permute-start(bf16[128,1536]{1,0:T(8,128)(2,1)} %copy-done.21), channel_id=1, source_target_pairs={{0,24},{4,28},{8,0},{12,4},{16,8},{20,12},{24,16},{28,20},{1,25},{... | collective-permute-start | bytes 1179656 | tf_op jit(solution)/shard_map/ppermute | solution.py:108
  366.0 31.0 %collective-permute-start.36 = (bf16[128,1536]{1,0:T(8,128)(2,1)}, bf16[128,1536]{1,0:T(8,128)(2,1)}, u32[]{:S(2)}, u32[]{:S(2)}) collective-permute-start(bf16[128,1536]{1,0:T(8,128)(2,1)} %copy-done.21), channel_id=1, source_target_pairs={{0,8},{4,12},{8,16},{12,20},{16,24},{20,28},{24,0},{28,4},{1,9},{5... | collective-permute-start | bytes 1179656 | tf_op jit(solution)/shard_map/ppermute | solution.py:108
  368.7 29.5 %collective-permute-start.35 = (bf16[128,1536]{1,0:T(8,128)(2,1)}, bf16[128,1536]{1,0:T(8,128)(2,1)}, u32[]{:S(2)}, u32[]{:S(2)}) collective-permute-start(bf16[128,1536]{1,0:T(8,128)(2,1)} %copy-done.21), channel_id=1, source_target_pairs={{0,4},{4,0},{8,12},{12,8},{16,20},{20,16},{24,28},{28,24},{1,5},{5... | collective-permute-start | bytes 1179656 | tf_op jit(solution)/shard_map/ppermute | solution.py:104
  379.1 33.4 %collective-permute-start.46 = (bf16[256,1536]{1,0:T(8,128)(2,1)S(1)}, bf16[256,1536]{1,0:T(8,128)(2,1)S(1)}, u32[]{:S(2)}, u32[]{:S(2)}) collective-permute-start(bf16[256,1536]{1,0:T(8,128)(2,1)S(1)} %get-tuple-element.116), channel_id=1, source_target_pairs={{0,4},{4,0},{8,12},{12,8},{16,20},{20,16},{24,28},{28,24},{1,5},{5... | collective-permute-start | bytes 2359304 | tf_op jit(solution)/shard_map/ppermute | solution.py:104
  402.6 37.7 %collective-permute-start.51 = (bf16[128,1536]{1,0:T(8,128)(2,1)S(1)}, bf16[128,1536]{1,0:T(8,128)(2,1)S(1)}, u32[]{:S(2)}, u32[]{:S(2)}) collective-permute-start(bf16[128,1536]{1,0:T(8,128)(2,1)S(1)} %broadcast_select_fusion.6), channel_id=1, source_target_pairs={{0,16},{4,20},{8,24},{12,28},{16,0},{20,4},{24,8},{28,12},{1,17},{... | collective-permute-start | bytes 1179656 | tf_op jit(solution)/shard_map/ppermute | solution.py:108
  415.7 36.5 %collective-permute-start.50 = (bf16[128,1536]{1,0:T(8,128)(2,1)S(1)}, bf16[128,1536]{1,0:T(8,128)(2,1)S(1)}, u32[]{:S(2)}, u32[]{:S(2)}) collective-permute-start(bf16[128,1536]{1,0:T(8,128)(2,1)S(1)} %get-tuple-element.114), channel_id=1, source_target_pairs={{0,4},{4,0},{8,12},{12,8},{16,20},{20,16},{24,28},{28,24},{1,5},{5... | collective-permute-start | bytes 1179656 | tf_op jit(solution)/shard_map/ppermute | solution.py:104
  444.9 24.5 %collective-permute-start.39 = (bf16[256,1536]{1,0:T(8,128)(2,1)S(1)}, bf16[256,1536]{1,0:T(8,128)(2,1)S(1)}, u32[]{:S(2)}, u32[]{:S(2)}) collective-permute-start(bf16[256,1536]{1,0:T(8,128)(2,1)S(1)} %slice.1092), channel_id=1, source_target_pairs={{0,4},{4,0},{8,12},{12,8},{16,20},{20,16},{24,28},{28,24},{1,5},{5... | collective-permute-start | bytes 2359304 | tf_op jit(solution)/shard_map/ppermute | solution.py:104
  473.7 25.8 %collective-permute-start.41 = (bf16[128,1536]{1,0:T(8,128)(2,1)S(1)}, bf16[128,1536]{1,0:T(8,128)(2,1)S(1)}, u32[]{:S(2)}, u32[]{:S(2)}) collective-permute-start(bf16[128,1536]{1,0:T(8,128)(2,1)S(1)} %get-tuple-element.183), channel_id=1, source_target_pairs={{0,8},{4,12},{8,16},{12,20},{16,24},{20,28},{24,0},{28,4},{1,9},{5... | collective-permute-start | bytes 1179656 | tf_op jit(solution)/shard_map/ppermute | solution.py:108
  473.8 25.8 %collective-permute-start.40 = (bf16[128,1536]{1,0:T(8,128)(2,1)S(1)}, bf16[128,1536]{1,0:T(8,128)(2,1)S(1)}, u32[]{:S(2)}, u32[]{:S(2)}) collective-permute-start(bf16[128,1536]{1,0:T(8,128)(2,1)S(1)} %get-tuple-element.184), channel_id=1, source_target_pairs={{0,24},{4,28},{8,0},{12,4},{16,8},{20,12},{24,16},{28,20},{1,25},{... | collective-permute-start | bytes 1179656 | tf_op jit(solution)/shard_map/ppermute | solution.py:108
  487.5 32.9 %collective-permute-start.54 = (bf16[2,384,1536]{2,1,0:T(8,128)(2,1)S(1)}, bf16[2,384,1536]{2,1,0:T(8,128)(2,1)S(1)}, u32[]{:S(2)}, u32[]{:S(2)}) collective-permute-start(bf16[2,384,1536]{2,1,0:T(8,128)(2,1)S(1)} %dynamic-slice_bitcast_fusion.1), channel_id=1, source_target_pairs={{0,1},{1,0},{2,3},{3,2},{4,5},{5,4},{6,7},{7,6},{8,9},{9,8},{10,11... | collective-permute-start | bytes 7077896 | tf_op jit(solution)/shard_map/ppermute | solution.py:98
  524.9 24.8 %collective-permute-start.108 = (bf16[192,1536]{1,0:T(8,128)(2,1)S(1)}, bf16[192,1536]{1,0:T(8,128)(2,1)S(1)}, u32[]{:S(2)}, u32[]{:S(2)}) collective-permute-start(bf16[192,1536]{1,0:T(8,128)(2,1)S(1)} %fusion.235), channel_id=1, source_target_pairs={{0,2},{1,3},{2,0},{3,1},{4,6},{5,7},{6,4},{7,5},{8,10},{9,11},{10,... | collective-permute-start | bytes 1769480 | tf_op jit(solution)/shard_map/ppermute | solution.py:101
  527.0 68.4 %collective-permute-start.106 = (bf16[384,1536]{1,0:T(8,128)(2,1)S(1)}, bf16[384,1536]{1,0:T(8,128)(2,1)S(1)}, u32[]{:S(2)}, u32[]{:S(2)}) collective-permute-start(bf16[384,1536]{1,0:T(8,128)(2,1)S(1)} %fusion.162), channel_id=1, source_target_pairs={{0,2},{1,3},{2,0},{3,1},{4,6},{5,7},{6,4},{7,5},{8,10},{9,11},{10,... | collective-permute-start | bytes 3538952 | tf_op jit(solution)/shard_map/ppermute | solution.py:101
  589.6 23.2 %collective-permute-start.65 = (bf16[128,1536]{1,0:T(8,128)(2,1)S(1)}, bf16[128,1536]{1,0:T(8,128)(2,1)S(1)}, u32[]{:S(2)}, u32[]{:S(2)}) collective-permute-start(bf16[128,1536]{1,0:T(8,128)(2,1)S(1)} %fusion.260), channel_id=1, source_target_pairs={{0,16},{4,20},{8,24},{12,28},{16,0},{20,4},{24,8},{28,12},{1,17},{... | collective-permute-start | bytes 1179656 | tf_op jit(solution)/shard_map/ppermute | solution.py:108
  616.0 21.1 %collective-permute-start.69 = (bf16[128,1536]{1,0:T(8,128)(2,1)S(1)}, bf16[128,1536]{1,0:T(8,128)(2,1)S(1)}, u32[]{:S(2)}, u32[]{:S(2)}) collective-permute-start(bf16[128,1536]{1,0:T(8,128)(2,1)S(1)} %get-tuple-element.107), channel_id=1, source_target_pairs={{0,24},{4,28},{8,0},{12,4},{16,8},{20,12},{24,16},{28,20},{1,25},{... | collective-permute-start | bytes 1179656 | tf_op jit(solution)/shard_map/ppermute | solution.py:108
  638.4 34.6 %collective-permute-start.74 = (bf16[128,1536]{1,0:T(8,128)(2,1)S(1)}, bf16[128,1536]{1,0:T(8,128)(2,1)S(1)}, u32[]{:S(2)}, u32[]{:S(2)}) collective-permute-start(bf16[128,1536]{1,0:T(8,128)(2,1)S(1)} %broadcast_select_fusion.4), channel_id=1, source_target_pairs={{0,16},{4,20},{8,24},{12,28},{16,0},{20,4},{24,8},{28,12},{1,17},{... | collective-permute-start | bytes 1179656 | tf_op jit(solution)/shard_map/ppermute | solution.py:108
  679.0 31.1 %collective-permute-start.71 = (bf16[256,1664]{1,0:T(8,128)(2,1)S(1)}, bf16[256,1664]{1,0:T(8,128)(2,1)}, u32[]{:S(2)}, u32[]{:S(2)}) collective-permute-start(bf16[256,1664]{1,0:T(8,128)(2,1)S(1)} %pad_maximum_fusion.7), channel_id=1, source_target_pairs={{0,4},{4,0},{8,12},{12,8},{16,20},{20,16},{24,28},{28,24},{1,5},{5... | collective-permute-start | bytes 2555912 | tf_op jit(solution)/shard_map/ppermute | solution.py:104
  701.2 37.4 %collective-permute-start.77 = (bf16[2,384,1536]{2,1,0:T(8,128)(2,1)S(1)}, bf16[2,384,1536]{2,1,0:T(8,128)(2,1)S(1)}, u32[]{:S(2)}, u32[]{:S(2)}) collective-permute-start(bf16[2,384,1536]{2,1,0:T(8,128)(2,1)S(1)} %dynamic-slice_bitcast_fusion), channel_id=1, source_target_pairs={{0,1},{1,0},{2,3},{3,2},{4,5},{5,4},{6,7},{7,6},{8,9},{9,8},{10,11... | collective-permute-start | bytes 7077896 | tf_op jit(solution)/shard_map/ppermute | solution.py:98
  701.4 36.7 %collective-permute-start.78 = (bf16[2,192,1536]{2,1,0:T(8,128)(2,1)S(1)}, bf16[2,192,1536]{2,1,0:T(8,128)(2,1)S(1)}, u32[]{:S(2)}, u32[]{:S(2)}) collective-permute-start(bf16[2,192,1536]{2,1,0:T(8,128)(2,1)S(1)} %dynamic-slice_bitcast_fusion.2), channel_id=1, source_target_pairs={{0,1},{1,0},{2,3},{3,2},{4,5},{5,4},{6,7},{7,6},{8,9},{9,8},{10,11... | collective-permute-start | bytes 3538952 | tf_op jit(solution)/shard_map/ppermute | solution.py:98
  712.7 24.3 %collective-permute-start.76 = (bf16[128,1664]{1,0:T(8,128)(2,1)S(1)}, bf16[128,1664]{1,0:T(8,128)(2,1)S(1)}, u32[]{:S(2)}, u32[]{:S(2)}) collective-permute-start(bf16[128,1664]{1,0:T(8,128)(2,1)S(1)} %fusion.256), channel_id=1, source_target_pairs={{0,4},{4,0},{8,12},{12,8},{16,20},{20,16},{24,28},{28,24},{1,5},{5... | collective-permute-start | bytes 1277960 | tf_op jit(solution)/shard_map/ppermute | solution.py:104
  741.1 35.0 %collective-permute-start.80 = (bf16[128,1664]{1,0:T(8,128)(2,1)S(1)}, bf16[128,1664]{1,0:T(8,128)(2,1)S(1)}, u32[]{:S(2)}, u32[]{:S(2)}) collective-permute-start(bf16[128,1664]{1,0:T(8,128)(2,1)S(1)} %fusion.254), channel_id=1, source_target_pairs={{0,16},{4,20},{8,24},{12,28},{16,0},{20,4},{24,8},{28,12},{1,17},{... | collective-permute-start | bytes 1277960 | tf_op jit(solution)/shard_map/ppermute | solution.py:108
  743.6 35.0 %collective-permute-start.107 = (bf16[192,1536]{1,0:T(8,128)(2,1)S(1)}, bf16[192,1536]{1,0:T(8,128)(2,1)S(1)}, u32[]{:S(2)}, u32[]{:S(2)}) collective-permute-start(bf16[192,1536]{1,0:T(8,128)(2,1)S(1)} %fusion.234), channel_id=1, source_target_pairs={{0,2},{1,3},{2,0},{3,1},{4,6},{5,7},{6,4},{7,5},{8,10},{9,11},{10,... | collective-permute-start | bytes 1769480 | tf_op jit(solution)/shard_map/ppermute | solution.py:101
  744.2 53.8 %collective-permute-start.105 = (bf16[384,1536]{1,0:T(8,128)(2,1)S(1)}, bf16[384,1536]{1,0:T(8,128)(2,1)S(1)}, u32[]{:S(2)}, u32[]{:S(2)}) collective-permute-start(bf16[384,1536]{1,0:T(8,128)(2,1)S(1)} %fusion.161), channel_id=1, source_target_pairs={{0,2},{1,3},{2,0},{3,1},{4,6},{5,7},{6,4},{7,5},{8,10},{9,11},{10,... | collective-permute-start | bytes 3538952 | tf_op jit(solution)/shard_map/ppermute | solution.py:101
  782.0 22.5 %collective-permute-start.82 = (bf16[4,2,96,384]{3,2,1,0:T(8,128)(2,1)S(1)}, bf16[4,2,96,384]{3,2,1,0:T(8,128)(2,1)S(1)}, u32[]{:S(2)}, u32[]{:S(2)}) collective-permute-start(bf16[4,2,96,384]{3,2,1,0:T(8,128)(2,1)S(1)} %dynamic-slice_bitcast_fusion.5), channel_id=1, source_target_pairs={{0,2},{1,3},{2,0},{3,1},{4,6},{5,7},{6,4},{7,5},{8,10},{9,11},{10,... | collective-permute-start | bytes 1769480 | tf_op jit(solution)/shard_map/ppermute | solution.py:101
  782.1 22.9 %collective-permute-start.83 = (bf16[4,2,96,384]{3,2,0,1:T(8,128)(2,1)S(1)}, bf16[4,2,96,384]{3,2,0,1:T(8,128)(2,1)S(1)}, u32[]{:S(2)}, u32[]{:S(2)}) collective-permute-start(bf16[4,2,96,384]{3,2,0,1:T(8,128)(2,1)S(1)} %bitcast.538), channel_id=1, source_target_pairs={{0,4},{4,0},{8,12},{12,8},{16,20},{20,16},{24,28},{28,24},{1,5},{5... | collective-permute-start | bytes 1769480 | tf_op jit(solution)/shard_map/ppermute | solution.py:104
  796.0 61.1 %collective-permute-start.89 = (bf16[4,2,96,768]{3,2,0,1:T(8,128)(2,1)}, bf16[4,2,96,768]{3,2,0,1:T(8,128)(2,1)}, u32[]{:S(2)}, u32[]{:S(2)}) collective-permute-start(bf16[4,2,96,768]{3,2,0,1:T(8,128)(2,1)} %bitcast.485), channel_id=1, source_target_pairs={{0,2},{1,3},{2,0},{3,1},{4,6},{5,7},{6,4},{7,5},{8,10},{9,11},{10,... | collective-permute-start | bytes 3538952 | tf_op jit(solution)/shard_map/ppermute | solution.py:101
  808.4 24.0 %collective-permute-start.87 = (bf16[256,256]{1,0:T(8,128)(2,1)S(1)}, bf16[256,256]{1,0:T(8,128)(2,1)S(1)}, u32[]{:S(2)}, u32[]{:S(2)}) collective-permute-start(bf16[256,256]{1,0:T(8,128)(2,1)S(1)} %get-tuple-element.190), channel_id=1, source_target_pairs={{2,0},{3,1},{4,2},{5,3},{6,4},{7,5},{8,6},{9,7},{10,8},{11,9},{12,... | collective-permute-start | bytes 393224 | tf_op jit(solution)/shard_map/ppermute | solution.py:114
  809.7 22.7 %collective-permute-start.86 = (bf16[256,256]{1,0:T(8,128)(2,1)S(1)}, bf16[256,256]{1,0:T(8,128)(2,1)S(1)}, u32[]{:S(2)}, u32[]{:S(2)}) collective-permute-start(bf16[256,256]{1,0:T(8,128)(2,1)S(1)} %get-tuple-element.191), channel_id=1, source_target_pairs={{4,0},{5,1},{6,2},{7,3},{8,4},{9,5},{10,6},{11,7},{12,8},{13,9},{1... | collective-permute-start | bytes 393224 | tf_op jit(solution)/shard_map/ppermute | solution.py:114
  811.0 22.3 %collective-permute-start.85 = (bf16[256,256]{1,0:T(8,128)(2,1)S(1)}, bf16[256,256]{1,0:T(8,128)(2,1)S(1)}, u32[]{:S(2)}, u32[]{:S(2)}) collective-permute-start(bf16[256,256]{1,0:T(8,128)(2,1)S(1)} %get-tuple-element.192), channel_id=1, source_target_pairs={{6,0},{7,1},{8,2},{9,3},{10,4},{11,5},{12,6},{13,7},{14,8},{15,9},... | collective-permute-start | bytes 393224 | tf_op jit(solution)/shard_map/ppermute | solution.py:114
  846.3 26.0 %collective-permute-start.100 = (bf16[96,768]{1,0:T(8,128)(2,1)}, bf16[96,768]{1,0:T(8,128)(2,1)}, u32[]{:S(2)}, u32[]{:S(2)}) collective-permute-start(bf16[96,768]{1,0:T(8,128)(2,1)} %get-tuple-element.197), channel_id=1, source_target_pairs={{0,24},{4,28},{8,0},{12,4},{16,8},{20,12},{24,16},{28,20},{1,25},{... | collective-permute-start | bytes 442376 | tf_op jit(solution)/shard_map/ppermute | solution.py:108
  848.3 24.0 %collective-permute-start.101 = (bf16[96,768]{1,0:T(8,128)(2,1)}, bf16[96,768]{1,0:T(8,128)(2,1)}, u32[]{:S(2)}, u32[]{:S(2)}) collective-permute-start(bf16[96,768]{1,0:T(8,128)(2,1)} %get-tuple-element.198), channel_id=1, source_target_pairs={{0,16},{4,20},{8,24},{12,28},{16,0},{20,4},{24,8},{28,12},{1,17},{... | collective-permute-start | bytes 442376 | tf_op jit(solution)/shard_map/ppermute | solution.py:108
  848.3 24.0 %collective-permute-start.102 = (bf16[96,768]{1,0:T(8,128)(2,1)}, bf16[96,768]{1,0:T(8,128)(2,1)}, u32[]{:S(2)}, u32[]{:S(2)}) collective-permute-start(bf16[96,768]{1,0:T(8,128)(2,1)} %get-tuple-element.199), channel_id=1, source_target_pairs={{0,8},{4,12},{8,16},{12,20},{16,24},{20,28},{24,0},{28,4},{1,9},{5... | collective-permute-start | bytes 442376 | tf_op jit(solution)/shard_map/ppermute | solution.py:108
  (228 other events, 2625.4 us)
Sparse Core Ops, SparseCore 0:
  151.3 122.4 all-gather.1
  630.4 167.0 reduce-scatter.3
